TPU v7x, 256 devices: a whole 4x4x8 slice. The times are simulated.
256 devices in a mesh: row: 32 (over z, y), col: 8 (over x, core).
Axes of the slice: x: 4, y: 4, z: 8, core: 2. Of those that a mesh axis runs over, the one named last changes fastest.
Arguments:
- tokens: bfloat16 [512, 8192], P('row', 'col'), may hold values from -6 to 6
- gate_weight: bfloat16 [8192, 28672], P('col', 'row'), may hold values from -0.0625 to 0.0625
- up_weight: bfloat16 [8192, 28672], P('col', 'row'), may hold values from -0.0625 to 0.0625
- down_weight: bfloat16 [28672, 8192], P('row', 'col'), may hold values from -0.03125 to 0.03125
- out_grad: bfloat16 [512, 8192], P('row', 'col'), may hold values from -1.5 to 1.5
Outputs:
- mixed: bfloat16 [512, 8192], P('row', 'col')
- tokens_grad: bfloat16 [512, 8192], P('row', 'col')
- gate_grad: bfloat16 [8192, 28672], P('col', 'row')
- up_grad: bfloat16 [8192, 28672], P('col', 'row')
- down_grad: bfloat16 [28672, 8192], P('row', 'col')
All inputs are finite; a program needn't handle non-finite values.
Results may differ from a plain program's by a relative error of at most 0.0049.
Values may be sent and summed in bfloat16 or wider, within the bound.
No kernel may reach another device: no remote copies, remote signals or barrier semaphores. Data moves between devices by JAX's collectives and lax.ppermute only.
A program may use at most 64 MiB of HBM per device.

v0:
```python
import jax
import jax.numpy as jnp
from jax import lax
from jax.sharding import PartitionSpec as P


def times_transposed(left, right):
    return lax.dot_general(
        left, right, (((1,), (1,)), ((), ())), preferred_element_type=jnp.float32
    )


def transposed_times(left, right):
    return lax.dot_general(
        left, right, (((0,), (0,)), ((), ())), preferred_element_type=jnp.float32
    )


def deltas(hidden_grad, gate_pre, up_pre, sigmoid_gate):
    gate_delta = (
        hidden_grad * up_pre * sigmoid_gate * (1.0 + gate_pre * (1.0 - sigmoid_gate))
    ).astype(jnp.bfloat16)
    up_delta = (hidden_grad * gate_pre * sigmoid_gate).astype(jnp.bfloat16)
    return (gate_delta, up_delta)


def body(tokens, gate_weight, up_weight, down_weight, out_grad):
    width = gate_weight.shape[1]
    panel = lax.all_gather(tokens, "row", axis=0, tiled=True)
    grad_panel = lax.all_gather(out_grad, "row", axis=0, tiled=True)
    both_pre = lax.psum_scatter(
        jnp.concatenate(
            [
                jnp.dot(panel, gate_weight, preferred_element_type=jnp.float32),
                jnp.dot(panel, up_weight, preferred_element_type=jnp.float32),
            ],
            axis=1,
        ),
        "col",
        scatter_dimension=0,
        tiled=True,
    )
    gate_pre = both_pre[:, :width]
    up_pre = both_pre[:, width:]
    sigmoid_gate = jax.nn.sigmoid(gate_pre)
    hidden = (gate_pre * sigmoid_gate * up_pre).astype(jnp.bfloat16)
    hidden_all = lax.all_gather(hidden, "col", axis=0, tiled=True)
    hidden_grad = lax.psum_scatter(
        times_transposed(grad_panel, down_weight), "col", scatter_dimension=0, tiled=True
    )
    gate_delta, up_delta = deltas(hidden_grad, gate_pre, up_pre, sigmoid_gate)
    gate_all, up_all = (
        lax.all_gather(gate_delta, "col", axis=0, tiled=True),
        lax.all_gather(up_delta, "col", axis=0, tiled=True),
    )
    mixed = lax.psum_scatter(
        jnp.dot(hidden_all, down_weight, preferred_element_type=jnp.float32),
        "row",
        scatter_dimension=0,
        tiled=True,
    ).astype(jnp.bfloat16)
    down_grad = transposed_times(hidden_all, grad_panel).astype(jnp.bfloat16)
    gate_grad = transposed_times(panel, gate_all).astype(jnp.bfloat16)
    up_grad = transposed_times(panel, up_all).astype(jnp.bfloat16)
    gate_part = lax.psum_scatter(
        times_transposed(gate_all, gate_weight), "row", scatter_dimension=0, tiled=True
    )
    up_part = lax.psum_scatter(
        times_transposed(up_all, up_weight), "row", scatter_dimension=0, tiled=True
    )
    tokens_grad = (gate_part + up_part).astype(jnp.bfloat16)
    return (mixed, tokens_grad, gate_grad, up_grad, down_grad)


def solution(mesh):
    placed = (P("row", "col"), P("col", "row"), P("col", "row"), P("row", "col"), P("row", "col"))
    return jax.shard_map(
        body,
        mesh=mesh,
        in_specs=placed,
        out_specs=(
            P("row", "col"),
            P("row", "col"),
            P("col", "row"),
            P("col", "row"),
            P("row", "col"),
        ),
        check_vma=False,
    )
```

profile of v0, /device:TPU:1, one launch (start us, length us, event | category | flops | bytes accessed | tf_op | source)
XLA Modules:
  0.0 714.8 jit_solution(9067063798063065397)
XLA Ops:
  7.2 0.0 copy-start
  7.2 0.0 all-gather.5.cloned.1.call-start
  7.2 0.7 all-gather.5.cloned.1.call-update
  7.9 0.0 all-gather.3.cloned.1.call-start
  8.0 0.7 all-gather.3.cloned.1.call-update
  8.7 0.0 reduce-scatter.9.cloned.1.call-start
  8.7 77.5 %all-gather.5.cloned.1.call-done = bf16[512,1024]{1,0:T(8,128)(2,1)} async-done(((bf16[16,1024]{1,0:T(8,128)(2,1)}), bf16[512,1024]{1,0:T(8,128)(2,1)}) %all-gather.5.cloned.1.call-update) | async-done | bytes 1048592 | tf_op jit(solution)/shard_map/all_gather | solution.py:30
  86.2 4.3 fusion.3
  90.6 0.0 reduce-scatter.9.cloned.1.call-update
  90.6 0.0 reduce-scatter.5.cloned.1.call-start
  90.7 72.0 %all-gather.3.cloned.1.call-done = bf16[512,1024]{1,0:T(8,128)(2,1)} async-done(((bf16[16,1024]{1,0:T(8,128)(2,1)}), bf16[512,1024]{1,0:T(8,128)(2,1)}) %all-gather.3.cloned.1.call-update) | async-done | bytes 1048592 | tf_op jit(solution)/shard_map/all_gather | solution.py:29
  162.7 0.0 copy-done
  162.7 0.0 copy-start.4
  162.7 0.0 copy-start.6
  162.7 2.6 fusion
  165.3 0.0 copy-done.4
  165.3 0.0 copy-done.6
  165.4 1.2 fusion.1
  166.6 2.1 pad_maximum_fusion
  168.7 0.0 reduce-scatter.5.cloned.1.call-update
  168.7 0.0 reduce-scatter.11.cloned.1.call-start
  168.8 32.3 %reduce-scatter.9.cloned.1.call-done = f32[64,896]{1,0:T(8,128)} async-done(((f32[512,896]{1,0:T(8,128)}), f32[64,896]{1,0:T(8,128)}) %reduce-scatter.9.cloned.1.call-update) | async-done | bytes 229392 | tf_op jit(solution)/shard_map/reduce_scatter | solution.py:48
  201.0 40.4 %reduce-scatter.5.cloned.1.call-done = f32[64,1792]{1,0:T(8,128)} async-done(((f32[512,1792]{1,0:T(8,128)}), f32[64,1792]{1,0:T(8,128)}) %reduce-scatter.5.cloned.1.call-update) | async-done | bytes 458768 | tf_op jit(solution)/shard_map/reduce_scatter | solution.py:31
  241.4 1.3 multiply_convert_fusion
  242.7 17.0 %all_gather.18 = bf16[512,896]{1,0:T(8,128)(2,1)S(1)} all-gather(bf16[64,896]{1,0:T(8,128)(2,1)S(1)} %get-tuple-element.11), channel_id=1, replica_groups=mesh['row'=32,'col'=8] {'col'}, dimensions={0}, use_global_device_ids=true | all-gather | bytes 1032192 | tf_op jit(solution)/shard_map/all_gather | solution.py:53
  259.7 0.0 copy-start.1
  259.7 1.3 fusion.4
  261.0 0.0 copy-done.1
  261.0 13.6 %all_gather.19 = bf16[512,896]{1,0:T(8,128)(2,1)S(1)} all-gather(bf16[64,896]{1,0:T(8,128)(2,1)S(1)} %get-tuple-element.10), channel_id=1, replica_groups=mesh['row'=32,'col'=8] {'col'}, dimensions={0}, use_global_device_ids=true | all-gather | bytes 1032192 | tf_op jit(solution)/shard_map/all_gather | solution.py:54
  274.6 0.0 copy-done.5
  274.6 2.6 convolution_add_fusion
  277.3 0.0 reduce-scatter.11.cloned.1.call-update
  277.3 0.0 reduce-scatter.7.cloned.1.call-start
  277.3 13.6 %all_gather.16 = bf16[512,896]{1,0:T(8,128)(2,1)S(1)} all-gather(bf16[64,896]{1,0:T(8,128)(2,1)S(1)} %get-tuple-element.12), channel_id=1, replica_groups=mesh['row'=32,'col'=8] {'col'}, dimensions={0}, use_global_device_ids=true | all-gather | bytes 1032192 | tf_op jit(solution)/shard_map/all_gather | solution.py:47
  291.0 0.0 copy-start.2
  291.0 1.0 copy-done.2
  291.9 4.1 fusion.2
  296.0 0.0 reduce-scatter.7.cloned.1.call-update
  296.0 3.9 convert_bitcast_fusion.1
  299.9 3.8 copy.10
  303.7 3.6 convert_bitcast_fusion
  307.3 3.9 copy.11
  311.2 0.0 copy-done.3
  311.2 3.6 convolution_convert_fusion
  314.8 173.0 %reduce-scatter.11.cloned.1.call-done = f32[16,1024]{1,0:T(8,128)} async-done(((f32[512,1024]{1,0:T(8,128)}), f32[16,1024]{1,0:T(8,128)}) %reduce-scatter.11.cloned.1.call-update) | async-done | bytes 65552 | tf_op jit(solution)/shard_map/reduce_scatter | solution.py:65
  487.9 1.5 convert_element_type.34
  489.3 217.2 %reduce-scatter.7.cloned.1.call-done = f32[16,1024]{1,0:T(8,128)} async-done(((f32[512,1024]{1,0:T(8,128)}), f32[16,1024]{1,0:T(8,128)}) %reduce-scatter.7.cloned.1.call-update) | async-done | bytes 65552 | tf_op jit(solution)/shard_map/reduce_scatter | solution.py:56
  706.5 1.5 convert_element_type.31
  (2 shorter events, 0.0 us)
Async XLA Ops:
  7.2 155.5 %copy-start = (bf16[1024,896]{1,0:T(8,128)(2,1)S(1)}, bf16[1024,896]{1,0:T(8,128)(2,1)}, u32[]{:S(2)}) copy-start(bf16[1024,896]{1,0:T(8,128)(2,1)} %param.6) | copy-start | bytes 5505028
  7.2 79.1 %all-gather.5.cloned.1.call-start = ((), (), s32[]{:S(2)}) async-start(), calls=%async_computation.7 | async-start | bytes 1081344 | tf_op jit(solution)/shard_map/all_gather | solution.py:30
  7.9 154.8 %all-gather.3.cloned.1.call-start = ((), (), s32[]{:S(2)}) async-start(), calls=%async_computation.4 | async-start | bytes 1081344 | tf_op jit(solution)/shard_map/all_gather | solution.py:29
  8.7 192.4 %reduce-scatter.9.cloned.1.call-start = ((), (), s32[]{:S(2)}) async-start(), calls=%async_computation.8 | async-start | bytes 2064384 | tf_op jit(solution)/shard_map/reduce_scatter | solution.py:48
  90.6 150.8 %reduce-scatter.5.cloned.1.call-start = ((), (), s32[]{:S(2)}) async-start(), calls=%async_computation.5 | async-start | bytes 4128768 | tf_op jit(solution)/shard_map/reduce_scatter | solution.py:31
  162.7 2.6 copy-start.4
  162.7 2.6 copy-start.6
  168.7 319.2 %reduce-scatter.11.cloned.1.call-start = ((), (), s32[]{:S(2)}) async-start(), calls=%async_computation.9 | async-start | bytes 2162688 | tf_op jit(solution)/shard_map/reduce_scatter | solution.py:65
  259.7 1.3 copy-start.1
  259.7 14.9 %copy-start.5 = (bf16[1024,896]{1,0:T(8,128)(2,1)S(1)}, bf16[1024,896]{1,0:T(8,128)(2,1)}, u32[]{:S(2)}) copy-start(bf16[1024,896]{1,0:T(8,128)(2,1)} %param.7) | copy-start | bytes 5505028
  277.3 429.2 %reduce-scatter.7.cloned.1.call-start = ((), (), s32[]{:S(2)}) async-start(), calls=%async_computation.6 | async-start | bytes 2162688 | tf_op jit(solution)/shard_map/reduce_scatter | solution.py:56
  291.0 1.0 copy-start.2
  307.3 3.9 copy-start.3
Sparse Core Ops, SparseCore 0:
  10.6 75.6 all-gather.4
  88.8 73.8 all-gather.2
  165.8 35.1 reduce-scatter.8
  203.5 37.9 reduce-scatter.4
  277.4 210.3 reduce-scatter.10
  492.0 214.4 reduce-scatter.6
where the time goes:
time: 720 us; the launch traced here: 715 us
  waiting for transfers between devices  614 us (85%)
  blocking collectives  44.2 us (6%)
  matrix products  27.3 us (4%)
  between operations  14.2 us (2%)
  local copies, waits for them, and re-layouts  8.67 us (1%)
    reduce_scatter x1, waiting for transfers between devices, body(): lax.psum_scatter(jnp.dot(hidden_all, down_weight, preferred_element_type=...  217 us
    reduce_scatter x1, waiting for transfers between devices, body(): lax.psum_scatter(times_transposed(gate_all, gate_weight), 'row', scatter_...  173 us
    all_gather x1, waiting for transfers between devices, body(): grad_panel = lax.all_gather(out_grad, 'row', axis=0, tiled=True)  77.5 us
    all_gather x1, waiting for transfers between devices, body(): panel = lax.all_gather(tokens, 'row', axis=0, tiled=True)  72 us
    reduce_scatter x1, waiting for transfers between devices, body(): lax.psum_scatter(jnp.concatenate([jnp.dot(panel, gate_weight, preferred_e...  40.4 us
    reduce_scatter x1, waiting for transfers between devices, body(): lax.psum_scatter(times_transposed(grad_panel, down_weight), 'col', scatte...  32.3 us
    all_gather x1, blocking collectives, body(): lax.all_gather(gate_delta, 'col', axis=0, tiled=True)  17 us
  transfers between devices with their start and end apart: 6, of which 6 were waited for; matrix products, arithmetic and copies ran while one was open for 5% of the time, Pallas kernels for 0%

commit v1 on v0

v1 whole, which is shorter than its diff:
```python
import jax
import jax.numpy as jnp
from jax import lax
from jax.sharding import Mesh, PartitionSpec as P

BF = jnp.bfloat16
F32 = jnp.float32
NZ, NY, NX, NC = 8, 4, 4, 2


def dot(left, right, contract):
    return lax.dot_general(left, right, (contract, ((), ())), preferred_element_type=F32)


def z_order(c):
    return [(p + 4 * c) % NZ for p in range(NZ)]


Z_GROUPS = [[z * NC + c for z in z_order(c)] for c in range(NC)]


def z_exchange(blocks):
    return lax.all_to_all(blocks, ("z", "c"), 0, 0, axis_index_groups=Z_GROUPS, tiled=True)


def gather_z(block):
    return z_exchange(jnp.broadcast_to(block[None], (NZ,) + block.shape)).reshape(-1, block.shape[1])


def y_partner(y, x, d):
    return (y - x - d) % NY


def gather_y(block):
    return [
        lax.ppermute(block, ("y", "x"), [(y_partner(y, x, d) * NX + x, y * NX + x) for y in range(NY) for x in range(NX)])
        for d in range(NY)
    ]


def scatter_y(slots):
    parts = [
        lax.ppermute(slots[d], ("y", "x"), [(y * NX + x, y_partner(y, x, d) * NX + x) for y in range(NY) for x in range(NX)])
        for d in range(NY)
    ]
    return sum(part.astype(F32) for part in parts)


def swap_core(half):
    return lax.ppermute(half, "c", [(0, 1), (1, 0)])


def scatter_col(partial):
    rows = partial.reshape(NX, NC, 64, partial.shape[1])
    held = rows[:, 0] + swap_core(rows[:, 1].astype(BF)).astype(F32)
    total = held[0]
    for d in range(1, NX):
        total = total + lax.ppermute(held[d].astype(BF), "x", [(i, (i + d) % NX) for i in range(NX)]).astype(F32)
    return total


def gather_col(block):
    slots = [block] + [lax.ppermute(block, "x", [((i + d) % NX, i) for i in range(NX)]) for d in range(1, NX)]
    own = jnp.stack(slots)
    return jnp.stack([own, swap_core(own)], axis=1).reshape(512, block.shape[1])


def scatter_row(partial):
    slots = partial.astype(BF).reshape(NY, 128, partial.shape[1])
    held = scatter_y([slots[d] for d in range(NY)]).astype(BF)
    blocks = z_exchange(held.reshape(NZ, 16, partial.shape[1]))
    return blocks.astype(F32).sum(axis=0).astype(BF)


def body(tokens, gate_weight, up_weight, down_weight, out_grad):
    width = gate_weight.shape[1]
    panel = jnp.concatenate(gather_y(gather_z(tokens)))
    grad_panel = jnp.concatenate(gather_y(gather_z(out_grad)))
    both = scatter_col(
        jnp.concatenate(
            [dot(panel, gate_weight, ((1,), (0,))), dot(panel, up_weight, ((1,), (0,)))], axis=1
        )
    )
    gate_pre, up_pre = both[:, :width], both[:, width:]
    sigmoid_gate = jax.nn.sigmoid(gate_pre)
    hidden = (gate_pre * sigmoid_gate * up_pre).astype(BF)
    hidden_all = gather_col(hidden)
    hidden_grad = scatter_col(dot(grad_panel, down_weight, ((1,), (1,))))
    gate_delta = (
        hidden_grad * up_pre * sigmoid_gate * (1.0 + gate_pre * (1.0 - sigmoid_gate))
    ).astype(BF)
    up_delta = (hidden_grad * gate_pre * sigmoid_gate).astype(BF)
    deltas = gather_col(jnp.concatenate([gate_delta, up_delta], axis=1))
    gate_all, up_all = deltas[:, :width], deltas[:, width:]
    mixed = scatter_row(dot(hidden_all, down_weight, ((1,), (0,))))
    tokens_grad = scatter_row(
        dot(gate_all, gate_weight, ((1,), (1,))) + dot(up_all, up_weight, ((1,), (1,)))
    )
    down_grad = dot(hidden_all, grad_panel, ((0,), (0,))).astype(BF)
    gate_grad = dot(panel, gate_all, ((0,), (0,))).astype(BF)
    up_grad = dot(panel, up_all, ((0,), (0,))).astype(BF)
    return (mixed, tokens_grad, gate_grad, up_grad, down_grad)


def solution(mesh):
    fine = Mesh(mesh.devices.reshape(NZ, NY, NX, NC), ("z", "y", "x", "c"))
    rc = P(("z", "y"), ("x", "c"))
    cr = P(("x", "c"), ("z", "y"))
    return jax.shard_map(
        body,
        mesh=fine,
        in_specs=(rc, cr, cr, rc, rc),
        out_specs=(rc, rc, cr, cr, rc),
        check_vma=False,
    )
```

time: 720 us -> 177 us (0.25)
  waiting for transfers between devices: 614 us -> 37.8 us
  starting transfers between devices: 0.24 us -> 92.5 us
  blocking collectives: 44.2 us -> 15.8 us
  between operations: 14.2 us -> 1.2 us
  matrix products: 27.3 us -> 16.3 us
    reduce_scatter x4 -> x0, waiting for transfers between devices: 463 us -> none  [the longest x1 217 us: body(): lax.psum_scatter(jnp.dot(hidden_all, down_weight, preferred_element_type=...]
    all_gather x2 -> x0, waiting for transfers between devices: 150 us -> none  [the longest x1 77.5 us: body(): grad_panel = lax.all_gather(out_grad, 'row', axis=0, tiled=True)]
    ppermute x0 -> x32, starting transfers between devices: none -> 69.4 us  [the longest x8 22.5 us: gather_y(): lax.ppermute(block, ('y', 'x'), [(y_partner(y, x, d) * NX + x, y * NX + x...]
    all_gather x3 -> x0, blocking collectives: 44.2 us -> none  [the longest x1 17 us: body(): lax.all_gather(gate_delta, 'col', axis=0, tiled=True)]
    ppermute x0 -> x32, waiting for transfers between devices: none -> 37.8 us  [the longest x8 14.6 us: scatter_y(): lax.ppermute(slots[d], ('y', 'x'), [(y * NX + x, y_partner(y, x, d) * NX...]
    all_to_all x0 -> x3, starting transfers between devices: none -> 23.1 us  [z_exchange(): lax.all_to_all(blocks, ('z', 'c'), 0, 0, axis_index_groups=Z_GROUPS, tile...]
    all_to_all x0 -> x1, blocking collectives: none -> 15.8 us  [z_exchange(): lax.all_to_all(blocks, ('z', 'c'), 0, 0, axis_index_groups=Z_GROUPS, tile...]
    dot_general x9, matrix products: 27.3 us -> 16.3 us  [dot(): lax.dot_general(left, right, (contract, ((), ())), preferred_element_type...]
  transfers between devices with their start and end apart: 6 -> 35, of which waited for: 6 -> 15; matrix products, arithmetic and copies ran while one was open for 5% -> 13% of each run, Pallas kernels for 0% -> 0%
where the time goes in v1:
time: 177 us; the launch traced here: 176 us
  starting transfers between devices  92.5 us (52%)
  waiting for transfers between devices  37.8 us (21%)
  matrix products  16.3 us (9%)
  blocking collectives  15.8 us (9%)
  other arithmetic  6.63 us (4%)
  local copies, waits for them, and re-layouts  5.94 us (3%)
    all_to_all x3, starting transfers between devices, z_exchange(): lax.all_to_all(blocks, ('z', 'c'), 0, 0, axis_index_groups=Z_GROUPS, tile...  23.1 us
    ppermute x8, starting transfers between devices, gather_y(): lax.ppermute(block, ('y', 'x'), [(y_partner(y, x, d) * NX + x, y * NX + x...  22.5 us
    ppermute x8, starting transfers between devices, scatter_y(): lax.ppermute(slots[d], ('y', 'x'), [(y * NX + x, y_partner(y, x, d) * NX...  19.8 us
    dot_general x9, matrix products, dot(): lax.dot_general(left, right, (contract, ((), ())), preferred_element_type...  16.3 us
    all_to_all x1, blocking collectives, z_exchange(): lax.all_to_all(blocks, ('z', 'c'), 0, 0, axis_index_groups=Z_GROUPS, tile...  15.8 us
    ppermute x8, waiting for transfers between devices, scatter_y(): lax.ppermute(slots[d], ('y', 'x'), [(y * NX + x, y_partner(y, x, d) * NX...  14.6 us
    ppermute x6, waiting for transfers between devices, scatter_col(): lax.ppermute(held[d].astype(BF), 'x', [(i, (i + d) % NX) for i in range(N...  13 us
    ppermute x4, starting transfers between devices, swap_core(): return lax.ppermute(half, 'c', [(0, 1), (1, 0)])  10.5 us
  transfers between devices with their start and end apart: 35, of which 15 were waited for; matrix products, arithmetic and copies ran while one was open for 13% of the time, Pallas kernels for 0%

profile of v1, /device:TPU:1, one launch (start us, length us, event | category | flops | bytes accessed | tf_op | source)
XLA Modules:
  0.0 176.2 jit_solution(10182896984401978476)
XLA Ops:
  1.6 15.8 %all_to_all.20 = bf16[8,16,1024]{2,1,0:T(8,128)(2,1)S(1)} all-to-all(bf16[8,16,1024]{2,1,0:T(8,128)(2,1)S(1)} %broadcast_in_dim.4), channel_id=1, replica_groups={{0,32,64,96,128,160,192,224},{129,161,193,225,1,33,65,97},{2,34,66,98,1..., dimensions={0} | all-to-all | bytes 524288 | tf_op jit(solution)/shard_map/all_to_all | solution.py:23
  17.3 1.5 broadcast_in_dim.5
  18.8 9.3 %all-to-all-start.2 = ((bf16[8,16,1024]{2,1,0:T(8,128)(2,1)}), bf16[8,16,1024]{2,1,0:T(8,128)(2,1)S(1)}, u32[]{:S(2)}, u32[]{:S(2)}) async-start(bf16[8,16,1024]{2,1,0:T(8,128)(2,1)} %broadcast_in_dim.5), calls=%async_computation.2 | async-start | bytes 524288 | tf_op jit(solution)/shard_map/all_to_all | solution.py:23
  28.8 3.2 %collective-permute-start.1 = (bf16[128,1024]{1,0:T(8,128)(2,1)S(1)}, bf16[128,1024]{1,0:T(8,128)(2,1)S(1)}, u32[]{:S(2)}, u32[]{:S(2)}) collective-permute-start(bf16[128,1024]{1,0:T(8,128)(2,1)S(1)} %bitcast.102), channel_id=1, source_target_pairs={{24,0},{18,2},{12,4},{6,6},{0,8},{26,10},{20,12},{14,14},{8,16},{2... | collective-permute-start | bytes 786440 | tf_op jit(solution)/shard_map/ppermute | solution.py:36
  32.0 4.5 %collective-permute-start.2 = (bf16[128,1024]{1,0:T(8,128)(2,1)S(1)}, bf16[128,1024]{1,0:T(8,128)(2,1)S(1)}, u32[]{:S(2)}, u32[]{:S(2)}) collective-permute-start(bf16[128,1024]{1,0:T(8,128)(2,1)S(1)} %bitcast.103), channel_id=1, source_target_pairs={{16,0},{10,2},{4,4},{30,6},{24,8},{18,10},{12,12},{6,14},{0,16},{2... | collective-permute-start | bytes 786440 | tf_op jit(solution)/shard_map/ppermute | solution.py:36
  36.5 3.0 %collective-permute-start.3 = (bf16[128,1024]{1,0:T(8,128)(2,1)S(1)}, bf16[128,1024]{1,0:T(8,128)(2,1)S(1)}, u32[]{:S(2)}, u32[]{:S(2)}) collective-permute-start(bf16[128,1024]{1,0:T(8,128)(2,1)S(1)} %bitcast.104), channel_id=1, source_target_pairs={{8,0},{2,2},{28,4},{22,6},{16,8},{10,10},{4,12},{30,14},{24,16},{1... | collective-permute-start | bytes 786440 | tf_op jit(solution)/shard_map/ppermute | solution.py:36
  40.4 2.3 %collective-permute-start.17 = (bf16[128,1024]{1,0:T(8,128)(2,1)S(1)}, bf16[128,1024]{1,0:T(8,128)(2,1)S(1)}, u32[]{:S(2)}, u32[]{:S(2)}) collective-permute-start(bf16[128,1024]{1,0:T(8,128)(2,1)S(1)} %bitcast.98), channel_id=1, source_target_pairs={{24,0},{18,2},{12,4},{6,6},{0,8},{26,10},{20,12},{14,14},{8,16},{2... | collective-permute-start | bytes 786440 | tf_op jit(solution)/shard_map/ppermute | solution.py:36
  42.7 6.1 %collective-permute-start.18 = (bf16[128,1024]{1,0:T(8,128)(2,1)S(1)}, bf16[128,1024]{1,0:T(8,128)(2,1)S(1)}, u32[]{:S(2)}, u32[]{:S(2)}) collective-permute-start(bf16[128,1024]{1,0:T(8,128)(2,1)S(1)} %bitcast.99), channel_id=1, source_target_pairs={{16,0},{10,2},{4,4},{30,6},{24,8},{18,10},{12,12},{6,14},{0,16},{2... | collective-permute-start | bytes 786440 | tf_op jit(solution)/shard_map/ppermute | solution.py:36
  48.9 1.9 %collective-permute-start.19 = (bf16[128,1024]{1,0:T(8,128)(2,1)S(1)}, bf16[128,1024]{1,0:T(8,128)(2,1)S(1)}, u32[]{:S(2)}, u32[]{:S(2)}) collective-permute-start(bf16[128,1024]{1,0:T(8,128)(2,1)S(1)} %bitcast.100), channel_id=1, source_target_pairs={{8,0},{2,2},{28,4},{22,6},{16,8},{10,10},{4,12},{30,14},{24,16},{1... | collective-permute-start | bytes 786440 | tf_op jit(solution)/shard_map/ppermute | solution.py:36
  50.9 1.2 fusion.25
  52.8 1.2 fusion.24
  54.6 2.9 %collective-permute-done.18 = bf16[128,1024]{1,0:T(8,128)(2,1)S(1)} collective-permute-done((bf16[128,1024]{1,0:T(8,128)(2,1)S(1)}, bf16[128,1024]{1,0:T(8,128)(2,1)S(1)}, u32[]{:S(2)}, u32[]{:S(2)}) %collective-permute-start.18) | collective-permute-done | bytes 262176 | tf_op jit(solution)/shard_map/ppermute | solution.py:36
  57.6 2.0 %collective-permute-done.19 = bf16[128,1024]{1,0:T(8,128)(2,1)S(1)} collective-permute-done((bf16[128,1024]{1,0:T(8,128)(2,1)S(1)}, bf16[128,1024]{1,0:T(8,128)(2,1)S(1)}, u32[]{:S(2)}, u32[]{:S(2)}) %collective-permute-start.19) | collective-permute-done | bytes 262176 | tf_op jit(solution)/shard_map/ppermute | solution.py:36
  59.6 1.3 fusion.26
  61.9 1.4 collective-permute-done.20
  63.8 4.7 %collective-permute-start.7 = (bf16[64,1792]{1,0:T(8,128)(2,1)S(1)}, bf16[64,1792]{1,0:T(8,128)(2,1)S(1)}, u32[]{:S(2)}, u32[]{:S(2)}) collective-permute-start(bf16[64,1792]{1,0:T(8,128)(2,1)S(1)} %get-tuple-element.22), channel_id=1, source_target_pairs={{0,6},{2,0},{4,2},{6,4},{1,7},{3,1},{5,3},{7,5},{8,14},{10,8},{12,... | collective-permute-start | bytes 688136 | tf_op jit(solution)/shard_map/ppermute | solution.py:58
  69.3 2.1 %collective-permute-start.23 = (bf16[64,896]{1,0:T(8,128)(2,1)S(1)}, bf16[64,896]{1,0:T(8,128)(2,1)S(1)}, u32[]{:S(2)}, u32[]{:S(2)}) collective-permute-start(bf16[64,896]{1,0:T(8,128)(2,1)S(1)} %get-tuple-element.26), channel_id=1, source_target_pairs={{0,6},{2,0},{4,2},{6,4},{1,7},{3,1},{5,3},{7,5},{8,14},{10,8},{12,... | collective-permute-start | bytes 344072 | tf_op jit(solution)/shard_map/ppermute | solution.py:58
  71.4 1.8 collective-permute-start.22
  73.1 5.7 %collective-permute-done.7 = bf16[64,1792]{1,0:T(8,128)(2,1)S(1)} collective-permute-done((bf16[64,1792]{1,0:T(8,128)(2,1)S(1)}, bf16[64,1792]{1,0:T(8,128)(2,1)S(1)}, u32[]{:S(2)}, u32[]{:S(2)}) %collective-permute-start.7) | collective-permute-done | bytes 229408 | tf_op jit(solution)/shard_map/ppermute | solution.py:58
  78.8 3.5 %collective-permute-done.5 = bf16[64,1792]{1,0:T(8,128)(2,1)S(1)} collective-permute-done((bf16[64,1792]{1,0:T(8,128)(2,1)S(1)}, bf16[64,1792]{1,0:T(8,128)(2,1)S(1)}, u32[]{:S(2)}, u32[]{:S(2)}) %collective-permute-start.5) | collective-permute-done | bytes 229408 | tf_op jit(solution)/shard_map/ppermute | solution.py:58
  84.0 2.2 %collective-permute-done.21 = bf16[64,896]{1,0:T(8,128)(2,1)S(1)} collective-permute-done((bf16[64,896]{1,0:T(8,128)(2,1)S(1)}, bf16[64,896]{1,0:T(8,128)(2,1)S(1)}, u32[]{:S(2)}, u32[]{:S(2)}) %collective-permute-start.21) | collective-permute-done | bytes 114720 | tf_op jit(solution)/shard_map/ppermute | solution.py:58
  86.5 2.6 %collective-permute-start.9 = (bf16[64,896]{1,0:T(8,128)(2,1)S(1)}, bf16[64,896]{1,0:T(8,128)(2,1)S(1)}, u32[]{:S(2)}, u32[]{:S(2)}) collective-permute-start(bf16[64,896]{1,0:T(8,128)(2,1)S(1)} %get-tuple-element.24), channel_id=1, source_target_pairs={{4,0},{6,2},{0,4},{2,6},{5,1},{7,3},{1,5},{3,7},{12,8},{14,10},{8,... | collective-permute-start | bytes 344072 | tf_op jit(solution)/shard_map/ppermute | solution.py:63
  90.7 1.0 collective-permute-start.25
  91.8 2.0 %collective-permute-start.24 = (bf16[64,1792]{1,0:T(8,128)(2,1)S(1)}, bf16[64,1792]{1,0:T(8,128)(2,1)S(1)}, u32[]{:S(2)}, u32[]{:S(2)}) collective-permute-start(bf16[64,1792]{1,0:T(8,128)(2,1)S(1)} %get-tuple-element.31), channel_id=1, source_target_pairs={{2,0},{4,2},{6,4},{0,6},{3,1},{5,3},{7,5},{1,7},{10,8},{12,10},{14... | collective-permute-start | bytes 688136 | tf_op jit(solution)/shard_map/ppermute | solution.py:63
  93.8 6.7 %collective-permute-start.11 = (bf16[4,64,896]{2,1,0:T(8,128)(2,1)S(1)}, bf16[4,64,896]{2,1,0:T(8,128)(2,1)S(1)}, u32[]{:S(2)}, u32[]{:S(2)}) collective-permute-start(bf16[4,64,896]{2,1,0:T(8,128)(2,1)S(1)} %get-tuple-element.29), channel_id=1, source_target_pairs={{0,1},{1,0},{2,3},{3,2},{4,5},{5,4},{6,7},{7,6},{8,9},{9,8},{10,11... | collective-permute-start | bytes 1376264 | tf_op jit(solution)/shard_map/ppermute | solution.py:50
  101.6 2.7 %collective-permute-done.24 = bf16[64,1792]{1,0:T(8,128)(2,1)S(1)} collective-permute-done((bf16[64,1792]{1,0:T(8,128)(2,1)S(1)}, bf16[64,1792]{1,0:T(8,128)(2,1)S(1)}, u32[]{:S(2)}, u32[]{:S(2)}) %collective-permute-start.24) | collective-permute-done | bytes 229408 | tf_op jit(solution)/shard_map/ppermute | solution.py:63
  104.3 1.1 fusion.17
  105.4 2.8 %collective-permute-start.27 = (bf16[4,64,1792]{2,1,0:T(8,128)(2,1)}, bf16[4,64,1792]{2,1,0:T(8,128)(2,1)}, u32[]{:S(2)}, u32[]{:S(2)}) collective-permute-start(bf16[4,64,1792]{2,1,0:T(8,128)(2,1)} %get-tuple-element.20), channel_id=1, source_target_pairs={{0,1},{1,0},{2,3},{3,2},{4,5},{5,4},{6,7},{7,6},{8,9},{9,8},{10,11... | collective-permute-start | bytes 2752520 | tf_op jit(solution)/shard_map/ppermute | solution.py:50
  108.3 1.3 convolution_convert_fusion.3
  109.7 1.9 %collective-permute-start.15 = (bf16[128,1024]{1,0:T(8,128)(2,1)S(1)}, bf16[128,1024]{1,0:T(8,128)(2,1)S(1)}, u32[]{:S(2)}, u32[]{:S(2)}) collective-permute-start(bf16[128,1024]{1,0:T(8,128)(2,1)S(1)} %get-tuple-element.16), channel_id=1, source_target_pairs={{0,8},{2,2},{4,28},{6,22},{8,16},{10,10},{12,4},{14,30},{16,24},{1... | collective-permute-start | bytes 786440 | tf_op jit(solution)/shard_map/ppermute | solution.py:43
  111.6 1.9 %collective-permute-start.14 = (bf16[128,1024]{1,0:T(8,128)(2,1)S(1)}, bf16[128,1024]{1,0:T(8,128)(2,1)S(1)}, u32[]{:S(2)}, u32[]{:S(2)}) collective-permute-start(bf16[128,1024]{1,0:T(8,128)(2,1)S(1)} %get-tuple-element.17), channel_id=1, source_target_pairs={{0,16},{2,10},{4,4},{6,30},{8,24},{10,18},{12,12},{14,6},{16,0},{1... | collective-permute-start | bytes 786440 | tf_op jit(solution)/shard_map/ppermute | solution.py:43
  113.5 4.6 %collective-permute-start.13 = (bf16[128,1024]{1,0:T(8,128)(2,1)S(1)}, bf16[128,1024]{1,0:T(8,128)(2,1)S(1)}, u32[]{:S(2)}, u32[]{:S(2)}) collective-permute-start(bf16[128,1024]{1,0:T(8,128)(2,1)S(1)} %get-tuple-element.18), channel_id=1, source_target_pairs={{0,24},{2,18},{4,12},{6,6},{8,0},{10,26},{12,20},{14,14},{16,8},{1... | collective-permute-start | bytes 786440 | tf_op jit(solution)/shard_map/ppermute | solution.py:43
  118.8 7.5 %collective-permute-done.15 = bf16[128,1024]{1,0:T(8,128)(2,1)S(1)} collective-permute-done((bf16[128,1024]{1,0:T(8,128)(2,1)S(1)}, bf16[128,1024]{1,0:T(8,128)(2,1)S(1)}, u32[]{:S(2)}, u32[]{:S(2)}) %collective-permute-start.15) | collective-permute-done | bytes 262176 | tf_op jit(solution)/shard_map/ppermute | solution.py:43
  126.3 2.2 %collective-permute-done.13 = bf16[128,1024]{1,0:T(8,128)(2,1)S(1)} collective-permute-done((bf16[128,1024]{1,0:T(8,128)(2,1)S(1)}, bf16[128,1024]{1,0:T(8,128)(2,1)S(1)}, u32[]{:S(2)}, u32[]{:S(2)}) %collective-permute-start.13) | collective-permute-done | bytes 262176 | tf_op jit(solution)/shard_map/ppermute | solution.py:43
  129.4 6.6 %all-to-all-start.1 = ((bf16[8,16,1024]{2,1,0:T(8,128)(2,1)}), bf16[8,16,1024]{2,1,0:T(8,128)(2,1)S(1)}, u32[]{:S(2)}, u32[]{:S(2)}) async-start(bf16[8,16,1024]{2,1,0:T(8,128)(2,1)} %bitcast.16), calls=%async_computation.1 | async-start | bytes 524288 | tf_op jit(solution)/shard_map/all_to_all | solution.py:23
  136.1 1.3 pad_maximum_fusion.1
  137.6 2.0 %copy-done.10 = bf16[1024,896]{1,0:T(8,128)(2,1)S(1)} copy-done((bf16[1024,896]{1,0:T(8,128)(2,1)S(1)}, bf16[1024,896]{1,0:T(8,128)(2,1)}, u32[]{:S(2)}) %copy-start.10) | copy-done | bytes 1835032
  139.6 1.3 fusion.6
  141.1 1.3 add_convert_fusion
  142.5 2.6 %collective-permute-start.31 = (bf16[128,1024]{1,0:T(8,128)(2,1)S(1)}, bf16[128,1024]{1,0:T(8,128)(2,1)S(1)}, u32[]{:S(2)}, u32[]{:S(2)}) collective-permute-start(bf16[128,1024]{1,0:T(8,128)(2,1)S(1)} %get-tuple-element.12), channel_id=1, source_target_pairs={{0,8},{2,2},{4,28},{6,22},{8,16},{10,10},{12,4},{14,30},{16,24},{1... | collective-permute-start | bytes 786440 | tf_op jit(solution)/shard_map/ppermute | solution.py:43
  145.1 5.5 %collective-permute-start.30 = (bf16[128,1024]{1,0:T(8,128)(2,1)S(1)}, bf16[128,1024]{1,0:T(8,128)(2,1)S(1)}, u32[]{:S(2)}, u32[]{:S(2)}) collective-permute-start(bf16[128,1024]{1,0:T(8,128)(2,1)S(1)} %get-tuple-element.13), channel_id=1, source_target_pairs={{0,16},{2,10},{4,4},{6,30},{8,24},{10,18},{12,12},{14,6},{16,0},{1... | collective-permute-start | bytes 786440 | tf_op jit(solution)/shard_map/ppermute | solution.py:43
  150.6 1.9 %collective-permute-start.29 = (bf16[128,1024]{1,0:T(8,128)(2,1)S(1)}, bf16[128,1024]{1,0:T(8,128)(2,1)S(1)}, u32[]{:S(2)}, u32[]{:S(2)}) collective-permute-start(bf16[128,1024]{1,0:T(8,128)(2,1)S(1)} %get-tuple-element.14), channel_id=1, source_target_pairs={{0,24},{2,18},{4,12},{6,6},{8,0},{10,26},{12,20},{14,14},{16,8},{1... | collective-permute-start | bytes 786440 | tf_op jit(solution)/shard_map/ppermute | solution.py:43
  153.3 2.4 %convolution_convert_fusion = bf16[896,1024]{1,0:T(8,128)(2,1)} fusion(bf16[512,896]{1,0:T(8,128)(2,1)S(1)} %bitcast.94, bf16[512,1024]{1,0:T(8,128)(2,1)S(1)} %copy-done.8), kind=kOutput, calls=%fused_computation.6 | convolution fusion | flops 940441600 | bytes 3801088 | tf_op jit(solution)/shard_map/dot_general | solution.py:12
  155.6 2.9 %collective-permute-done.30 = bf16[128,1024]{1,0:T(8,128)(2,1)S(1)} collective-permute-done((bf16[128,1024]{1,0:T(8,128)(2,1)S(1)}, bf16[128,1024]{1,0:T(8,128)(2,1)S(1)}, u32[]{:S(2)}, u32[]{:S(2)}) %collective-permute-start.30) | collective-permute-done | bytes 262176 | tf_op jit(solution)/shard_map/ppermute | solution.py:43
  158.6 1.9 %collective-permute-done.29 = bf16[128,1024]{1,0:T(8,128)(2,1)S(1)} collective-permute-done((bf16[128,1024]{1,0:T(8,128)(2,1)S(1)}, bf16[128,1024]{1,0:T(8,128)(2,1)S(1)}, u32[]{:S(2)}, u32[]{:S(2)}) %collective-permute-start.29) | collective-permute-done | bytes 262176 | tf_op jit(solution)/shard_map/ppermute | solution.py:43
  161.4 7.2 %all-to-all-start.3 = ((bf16[8,16,1024]{2,1,0:T(8,128)(2,1)}), bf16[8,16,1024]{2,1,0:T(8,128)(2,1)S(1)}, u32[]{:S(2)}, u32[]{:S(2)}) async-start(bf16[8,16,1024]{2,1,0:T(8,128)(2,1)} %bitcast.32), calls=%async_computation.3 | async-start | bytes 524288 | tf_op jit(solution)/shard_map/all_to_all | solution.py:23
  168.5 3.8 %convolution_convert_fusion.2 = bf16[1024,896]{1,0:T(8,128)(2,1)} fusion(bf16[512,1024]{1,0:T(8,128)(2,1)S(1)} %copy-done.6, bf16[512,1792]{1,0:T(8,128)(2,1)} %bitcast.89), kind=kOutput, calls=%fused_computation.8 | convolution fusion | flops 940441600 | bytes 3801088 | tf_op jit(solution)/shard_map/dot_general | solution.py:12
  172.4 2.5 %convolution_convert_fusion.1 = bf16[1024,896]{1,0:T(8,128)(2,1)} fusion(bf16[512,1024]{1,0:T(8,128)(2,1)S(1)} %copy-done.6, bf16[512,1792]{1,0:T(8,128)(2,1)S(1)} %bitcast.90), kind=kOutput, calls=%fused_computation.7 | convolution fusion | flops 940441600 | bytes 3801088 | tf_op jit(solution)/shard_map/dot_general | solution.py:12
  (89 shorter events, 15.6 us)
Async XLA Ops:
  0.6 59.0 %copy-start = (bf16[896,1024]{1,0:T(8,128)(2,1)S(1)}, bf16[896,1024]{1,0:T(8,128)(2,1)}, u32[]{:S(2)}) copy-start(bf16[896,1024]{1,0:T(8,128)(2,1)} %param.8) | copy-start | bytes 5505028
  18.8 20.7 %all-to-all-start.2 = ((bf16[8,16,1024]{2,1,0:T(8,128)(2,1)}), bf16[8,16,1024]{2,1,0:T(8,128)(2,1)S(1)}, u32[]{:S(2)}, u32[]{:S(2)}) async-start(bf16[8,16,1024]{2,1,0:T(8,128)(2,1)} %broadcast_in_dim.5), calls=%async_computation.2 | async-start | bytes 524288 | tf_op jit(solution)/shard_map/all_to_all | solution.py:23
  28.1 12.2 %collective-permute-start = (bf16[128,1024]{1,0:T(8,128)(2,1)S(1)}, bf16[128,1024]{1,0:T(8,128)(2,1)S(1)}, u32[]{:S(2)}, u32[]{:S(2)}) collective-permute-start(bf16[128,1024]{1,0:T(8,128)(2,1)S(1)} %bitcast.101), channel_id=1, source_target_pairs={{0,0},{26,2},{20,4},{14,6},{8,8},{2,10},{28,12},{22,14},{16,16},{1... | collective-permute-start | bytes 786440 | tf_op jit(solution)/shard_map/ppermute | solution.py:36
  28.8 13.9 %collective-permute-start.1 = (bf16[128,1024]{1,0:T(8,128)(2,1)S(1)}, bf16[128,1024]{1,0:T(8,128)(2,1)S(1)}, u32[]{:S(2)}, u32[]{:S(2)}) collective-permute-start(bf16[128,1024]{1,0:T(8,128)(2,1)S(1)} %bitcast.102), channel_id=1, source_target_pairs={{24,0},{18,2},{12,4},{6,6},{0,8},{26,10},{20,12},{14,14},{8,16},{2... | collective-permute-start | bytes 786440 | tf_op jit(solution)/shard_map/ppermute | solution.py:36
  32.0 16.9 %collective-permute-start.2 = (bf16[128,1024]{1,0:T(8,128)(2,1)S(1)}, bf16[128,1024]{1,0:T(8,128)(2,1)S(1)}, u32[]{:S(2)}, u32[]{:S(2)}) collective-permute-start(bf16[128,1024]{1,0:T(8,128)(2,1)S(1)} %bitcast.103), channel_id=1, source_target_pairs={{16,0},{10,2},{4,4},{30,6},{24,8},{18,10},{12,12},{6,14},{0,16},{2... | collective-permute-start | bytes 786440 | tf_op jit(solution)/shard_map/ppermute | solution.py:36
  36.5 14.3 %collective-permute-start.3 = (bf16[128,1024]{1,0:T(8,128)(2,1)S(1)}, bf16[128,1024]{1,0:T(8,128)(2,1)S(1)}, u32[]{:S(2)}, u32[]{:S(2)}) collective-permute-start(bf16[128,1024]{1,0:T(8,128)(2,1)S(1)} %bitcast.104), channel_id=1, source_target_pairs={{8,0},{2,2},{28,4},{22,6},{16,8},{10,10},{4,12},{30,14},{24,16},{1... | collective-permute-start | bytes 786440 | tf_op jit(solution)/shard_map/ppermute | solution.py:36
  39.5 11.4 %copy-start.11 = (bf16[1024,896]{1,0:T(8,128)(2,1)S(1)}, bf16[1024,896]{1,0:T(8,128)(2,1)}, u32[]{:S(2)}) copy-start(bf16[1024,896]{1,0:T(8,128)(2,1)} %param.7) | copy-start | bytes 5505028
  39.6 15.0 %collective-permute-start.16 = (bf16[128,1024]{1,0:T(8,128)(2,1)S(1)}, bf16[128,1024]{1,0:T(8,128)(2,1)S(1)}, u32[]{:S(2)}, u32[]{:S(2)}) collective-permute-start(bf16[128,1024]{1,0:T(8,128)(2,1)S(1)} %bitcast.97), channel_id=1, source_target_pairs={{0,0},{26,2},{20,4},{14,6},{8,8},{2,10},{28,12},{22,14},{16,16},{1... | collective-permute-start | bytes 786440 | tf_op jit(solution)/shard_map/ppermute | solution.py:36
  40.4 14.2 %collective-permute-start.17 = (bf16[128,1024]{1,0:T(8,128)(2,1)S(1)}, bf16[128,1024]{1,0:T(8,128)(2,1)S(1)}, u32[]{:S(2)}, u32[]{:S(2)}) collective-permute-start(bf16[128,1024]{1,0:T(8,128)(2,1)S(1)} %bitcast.98), channel_id=1, source_target_pairs={{24,0},{18,2},{12,4},{6,6},{0,8},{26,10},{20,12},{14,14},{8,16},{2... | collective-permute-start | bytes 786440 | tf_op jit(solution)/shard_map/ppermute | solution.py:36
  42.7 14.8 %collective-permute-start.18 = (bf16[128,1024]{1,0:T(8,128)(2,1)S(1)}, bf16[128,1024]{1,0:T(8,128)(2,1)S(1)}, u32[]{:S(2)}, u32[]{:S(2)}) collective-permute-start(bf16[128,1024]{1,0:T(8,128)(2,1)S(1)} %bitcast.99), channel_id=1, source_target_pairs={{16,0},{10,2},{4,4},{30,6},{24,8},{18,10},{12,12},{6,14},{0,16},{2... | collective-permute-start | bytes 786440 | tf_op jit(solution)/shard_map/ppermute | solution.py:36
  48.9 10.7 %collective-permute-start.19 = (bf16[128,1024]{1,0:T(8,128)(2,1)S(1)}, bf16[128,1024]{1,0:T(8,128)(2,1)S(1)}, u32[]{:S(2)}, u32[]{:S(2)}) collective-permute-start(bf16[128,1024]{1,0:T(8,128)(2,1)S(1)} %bitcast.100), channel_id=1, source_target_pairs={{8,0},{2,2},{28,4},{22,6},{16,8},{10,10},{4,12},{30,14},{24,16},{1... | collective-permute-start | bytes 786440 | tf_op jit(solution)/shard_map/ppermute | solution.py:36
  50.9 1.3 copy-start.5
  50.9 1.9 %copy-start.9 = (bf16[1024,896]{1,0:T(8,128)(2,1)S(1)}, bf16[1024,896]{1,0:T(8,128)(2,1)}, u32[]{:S(2)}) copy-start(bf16[1024,896]{1,0:T(8,128)(2,1)} %param.6) | copy-start | bytes 5505028
  54.4 9.1 %collective-permute-start.4 = (bf16[4,64,1792]{2,1,0:T(8,128)(2,1)S(1)}, bf16[4,64,1792]{2,1,0:T(8,128)(2,1)S(1)}, u32[]{:S(2)}, u32[]{:S(2)}) collective-permute-start(bf16[4,64,1792]{2,1,0:T(8,128)(2,1)S(1)} %fusion.1), channel_id=1, source_target_pairs={{0,1},{1,0},{2,3},{3,2},{4,5},{5,4},{6,7},{7,6},{8,9},{9,8},{10,11... | collective-permute-start | bytes 2752520 | tf_op jit(solution)/shard_map/ppermute | solution.py:50
  59.6 1.3 copy-start.7
  61.0 2.4 %collective-permute-start.20 = (bf16[4,64,896]{2,1,0:T(8,128)(2,1)S(1)}, bf16[4,64,896]{2,1,0:T(8,128)(2,1)S(1)}, u32[]{:S(2)}, u32[]{:S(2)}) collective-permute-start(bf16[4,64,896]{2,1,0:T(8,128)(2,1)S(1)} %fusion.8), channel_id=1, source_target_pairs={{0,1},{1,0},{2,3},{3,2},{4,5},{5,4},{6,7},{7,6},{8,9},{9,8},{10,11... | collective-permute-start | bytes 1376264 | tf_op jit(solution)/shard_map/ppermute | solution.py:50
  63.8 14.9 %collective-permute-start.7 = (bf16[64,1792]{1,0:T(8,128)(2,1)S(1)}, bf16[64,1792]{1,0:T(8,128)(2,1)S(1)}, u32[]{:S(2)}, u32[]{:S(2)}) collective-permute-start(bf16[64,1792]{1,0:T(8,128)(2,1)S(1)} %get-tuple-element.22), channel_id=1, source_target_pairs={{0,6},{2,0},{4,2},{6,4},{1,7},{3,1},{5,3},{7,5},{8,14},{10,8},{12,... | collective-permute-start | bytes 688136 | tf_op jit(solution)/shard_map/ppermute | solution.py:58
  68.6 10.2 %collective-permute-start.6 = (bf16[64,1792]{1,0:T(8,128)(2,1)S(1)}, bf16[64,1792]{1,0:T(8,128)(2,1)S(1)}, u32[]{:S(2)}, u32[]{:S(2)}) collective-permute-start(bf16[64,1792]{1,0:T(8,128)(2,1)S(1)} %get-tuple-element.23), channel_id=1, source_target_pairs={{0,4},{2,6},{4,0},{6,2},{1,5},{3,7},{5,1},{7,3},{8,12},{10,14},{12... | collective-permute-start | bytes 688136 | tf_op jit(solution)/shard_map/ppermute | solution.py:58
  68.6 13.7 %collective-permute-start.5 = (bf16[64,1792]{1,0:T(8,128)(2,1)S(1)}, bf16[64,1792]{1,0:T(8,128)(2,1)S(1)}, u32[]{:S(2)}, u32[]{:S(2)}) collective-permute-start(bf16[64,1792]{1,0:T(8,128)(2,1)S(1)} %get-tuple-element.21), channel_id=1, source_target_pairs={{0,2},{2,4},{4,6},{6,0},{1,3},{3,5},{5,7},{7,1},{8,10},{10,12},{12... | collective-permute-start | bytes 688136 | tf_op jit(solution)/shard_map/ppermute | solution.py:58
  69.3 13.8 %collective-permute-start.23 = (bf16[64,896]{1,0:T(8,128)(2,1)S(1)}, bf16[64,896]{1,0:T(8,128)(2,1)S(1)}, u32[]{:S(2)}, u32[]{:S(2)}) collective-permute-start(bf16[64,896]{1,0:T(8,128)(2,1)S(1)} %get-tuple-element.26), channel_id=1, source_target_pairs={{0,6},{2,0},{4,2},{6,4},{1,7},{3,1},{5,3},{7,5},{8,14},{10,8},{12,... | collective-permute-start | bytes 344072 | tf_op jit(solution)/shard_map/ppermute | solution.py:58
  71.4 12.7 %collective-permute-start.22 = (bf16[64,896]{1,0:T(8,128)(2,1)S(1)}, bf16[64,896]{1,0:T(8,128)(2,1)S(1)}, u32[]{:S(2)}, u32[]{:S(2)}) collective-permute-start(bf16[64,896]{1,0:T(8,128)(2,1)S(1)} %get-tuple-element.27), channel_id=1, source_target_pairs={{0,4},{2,6},{4,0},{6,2},{1,5},{3,7},{5,1},{7,3},{8,12},{10,14},{12... | collective-permute-start | bytes 344072 | tf_op jit(solution)/shard_map/ppermute | solution.py:58
  78.8 7.5 %collective-permute-start.21 = (bf16[64,896]{1,0:T(8,128)(2,1)S(1)}, bf16[64,896]{1,0:T(8,128)(2,1)S(1)}, u32[]{:S(2)}, u32[]{:S(2)}) collective-permute-start(bf16[64,896]{1,0:T(8,128)(2,1)S(1)} %get-tuple-element.25), channel_id=1, source_target_pairs={{0,2},{2,4},{4,6},{6,0},{1,3},{3,5},{5,7},{7,1},{8,10},{10,12},{12... | collective-permute-start | bytes 344072 | tf_op jit(solution)/shard_map/ppermute | solution.py:58
  86.4 5.3 %collective-permute-start.10 = (bf16[64,896]{1,0:T(8,128)(2,1)S(1)}, bf16[64,896]{1,0:T(8,128)(2,1)S(1)}, u32[]{:S(2)}, u32[]{:S(2)}) collective-permute-start(bf16[64,896]{1,0:T(8,128)(2,1)S(1)} %get-tuple-element.24), channel_id=1, source_target_pairs={{6,0},{0,2},{2,4},{4,6},{7,1},{1,3},{3,5},{5,7},{14,8},{8,10},{10,... | collective-permute-start | bytes 344072 | tf_op jit(solution)/shard_map/ppermute | solution.py:63
  86.5 7.2 %collective-permute-start.9 = (bf16[64,896]{1,0:T(8,128)(2,1)S(1)}, bf16[64,896]{1,0:T(8,128)(2,1)S(1)}, u32[]{:S(2)}, u32[]{:S(2)}) collective-permute-start(bf16[64,896]{1,0:T(8,128)(2,1)S(1)} %get-tuple-element.24), channel_id=1, source_target_pairs={{4,0},{6,2},{0,4},{2,6},{5,1},{7,3},{1,5},{3,7},{12,8},{14,10},{8,... | collective-permute-start | bytes 344072 | tf_op jit(solution)/shard_map/ppermute | solution.py:63
  89.2 4.6 %collective-permute-start.8 = (bf16[64,896]{1,0:T(8,128)(2,1)S(1)}, bf16[64,896]{1,0:T(8,128)(2,1)S(1)}, u32[]{:S(2)}, u32[]{:S(2)}) collective-permute-start(bf16[64,896]{1,0:T(8,128)(2,1)S(1)} %get-tuple-element.24), channel_id=1, source_target_pairs={{2,0},{4,2},{6,4},{0,6},{3,1},{5,3},{7,5},{1,7},{10,8},{12,10},{14... | collective-permute-start | bytes 344072 | tf_op jit(solution)/shard_map/ppermute | solution.py:63
  89.8 11.1 %collective-permute-start.26 = (bf16[64,1792]{1,0:T(8,128)(2,1)S(1)}, bf16[64,1792]{1,0:T(8,128)(2,1)S(1)}, u32[]{:S(2)}, u32[]{:S(2)}) collective-permute-start(bf16[64,1792]{1,0:T(8,128)(2,1)S(1)} %get-tuple-element.31), channel_id=1, source_target_pairs={{6,0},{0,2},{2,4},{4,6},{7,1},{1,3},{3,5},{5,7},{14,8},{8,10},{10,... | collective-permute-start | bytes 688136 | tf_op jit(solution)/shard_map/ppermute | solution.py:63
  90.7 10.9 %collective-permute-start.25 = (bf16[64,1792]{1,0:T(8,128)(2,1)S(1)}, bf16[64,1792]{1,0:T(8,128)(2,1)S(1)}, u32[]{:S(2)}, u32[]{:S(2)}) collective-permute-start(bf16[64,1792]{1,0:T(8,128)(2,1)S(1)} %get-tuple-element.31), channel_id=1, source_target_pairs={{4,0},{6,2},{0,4},{2,6},{5,1},{7,3},{1,5},{3,7},{12,8},{14,10},{8,... | collective-permute-start | bytes 688136 | tf_op jit(solution)/shard_map/ppermute | solution.py:63
  91.8 12.6 %collective-permute-start.24 = (bf16[64,1792]{1,0:T(8,128)(2,1)S(1)}, bf16[64,1792]{1,0:T(8,128)(2,1)S(1)}, u32[]{:S(2)}, u32[]{:S(2)}) collective-permute-start(bf16[64,1792]{1,0:T(8,128)(2,1)S(1)} %get-tuple-element.31), channel_id=1, source_target_pairs={{2,0},{4,2},{6,4},{0,6},{3,1},{5,3},{7,5},{1,7},{10,8},{12,10},{14... | collective-permute-start | bytes 688136 | tf_op jit(solution)/shard_map/ppermute | solution.py:63
  93.8 14.3 %collective-permute-start.11 = (bf16[4,64,896]{2,1,0:T(8,128)(2,1)S(1)}, bf16[4,64,896]{2,1,0:T(8,128)(2,1)S(1)}, u32[]{:S(2)}, u32[]{:S(2)}) collective-permute-start(bf16[4,64,896]{2,1,0:T(8,128)(2,1)S(1)} %get-tuple-element.29), channel_id=1, source_target_pairs={{0,1},{1,0},{2,3},{3,2},{4,5},{5,4},{6,7},{7,6},{8,9},{9,8},{10,11... | collective-permute-start | bytes 1376264 | tf_op jit(solution)/shard_map/ppermute | solution.py:50
  105.4 30.7 %collective-permute-start.27 = (bf16[4,64,1792]{2,1,0:T(8,128)(2,1)}, bf16[4,64,1792]{2,1,0:T(8,128)(2,1)}, u32[]{:S(2)}, u32[]{:S(2)}) collective-permute-start(bf16[4,64,1792]{2,1,0:T(8,128)(2,1)} %get-tuple-element.20), channel_id=1, source_target_pairs={{0,1},{1,0},{2,3},{3,2},{4,5},{5,4},{6,7},{7,6},{8,9},{9,8},{10,11... | collective-permute-start | bytes 2752520 | tf_op jit(solution)/shard_map/ppermute | solution.py:50
  108.3 1.3 copy-start.3
  109.7 16.7 %collective-permute-start.15 = (bf16[128,1024]{1,0:T(8,128)(2,1)S(1)}, bf16[128,1024]{1,0:T(8,128)(2,1)S(1)}, u32[]{:S(2)}, u32[]{:S(2)}) collective-permute-start(bf16[128,1024]{1,0:T(8,128)(2,1)S(1)} %get-tuple-element.16), channel_id=1, source_target_pairs={{0,8},{2,2},{4,28},{6,22},{8,16},{10,10},{12,4},{14,30},{16,24},{1... | collective-permute-start | bytes 786440 | tf_op jit(solution)/shard_map/ppermute | solution.py:43
  111.6 14.7 %collective-permute-start.14 = (bf16[128,1024]{1,0:T(8,128)(2,1)S(1)}, bf16[128,1024]{1,0:T(8,128)(2,1)S(1)}, u32[]{:S(2)}, u32[]{:S(2)}) collective-permute-start(bf16[128,1024]{1,0:T(8,128)(2,1)S(1)} %get-tuple-element.17), channel_id=1, source_target_pairs={{0,16},{2,10},{4,4},{6,30},{8,24},{10,18},{12,12},{14,6},{16,0},{1... | collective-permute-start | bytes 786440 | tf_op jit(solution)/shard_map/ppermute | solution.py:43
  113.5 15.0 %collective-permute-start.13 = (bf16[128,1024]{1,0:T(8,128)(2,1)S(1)}, bf16[128,1024]{1,0:T(8,128)(2,1)S(1)}, u32[]{:S(2)}, u32[]{:S(2)}) collective-permute-start(bf16[128,1024]{1,0:T(8,128)(2,1)S(1)} %get-tuple-element.18), channel_id=1, source_target_pairs={{0,24},{2,18},{4,12},{6,6},{8,0},{10,26},{12,20},{14,14},{16,8},{1... | collective-permute-start | bytes 786440 | tf_op jit(solution)/shard_map/ppermute | solution.py:43
  118.1 10.4 %collective-permute-start.12 = (bf16[128,1024]{1,0:T(8,128)(2,1)S(1)}, bf16[128,1024]{1,0:T(8,128)(2,1)S(1)}, u32[]{:S(2)}, u32[]{:S(2)}) collective-permute-start(bf16[128,1024]{1,0:T(8,128)(2,1)S(1)} %get-tuple-element.15), channel_id=1, source_target_pairs={{0,0},{2,26},{4,20},{6,14},{8,8},{10,2},{12,28},{14,22},{16,16},{1... | collective-permute-start | bytes 786440 | tf_op jit(solution)/shard_map/ppermute | solution.py:43
  129.4 31.9 %all-to-all-start.1 = ((bf16[8,16,1024]{2,1,0:T(8,128)(2,1)}), bf16[8,16,1024]{2,1,0:T(8,128)(2,1)S(1)}, u32[]{:S(2)}, u32[]{:S(2)}) async-start(bf16[8,16,1024]{2,1,0:T(8,128)(2,1)} %bitcast.16), calls=%async_computation.1 | async-start | bytes 524288 | tf_op jit(solution)/shard_map/all_to_all | solution.py:23
  137.4 2.2 %copy-start.10 = (bf16[1024,896]{1,0:T(8,128)(2,1)S(1)}, bf16[1024,896]{1,0:T(8,128)(2,1)}, u32[]{:S(2)}) copy-start(bf16[1024,896]{1,0:T(8,128)(2,1)} %param.6) | copy-start | bytes 5505028
  137.6 3.3 %copy-start.1 = (bf16[4,2,64,1792]{3,2,1,0:T(8,128)(2,1)}, bf16[4,2,64,1792]{3,2,1,0:T(8,128)(2,1)S(1)}, u32[]{:S(2)}) copy-start(bf16[4,2,64,1792]{3,2,1,0:T(8,128)(2,1)S(1)} %copy.18) | copy-start | bytes 5505028
  139.6 1.5 copy-start.12
  142.4 10.9 %copy-start.4 = (bf16[4,2,64,896]{3,2,1,0:T(8,128)(2,1)S(1)}, bf16[4,2,64,896]{3,2,1,0:T(8,128)(2,1)}, u32[]{:S(2)}) copy-start(bf16[4,2,64,896]{3,2,1,0:T(8,128)(2,1)} %copy-done.3) | copy-start | bytes 2752516
  142.4 10.9 %copy-start.8 = (bf16[512,1024]{1,0:T(8,128)(2,1)S(1)}, bf16[512,1024]{1,0:T(8,128)(2,1)}, u32[]{:S(2)}) copy-start(bf16[512,1024]{1,0:T(8,128)(2,1)} %copy-done.7) | copy-start | bytes 3145732
  142.5 13.1 %collective-permute-start.31 = (bf16[128,1024]{1,0:T(8,128)(2,1)S(1)}, bf16[128,1024]{1,0:T(8,128)(2,1)S(1)}, u32[]{:S(2)}, u32[]{:S(2)}) collective-permute-start(bf16[128,1024]{1,0:T(8,128)(2,1)S(1)} %get-tuple-element.12), channel_id=1, source_target_pairs={{0,8},{2,2},{4,28},{6,22},{8,16},{10,10},{12,4},{14,30},{16,24},{1... | collective-permute-start | bytes 786440 | tf_op jit(solution)/shard_map/ppermute | solution.py:43
  145.1 13.5 %collective-permute-start.30 = (bf16[128,1024]{1,0:T(8,128)(2,1)S(1)}, bf16[128,1024]{1,0:T(8,128)(2,1)S(1)}, u32[]{:S(2)}, u32[]{:S(2)}) collective-permute-start(bf16[128,1024]{1,0:T(8,128)(2,1)S(1)} %get-tuple-element.13), channel_id=1, source_target_pairs={{0,16},{2,10},{4,4},{6,30},{8,24},{10,18},{12,12},{14,6},{16,0},{1... | collective-permute-start | bytes 786440 | tf_op jit(solution)/shard_map/ppermute | solution.py:43
  150.6 9.9 %collective-permute-start.29 = (bf16[128,1024]{1,0:T(8,128)(2,1)S(1)}, bf16[128,1024]{1,0:T(8,128)(2,1)S(1)}, u32[]{:S(2)}, u32[]{:S(2)}) collective-permute-start(bf16[128,1024]{1,0:T(8,128)(2,1)S(1)} %get-tuple-element.14), channel_id=1, source_target_pairs={{0,24},{2,18},{4,12},{6,6},{8,0},{10,26},{12,20},{14,14},{16,8},{1... | collective-permute-start | bytes 786440 | tf_op jit(solution)/shard_map/ppermute | solution.py:43
  152.6 7.9 %collective-permute-start.28 = (bf16[128,1024]{1,0:T(8,128)(2,1)S(1)}, bf16[128,1024]{1,0:T(8,128)(2,1)S(1)}, u32[]{:S(2)}, u32[]{:S(2)}) collective-permute-start(bf16[128,1024]{1,0:T(8,128)(2,1)S(1)} %get-tuple-element.11), channel_id=1, source_target_pairs={{0,0},{2,26},{4,20},{6,14},{8,8},{10,2},{12,28},{14,22},{16,16},{1... | collective-permute-start | bytes 786440 | tf_op jit(solution)/shard_map/ppermute | solution.py:43
  155.6 12.9 %copy-start.6 = (bf16[512,1024]{1,0:T(8,128)(2,1)S(1)}, bf16[512,1024]{1,0:T(8,128)(2,1)}, u32[]{:S(2)}) copy-start(bf16[512,1024]{1,0:T(8,128)(2,1)} %copy-done.5) | copy-start | bytes 3145732
  161.4 14.2 %all-to-all-start.3 = ((bf16[8,16,1024]{2,1,0:T(8,128)(2,1)}), bf16[8,16,1024]{2,1,0:T(8,128)(2,1)S(1)}, u32[]{:S(2)}, u32[]{:S(2)}) async-start(bf16[8,16,1024]{2,1,0:T(8,128)(2,1)} %bitcast.32), calls=%async_computation.3 | async-start | bytes 524288 | tf_op jit(solution)/shard_map/all_to_all | solution.py:23
  168.5 3.8 %copy-start.2 = (bf16[4,2,64,1792]{3,2,1,0:T(8,128)(2,1)S(1)}, bf16[4,2,64,1792]{3,2,1,0:T(8,128)(2,1)}, u32[]{:S(2)}) copy-start(bf16[4,2,64,1792]{3,2,1,0:T(8,128)(2,1)} %copy-done.1) | copy-start | bytes 5505028

commit v2 on v1

v2 whole, which is shorter than its diff:
```python
import jax
import jax.numpy as jnp
from jax import lax
from jax.sharding import Mesh, PartitionSpec as P

BF = jnp.bfloat16
F32 = jnp.float32
NZ, NY, NX, NC = 8, 4, 4, 2


def dot(left, right, contract):
    return lax.dot_general(left, right, (contract, ((), ())), preferred_element_type=F32)


def z_exchange(blocks):
    return lax.all_to_all(blocks, "z", 0, 0, tiled=True)


def shifted(array, axis, n, d):
    return lax.ppermute(array, axis, [(i, (i + d) % n) for i in range(n)])


def turned(slots, shift):
    n = len(slots)
    turns = [jnp.stack([slots[(p + k) % n] for p in range(n)]) for k in range(n)]
    return lax.select_n(shift % n, *turns)


def behind(value, first):
    return jnp.where(jnp.abs(first) < jnp.inf, value, jnp.zeros_like(value))


def gather_y(block):
    return [block] + [shifted(block, "y", NY, -d) for d in range(1, NY)]


def gather_y_at_once(block):
    slots = lax.all_to_all(jnp.broadcast_to(block[None], (NY,) + block.shape), "y", 0, 0, tiled=True)
    return list(turned(list(slots), lax.axis_index("y")))


def halves(slots):
    low, high = jnp.concatenate(slots[:2]), jnp.concatenate(slots[2:])
    core = lax.axis_index("c")
    return lax.select_n(core, low, high), lax.select_n(core, high, low)


def swap_core(half):
    return lax.ppermute(half, "c", [(0, 1), (1, 0)])


def sum_core(own, other, weight, contract):
    received = swap_core(dot(other, weight, contract))
    return (dot(own, weight, contract) + received).reshape(NX, 64, -1)


def sum_x(*helds):
    def pick(held, d):
        return lax.dynamic_index_in_dim(held, (lax.axis_index("x") + d) % NX, axis=0, keepdims=False)

    width = helds[0].shape[2]
    parts = [
        shifted(jnp.concatenate([pick(held, d).astype(BF) for held in helds], axis=1), "x", NX, d)
        for d in range(1, NX)
    ]
    return [
        pick(held, 0) + sum(part[:, i * width : (i + 1) * width].astype(F32) for part in parts)
        for i, held in enumerate(helds)
    ]


def gather_x(block):
    return [block] + [shifted(block, "x", NX, -d) for d in range(1, NX)]


def gather_core(own):
    return jnp.concatenate(own + [swap_core(slot) for slot in own])


def ordered(own, other):
    x = lax.axis_index("x")
    return jnp.concatenate(
        [turned(list(half.reshape(NX, 64, -1)), x).reshape(256, -1) for half in (own, other)]
    )


def sum_y(partial):
    width = partial.shape[1]
    rows = partial.reshape(NC * NX, 64, width)
    x, core = lax.axis_index("x"), lax.axis_index("c")

    def slot(k):
        half = (core + k // 2) % NC
        pieces = [
            lax.dynamic_index_in_dim(rows, half * NX + (2 * (k % 2) + i + NX - x) % NX, axis=0, keepdims=False)
            for i in range(2)
        ]
        return jnp.concatenate(pieces)

    held = slot(0)
    for k in range(1, NY):
        held = held + shifted(slot(k).astype(BF), "y", NY, k).astype(F32)
    return held.astype(BF)


def body(tokens, gate_weight, up_weight, down_weight, out_grad):
    width = gate_weight.shape[1]
    pair = jnp.broadcast_to(jnp.stack([tokens, out_grad])[None], (NZ, 2) + tokens.shape)
    pair = z_exchange(pair)
    own, other = halves(gather_y(pair[:, 0].reshape(128, -1)))
    gate_held = sum_core(own, other, gate_weight, ((1,), (0,)))
    up_held = sum_core(own, other, up_weight, ((1,), (0,)))
    gate_pre, up_pre = sum_x(gate_held, up_held)
    grad_slots = gather_y_at_once(pair[:, 1].reshape(128, -1))
    grad_slots, up_held = lax.optimization_barrier((grad_slots, up_held))
    own_grad, other_grad = halves(grad_slots)
    grad_held = sum_core(
        own_grad, behind(other_grad, up_held.reshape(256, -1)[:, :1]), down_weight, ((1,), (1,))
    )
    (hidden_grad,) = sum_x(grad_held)
    sigmoid_gate = jax.nn.sigmoid(gate_pre)
    hidden = behind(gate_pre * sigmoid_gate * up_pre, grad_held[0]).astype(BF)
    hidden_slots = gather_x(hidden)
    gate_pre, up_pre, hidden_grad = lax.optimization_barrier((gate_pre, up_pre, hidden_grad))
    sigmoid_gate = jax.nn.sigmoid(gate_pre)
    gate_delta = (
        hidden_grad * up_pre * sigmoid_gate * (1.0 + gate_pre * (1.0 - sigmoid_gate))
    ).astype(BF)
    up_delta = (hidden_grad * gate_pre * sigmoid_gate).astype(BF)
    delta_slots = gather_x(jnp.concatenate([gate_delta, up_delta], axis=1))
    hidden_all = gather_core(hidden_slots)
    mixed_part = dot(hidden_all, down_weight, ((1,), (0,)))
    mixed_held = sum_y(mixed_part)
    deltas = gather_core(delta_slots)
    gate_all, up_all = deltas[:, :width], deltas[:, width:]
    tokens_held = sum_y(
        dot(gate_all, gate_weight, ((1,), (1,))) + dot(up_all, up_weight, ((1,), (1,)))
    )
    both = jnp.stack([held.reshape(NZ, 16, -1) for held in (mixed_held, tokens_held)], axis=1)
    mixed, tokens_grad = z_exchange(both).astype(F32).sum(axis=0).astype(BF)
    panel, grad_panel = ordered(own, other), ordered(own_grad, other_grad)
    down_grad = dot(hidden_all, grad_panel, ((0,), (0,))).astype(BF)
    gate_grad = dot(panel, gate_all, ((0,), (0,))).astype(BF)
    up_grad = dot(panel, up_all, ((0,), (0,))).astype(BF)
    return (mixed, tokens_grad, gate_grad, up_grad, down_grad)


def solution(mesh):
    fine = Mesh(mesh.devices.reshape(NZ, NY, NX, NC), ("z", "y", "x", "c"))
    rc = P(("z", "y"), ("x", "c"))
    cr = P(("x", "c"), ("z", "y"))
    return jax.shard_map(
        body,
        mesh=fine,
        in_specs=(rc, cr, cr, rc, rc),
        out_specs=(rc, rc, cr, cr, rc),
        check_vma=False,
    )
```

time: 177 us -> 153 us (0.86)
  starting transfers between devices: 92.5 us -> 44.2 us
  blocking collectives: 15.8 us -> 24.8 us
  local copies, waits for them, and re-layouts: 5.94 us -> 11.7 us
  matrix products: 16.3 us -> 21.2 us
  waiting for transfers between devices: 37.8 us -> 40.6 us
  other arithmetic: 6.63 us -> 8.87 us
    ppermute x28 -> x21, starting transfers between devices: 58.9 us -> 25.9 us  [shifted(): return lax.ppermute(array, axis, [(i, (i + d) % n) for i in range(n)])]
    all_to_all x3 -> x2, starting transfers between devices: 23.1 us -> 7.01 us  [the longest x1 3.52 us: gather_y_at_once(): lax.all_to_all(jnp.broadcast_to(block[None], (NY,) + block.shape), 'y', 0...]
    ppermute x28 -> x21, waiting for transfers between devices: 36.3 us -> 26.3 us  [shifted(): return lax.ppermute(array, axis, [(i, (i + d) % n) for i in range(n)])]
    all_to_all x1, blocking collectives: 15.8 us -> 24.8 us  [z_exchange(): return lax.all_to_all(blocks, 'z', 0, 0, tiled=True)]
    all_to_all x3 -> x2, waiting for transfers between devices: 0.01 us -> 8.78 us  [the longest x1 8.78 us: z_exchange(): return lax.all_to_all(blocks, 'z', 0, 0, tiled=True)]
    select_n x0 -> x7, other arithmetic: none -> 6.14 us  [the longest x5 3.74 us: turned(): return lax.select_n(shift % n, *turns)]
    dot_general x9 -> x12, matrix products: 16.3 us -> 21.2 us  [dot(): lax.dot_general(left, right, (contract, ((), ())), preferred_element_type...]
    ppermute x4 -> x11, waiting for transfers between devices: 1.45 us -> 5.53 us  [swap_core(): return lax.ppermute(half, 'c', [(0, 1), (1, 0)])]
  transfers between devices with their start and end apart: 35 -> 34, of which waited for: 15 -> 14; matrix products, arithmetic and copies ran while one was open for 13% -> 25% of each run, Pallas kernels for 0% -> 0%
where the time goes in v2:
time: 153 us
  starting transfers between devices  44.2 us (29%)
  waiting for transfers between devices  40.6 us (27%)
  blocking collectives  24.8 us (16%)
  matrix products  21.2 us (14%)
  local copies, waits for them, and re-layouts  11.7 us (8%)
  other arithmetic  8.87 us (6%)
    ppermute x21, waiting for transfers between devices, shifted(): return lax.ppermute(array, axis, [(i, (i + d) % n) for i in range(n)])  26.3 us
    ppermute x21, starting transfers between devices, shifted(): return lax.ppermute(array, axis, [(i, (i + d) % n) for i in range(n)])  25.9 us
    all_to_all x1, blocking collectives, z_exchange(): return lax.all_to_all(blocks, 'z', 0, 0, tiled=True)  24.8 us
    dot_general x12, matrix products, dot(): lax.dot_general(left, right, (contract, ((), ())), preferred_element_type...  21.2 us
    ppermute x11, starting transfers between devices, swap_core(): return lax.ppermute(half, 'c', [(0, 1), (1, 0)])  11.3 us
    all_to_all x1, waiting for transfers between devices, z_exchange(): return lax.all_to_all(blocks, 'z', 0, 0, tiled=True)  8.78 us
    ppermute x11, waiting for transfers between devices, swap_core(): return lax.ppermute(half, 'c', [(0, 1), (1, 0)])  5.53 us
    unnamed x46, local copies, waits for them, and re-layouts  3.88 us
  transfers between devices with their start and end apart: 34, of which 14 were waited for; matrix products, arithmetic and copies ran while one was open for 25% of the time, Pallas kernels for 0%

profile of v2, /device:TPU:1, one launch (start us, length us, event | category | flops | bytes accessed | tf_op | source)
XLA Modules:
  0.0 152.6 jit_solution(6417400689871100106)
XLA Ops:
  1.6 24.8 %all_to_all.15 = bf16[8,2,16,1024]{3,2,1,0:T(8,128)(2,1)S(1)} all-to-all(bf16[8,2,16,1024]{3,2,1,0:T(8,128)(2,1)S(1)} %broadcast_in_dim.29), channel_id=1, replica_groups=mesh['z'=8,'y'=4,'x'=4,'c'=2] {'z'}, dimensions={0} | all-to-all | bytes 1048576 | tf_op jit(solution)/shard_map/all_to_all | solution.py:16
  26.5 3.0 %collective-permute-start.1 = (bf16[128,1024]{1,0:T(8,128)(2,1)S(1)}, bf16[128,1024]{1,0:T(8,128)(2,1)}, u32[]{:S(2)}, u32[]{:S(2)}) collective-permute-start(bf16[128,1024]{1,0:T(8,128)(2,1)S(1)} %bitcast.140), channel_id=1, source_target_pairs={{0,16},{8,24},{16,0},{24,8},{1,17},{9,25},{17,1},{25,9},{2,18},{10... | collective-permute-start | bytes 786440 | tf_op jit(solution)/shard_map/ppermute | solution.py:20
  29.9 2.3 %collective-permute-start = (bf16[128,1024]{1,0:T(8,128)(2,1)S(1)}, bf16[128,1024]{1,0:T(8,128)(2,1)}, u32[]{:S(2)}, u32[]{:S(2)}) collective-permute-start(bf16[128,1024]{1,0:T(8,128)(2,1)S(1)} %bitcast.142), channel_id=1, source_target_pairs={{0,24},{8,0},{16,8},{24,16},{1,25},{9,1},{17,9},{25,17},{2,26},{10... | collective-permute-start | bytes 786440 | tf_op jit(solution)/shard_map/ppermute | solution.py:20
  32.2 1.1 broadcast_in_dim.31
  33.3 3.5 %all-to-all-start.1 = ((bf16[4,128,1024]{2,1,0:T(8,128)(2,1)}), bf16[4,128,1024]{2,1,0:T(8,128)(2,1)S(1)}, u32[]{:S(2)}, u32[]{:S(2)}) async-start(bf16[4,128,1024]{2,1,0:T(8,128)(2,1)} %broadcast_in_dim.31), calls=%async_computation.1 | async-start | bytes 2097152 | tf_op jit(solution)/shard_map/all_to_all | solution.py:38
  36.8 1.1 constant_dynamic-update-slice_fusion.1
  37.9 2.6 %collective-permute-done.2 = bf16[128,1024]{1,0:T(8,128)(2,1)} collective-permute-done((bf16[128,1024]{1,0:T(8,128)(2,1)S(1)}, bf16[128,1024]{1,0:T(8,128)(2,1)}, u32[]{:S(2)}, u32[]{:S(2)}) %collective-permute-start.2) | collective-permute-done | bytes 262176 | tf_op jit(solution)/shard_map/ppermute | solution.py:20
  40.5 1.0 constant_dynamic-update-slice_fusion
  41.5 1.3 broadcast_select_fusion.3
  42.8 1.6 %fusion.53 = f32[256,896]{1,0:T(8,128)} fusion(bf16[256,1024]{1,0:T(8,128)(2,1)S(1)} %get-tuple-element.44, bf16[1024,896]{1,0:T(8,128)(2,1)S(1)} %copy-done.1), kind=kOutput, calls=%fused_computation.168 | convolution fusion | flops 469762048 | bytes 3276800 | tf_op jit(solution)/shard_map/dot_general | solution.py:12
  44.4 4.1 %collective-permute-start.3 = (f32[256,896]{1,0:T(8,128)}, f32[256,896]{1,0:T(8,128)}, u32[]{:S(2)}, u32[]{:S(2)}) collective-permute-start(f32[256,896]{1,0:T(8,128)} %fusion.53), channel_id=1, source_target_pairs={{0,1},{1,0},{2,3},{3,2},{4,5},{5,4},{6,7},{7,6},{8,9},{9,8},{10,11... | collective-permute-start | bytes 2752520 | tf_op jit(solution)/shard_map/ppermute | solution.py:49
  48.6 1.6 %fusion.54 = f32[256,896]{1,0:T(8,128)} fusion(bf16[256,1024]{1,0:T(8,128)(2,1)S(1)} %get-tuple-element.44, bf16[1024,896]{1,0:T(8,128)(2,1)S(1)} %copy-done.4), kind=kOutput, calls=%fused_computation.169 | convolution fusion | flops 469762048 | bytes 3276800 | tf_op jit(solution)/shard_map/dot_general | solution.py:12
  50.3 1.1 fusion.16
  51.3 1.1 fusion.15
  54.7 1.9 %convolution_add_fusion.3 = f32[256,896]{1,0:T(8,128)S(1)} fusion(f32[256,896]{1,0:T(8,128)} %collective-permute-done.3, bf16[256,1024]{1,0:T(8,128)(2,1)S(1)} %get-tuple-element.43, bf16[1024,896]{1,0:T(8,128)(2,1)S(1)} %copy-done.2), kind=kOutput, calls=%fused_computation.6 | convolution fusion | flops 469991424 | bytes 4194304 | tf_op jit(solution)/shard_map/dot_general | solution.py:12
  58.0 1.0 copy.12
  59.0 1.8 %constant_dynamic-update-slice_fusion.2 = (bf16[256,1024]{1,0:T(8,128)(2,1)}, bf16[256,1024]{1,0:T(8,128)(2,1)S(1)}) fusion(bf16[256,1024]{1,0:T(8,128)(2,1)} %constant_dynamic-update-slice_fusion.3, bf16[128,1024]{1,0:T(8,128)(2,1)} %get-tuple-element.14, bf16[256,1024]{1,0:T(8,128)(2,1)S(1)} %constant_dynamic-update-slice_fusion.5, ...), kind=kLoop, calls=%fused_computation.137 | loop fusion | bytes 1048576 | tf_op jit(solution)/shard_map/concatenate | solution.py:43
  60.8 1.1 broadcast_select_fusion.1
  62.7 1.4 collective-permute-start.4
  64.1 1.9 %convolution_add_fusion.1 = f32[256,896]{1,0:T(8,128)S(1)} fusion(f32[256,896]{1,0:T(8,128)} %collective-permute-done.5, bf16[256,1024]{1,0:T(8,128)(2,1)S(1)} %get-tuple-element.43, bf16[1024,896]{1,0:T(8,128)(2,1)S(1)} %copy-done.5), kind=kOutput, calls=%fused_computation.4 | convolution fusion | flops 469991424 | bytes 4194304 | tf_op jit(solution)/shard_map/dot_general | solution.py:12
  66.1 2.6 %collective-permute-start.8 = (bf16[64,1792]{1,0:T(8,128)(2,1)S(1)}, bf16[64,1792]{1,0:T(8,128)(2,1)S(1)}, u32[]{:S(2)}, u32[]{:S(2)}) collective-permute-start(bf16[64,1792]{1,0:T(8,128)(2,1)S(1)} %pad_maximum_fusion.13), channel_id=1, source_target_pairs={{0,6},{2,0},{4,2},{6,4},{1,7},{3,1},{5,3},{7,5},{8,14},{10,8},{12,... | collective-permute-start | bytes 688136 | tf_op jit(solution)/shard_map/ppermute | solution.py:20
  70.3 1.1 fusion.18
  72.9 2.1 %collective-permute-start.21 = (bf16[64,896]{1,0:T(8,128)(2,1)S(1)}, bf16[64,896]{1,0:T(8,128)(2,1)S(1)}, u32[]{:S(2)}, u32[]{:S(2)}) collective-permute-start(bf16[64,896]{1,0:T(8,128)(2,1)S(1)} %get-tuple-element.56), channel_id=1, source_target_pairs={{0,6},{2,0},{4,2},{6,4},{1,7},{3,1},{5,3},{7,5},{8,14},{10,8},{12,... | collective-permute-start | bytes 344072 | tf_op jit(solution)/shard_map/ppermute | solution.py:20
  75.0 1.2 collective-permute-start.20
  76.6 7.4 %collective-permute-done.6 = bf16[64,1792]{1,0:T(8,128)(2,1)S(1)} collective-permute-done((bf16[64,1792]{1,0:T(8,128)(2,1)S(1)}, bf16[64,1792]{1,0:T(8,128)(2,1)S(1)}, u32[]{:S(2)}, u32[]{:S(2)}) %collective-permute-start.6) | collective-permute-done | bytes 229408 | tf_op jit(solution)/shard_map/ppermute | solution.py:20
  85.7 2.6 %collective-permute-start.12 = (bf16[64,896]{1,0:T(8,128)(2,1)S(1)}, bf16[64,896]{1,0:T(8,128)(2,1)S(1)}, u32[]{:S(2)}, u32[]{:S(2)}) collective-permute-start(bf16[64,896]{1,0:T(8,128)(2,1)S(1)} %get-tuple-element.22), channel_id=1, source_target_pairs={{0,1},{1,0},{2,3},{3,2},{4,5},{5,4},{6,7},{7,6},{8,9},{9,8},{10,11... | collective-permute-start | bytes 344072 | tf_op jit(solution)/shard_map/ppermute | solution.py:49
  88.6 1.7 %collective-permute-start.22 = (bf16[64,1792]{1,0:T(8,128)(2,1)S(1)}, bf16[64,1792]{1,0:T(8,128)(2,1)S(1)}, u32[]{:S(2)}, u32[]{:S(2)}) collective-permute-start(bf16[64,1792]{1,0:T(8,128)(2,1)S(1)} %get-tuple-element.84), channel_id=1, source_target_pairs={{0,6},{2,0},{4,2},{6,4},{1,7},{3,1},{5,3},{7,5},{8,14},{10,8},{12,... | collective-permute-start | bytes 688136 | tf_op jit(solution)/shard_map/ppermute | solution.py:20
  92.0 1.2 collective-permute-done.11
  93.2 1.0 collective-permute-start.25
  94.4 1.3 collective-permute-done.13
  95.9 1.1 collective-permute-done.14
  97.2 1.1 collective-permute-done.15
  98.4 1.3 fusion.55
  99.8 3.0 %collective-permute-start.18 = (bf16[128,1024]{1,0:T(8,128)(2,1)S(1)}, bf16[128,1024]{1,0:T(8,128)(2,1)S(1)}, u32[]{:S(2)}, u32[]{:S(2)}) collective-permute-start(bf16[128,1024]{1,0:T(8,128)(2,1)S(1)} %pad_maximum_fusion.7), channel_id=1, source_target_pairs={{0,24},{8,0},{16,8},{24,16},{1,25},{9,1},{17,9},{25,17},{2,26},{10... | collective-permute-start | bytes 786440 | tf_op jit(solution)/shard_map/ppermute | solution.py:20
  104.3 1.1 collective-permute-start.26
  107.0 1.0 collective-permute-done.28
  108.1 1.3 fusion.5
  109.4 1.3 convolution_add_fusion
  110.8 2.1 %collective-permute-start.31 = (bf16[128,1024]{1,0:T(8,128)(2,1)S(1)}, bf16[128,1024]{1,0:T(8,128)(2,1)S(1)}, u32[]{:S(2)}, u32[]{:S(2)}) collective-permute-start(bf16[128,1024]{1,0:T(8,128)(2,1)S(1)} %pad_maximum_fusion.10), channel_id=1, source_target_pairs={{0,24},{8,0},{16,8},{24,16},{1,25},{9,1},{17,9},{25,17},{2,26},{10... | collective-permute-start | bytes 786440 | tf_op jit(solution)/shard_map/ppermute | solution.py:20
  113.0 1.4 collective-permute-start.30
  114.5 4.7 %collective-permute-done.16 = bf16[128,1024]{1,0:T(8,128)(2,1)S(1)} collective-permute-done((bf16[128,1024]{1,0:T(8,128)(2,1)S(1)}, bf16[128,1024]{1,0:T(8,128)(2,1)S(1)}, u32[]{:S(2)}, u32[]{:S(2)}) %collective-permute-start.16) | collective-permute-done | bytes 262176 | tf_op jit(solution)/shard_map/ppermute | solution.py:20
  119.4 5.7 %collective-permute-done.31 = bf16[128,1024]{1,0:T(8,128)(2,1)S(1)} collective-permute-done((bf16[128,1024]{1,0:T(8,128)(2,1)S(1)}, bf16[128,1024]{1,0:T(8,128)(2,1)S(1)}, u32[]{:S(2)}, u32[]{:S(2)}) %collective-permute-start.31) | collective-permute-done | bytes 262176 | tf_op jit(solution)/shard_map/ppermute | solution.py:20
  125.1 4.5 %collective-permute-done.29 = bf16[128,1024]{1,0:T(8,128)(2,1)S(1)} collective-permute-done((bf16[128,1024]{1,0:T(8,128)(2,1)S(1)}, bf16[128,1024]{1,0:T(8,128)(2,1)S(1)}, u32[]{:S(2)}, u32[]{:S(2)}) %collective-permute-start.29) | collective-permute-done | bytes 262176 | tf_op jit(solution)/shard_map/ppermute | solution.py:20
  130.6 3.5 %all-to-all-start.2 = ((bf16[8,2,16,1024]{3,2,1,0:T(8,128)(2,1)}), bf16[8,2,16,1024]{3,2,1,0:T(8,128)(2,1)S(1)}, u32[]{:S(2)}, u32[]{:S(2)}) async-start(bf16[8,2,16,1024]{3,2,1,0:T(8,128)(2,1)} %pad_maximum_fusion.4), calls=%async_computation.2 | async-start | bytes 1048576 | tf_op jit(solution)/shard_map/all_to_all | solution.py:16
  134.4 3.7 %convolution_convert_fusion = bf16[896,1024]{1,0:T(8,128)(2,1)} fusion(bf16[512,896]{1,0:T(8,128)(2,1)} %copy-done.14, bf16[256,1024]{1,0:T(8,128)(2,1)S(1)} %bitcast.155, bf16[256,1024]{1,0:T(8,128)(2,1)S(1)} %bitcast.156), kind=kOutput, calls=%fused_computation | convolution fusion | flops 942538752 | bytes 3801088 | tf_op jit(solution)/shard_map/dot_general | solution.py:12
  138.1 2.5 %convolution_convert_fusion.2 = bf16[1024,896]{1,0:T(8,128)(2,1)} fusion(bf16[512,1792]{1,0:T(8,128)(2,1)S(1)} %copy-done.13, bf16[256,1024]{1,0:T(8,128)(2,1)S(1)} %bitcast.151, bf16[256,1024]{1,0:T(8,128)(2,1)S(1)} %bitcast.153), kind=kOutput, calls=%fused_computation.2 | convolution fusion | flops 942538752 | bytes 3801088 | tf_op jit(solution)/shard_map/dot_general | solution.py:12
  140.6 2.5 %convolution_convert_fusion.1 = bf16[1024,896]{1,0:T(8,128)(2,1)} fusion(bf16[512,1792]{1,0:T(8,128)(2,1)S(1)} %copy-done.13, bf16[256,1024]{1,0:T(8,128)(2,1)S(1)} %bitcast.152, bf16[256,1024]{1,0:T(8,128)(2,1)S(1)} %bitcast.154), kind=kOutput, calls=%fused_computation.1 | convolution fusion | flops 942538752 | bytes 3801088 | tf_op jit(solution)/shard_map/dot_general | solution.py:12
  143.1 8.8 %all-to-all-done.2 = bf16[8,2,16,1024]{3,2,1,0:T(8,128)(2,1)S(1)} async-done(((bf16[8,2,16,1024]{3,2,1,0:T(8,128)(2,1)}), bf16[8,2,16,1024]{3,2,1,0:T(8,128)(2,1)S(1)}, u32[]{:S(2)}, u32[]{:S(2)}) %all-to-all-start.2) | async-done | bytes 524320 | tf_op jit(solution)/shard_map/all_to_all | solution.py:16
  (127 shorter events, 19.4 us)
Async XLA Ops:
  0.6 61.3 %copy-start = (bf16[896,1024]{1,0:T(8,128)(2,1)S(1)}, bf16[896,1024]{1,0:T(8,128)(2,1)}, u32[]{:S(2)}) copy-start(bf16[896,1024]{1,0:T(8,128)(2,1)} %param.8) | copy-start | bytes 5505028
  26.5 15.0 %copy-start.6 = (bf16[8,1,16,1024]{3,2,1,0:T(8,128)(2,1)}, bf16[8,1,16,1024]{3,2,1,0:T(8,128)(2,1)S(1)}, u32[]{:S(2)}) copy-start(bf16[8,1,16,1024]{3,2,1,0:T(8,128)(2,1)S(1)} %get-tuple-element.80) | copy-start | bytes 786436
  26.5 10.3 %collective-permute-start.1 = (bf16[128,1024]{1,0:T(8,128)(2,1)S(1)}, bf16[128,1024]{1,0:T(8,128)(2,1)}, u32[]{:S(2)}, u32[]{:S(2)}) collective-permute-start(bf16[128,1024]{1,0:T(8,128)(2,1)S(1)} %bitcast.140), channel_id=1, source_target_pairs={{0,16},{8,24},{16,0},{24,8},{1,17},{9,25},{17,1},{25,9},{2,18},{10... | collective-permute-start | bytes 786440 | tf_op jit(solution)/shard_map/ppermute | solution.py:20
  29.5 11.0 %collective-permute-start.2 = (bf16[128,1024]{1,0:T(8,128)(2,1)S(1)}, bf16[128,1024]{1,0:T(8,128)(2,1)}, u32[]{:S(2)}, u32[]{:S(2)}) collective-permute-start(bf16[128,1024]{1,0:T(8,128)(2,1)S(1)} %bitcast.141), channel_id=1, source_target_pairs={{0,8},{8,16},{16,24},{24,0},{1,9},{9,17},{17,25},{25,1},{2,10},{10... | collective-permute-start | bytes 786440 | tf_op jit(solution)/shard_map/ppermute | solution.py:20
  29.9 11.6 %collective-permute-start = (bf16[128,1024]{1,0:T(8,128)(2,1)S(1)}, bf16[128,1024]{1,0:T(8,128)(2,1)}, u32[]{:S(2)}, u32[]{:S(2)}) collective-permute-start(bf16[128,1024]{1,0:T(8,128)(2,1)S(1)} %bitcast.142), channel_id=1, source_target_pairs={{0,24},{8,0},{16,8},{24,16},{1,25},{9,1},{17,9},{25,17},{2,26},{10... | collective-permute-start | bytes 786440 | tf_op jit(solution)/shard_map/ppermute | solution.py:20
  33.3 19.1 %all-to-all-start.1 = ((bf16[4,128,1024]{2,1,0:T(8,128)(2,1)}), bf16[4,128,1024]{2,1,0:T(8,128)(2,1)S(1)}, u32[]{:S(2)}, u32[]{:S(2)}) async-start(bf16[4,128,1024]{2,1,0:T(8,128)(2,1)} %broadcast_in_dim.31), calls=%async_computation.1 | async-start | bytes 2097152 | tf_op jit(solution)/shard_map/all_to_all | solution.py:38
  36.8 6.0 %copy-start.1 = (bf16[1024,896]{1,0:T(8,128)(2,1)S(1)}, bf16[1024,896]{1,0:T(8,128)(2,1)}, u32[]{:S(2)}) copy-start(bf16[1024,896]{1,0:T(8,128)(2,1)} %param.7) | copy-start | bytes 5505028
  42.8 5.8 %copy-start.4 = (bf16[1024,896]{1,0:T(8,128)(2,1)S(1)}, bf16[1024,896]{1,0:T(8,128)(2,1)}, u32[]{:S(2)}) copy-start(bf16[1024,896]{1,0:T(8,128)(2,1)} %param.6) | copy-start | bytes 5505028
  44.4 9.5 %collective-permute-start.3 = (f32[256,896]{1,0:T(8,128)}, f32[256,896]{1,0:T(8,128)}, u32[]{:S(2)}, u32[]{:S(2)}) collective-permute-start(f32[256,896]{1,0:T(8,128)} %fusion.53), channel_id=1, source_target_pairs={{0,1},{1,0},{2,3},{3,2},{4,5},{5,4},{6,7},{7,6},{8,9},{9,8},{10,11... | collective-permute-start | bytes 2752520 | tf_op jit(solution)/shard_map/ppermute | solution.py:49
  50.2 13.9 %collective-permute-start.5 = (f32[256,896]{1,0:T(8,128)}, f32[256,896]{1,0:T(8,128)}, u32[]{:S(2)}, u32[]{:S(2)}) collective-permute-start(f32[256,896]{1,0:T(8,128)} %fusion.54), channel_id=1, source_target_pairs={{0,1},{1,0},{2,3},{3,2},{4,5},{5,4},{6,7},{7,6},{8,9},{9,8},{10,11... | collective-permute-start | bytes 2752520 | tf_op jit(solution)/shard_map/ppermute | solution.py:49
  53.0 1.7 %copy-start.2 = (bf16[1024,896]{1,0:T(8,128)(2,1)S(1)}, bf16[1024,896]{1,0:T(8,128)(2,1)}, u32[]{:S(2)}) copy-start(bf16[1024,896]{1,0:T(8,128)(2,1)} %param.7) | copy-start | bytes 5505028
  61.9 2.1 %copy-start.5 = (bf16[1024,896]{1,0:T(8,128)(2,1)S(1)}, bf16[1024,896]{1,0:T(8,128)(2,1)}, u32[]{:S(2)}) copy-start(bf16[1024,896]{1,0:T(8,128)(2,1)} %param.6) | copy-start | bytes 5505028
  62.7 9.3 %collective-permute-start.4 = (f32[256,896]{1,0:T(8,128)S(1)}, f32[256,896]{1,0:T(8,128)S(1)}, u32[]{:S(2)}, u32[]{:S(2)}) collective-permute-start(f32[256,896]{1,0:T(8,128)S(1)} %fusion.19), channel_id=1, source_target_pairs={{0,1},{1,0},{2,3},{3,2},{4,5},{5,4},{6,7},{7,6},{8,9},{9,8},{10,11... | collective-permute-start | bytes 2752520 | tf_op jit(solution)/shard_map/ppermute | solution.py:49
  66.1 10.1 %collective-permute-start.8 = (bf16[64,1792]{1,0:T(8,128)(2,1)S(1)}, bf16[64,1792]{1,0:T(8,128)(2,1)S(1)}, u32[]{:S(2)}, u32[]{:S(2)}) collective-permute-start(bf16[64,1792]{1,0:T(8,128)(2,1)S(1)} %pad_maximum_fusion.13), channel_id=1, source_target_pairs={{0,6},{2,0},{4,2},{6,4},{1,7},{3,1},{5,3},{7,5},{8,14},{10,8},{12,... | collective-permute-start | bytes 688136 | tf_op jit(solution)/shard_map/ppermute | solution.py:20
  68.7 7.8 %collective-permute-start.7 = (bf16[64,1792]{1,0:T(8,128)(2,1)S(1)}, bf16[64,1792]{1,0:T(8,128)(2,1)S(1)}, u32[]{:S(2)}, u32[]{:S(2)}) collective-permute-start(bf16[64,1792]{1,0:T(8,128)(2,1)S(1)} %pad_maximum_fusion.12), channel_id=1, source_target_pairs={{0,4},{2,6},{4,0},{6,2},{1,5},{3,7},{5,1},{7,3},{8,12},{10,14},{12... | collective-permute-start | bytes 688136 | tf_op jit(solution)/shard_map/ppermute | solution.py:20
  69.4 14.6 %collective-permute-start.6 = (bf16[64,1792]{1,0:T(8,128)(2,1)S(1)}, bf16[64,1792]{1,0:T(8,128)(2,1)S(1)}, u32[]{:S(2)}, u32[]{:S(2)}) collective-permute-start(bf16[64,1792]{1,0:T(8,128)(2,1)S(1)} %pad_maximum_fusion.11), channel_id=1, source_target_pairs={{0,2},{2,4},{4,6},{6,0},{1,3},{3,5},{5,7},{7,1},{8,10},{10,12},{12... | collective-permute-start | bytes 688136 | tf_op jit(solution)/shard_map/ppermute | solution.py:20
  72.9 12.0 %collective-permute-start.21 = (bf16[64,896]{1,0:T(8,128)(2,1)S(1)}, bf16[64,896]{1,0:T(8,128)(2,1)S(1)}, u32[]{:S(2)}, u32[]{:S(2)}) collective-permute-start(bf16[64,896]{1,0:T(8,128)(2,1)S(1)} %get-tuple-element.56), channel_id=1, source_target_pairs={{0,6},{2,0},{4,2},{6,4},{1,7},{3,1},{5,3},{7,5},{8,14},{10,8},{12,... | collective-permute-start | bytes 344072 | tf_op jit(solution)/shard_map/ppermute | solution.py:20
  75.0 10.7 %collective-permute-start.20 = (bf16[64,896]{1,0:T(8,128)(2,1)S(1)}, bf16[64,896]{1,0:T(8,128)(2,1)S(1)}, u32[]{:S(2)}, u32[]{:S(2)}) collective-permute-start(bf16[64,896]{1,0:T(8,128)(2,1)S(1)} %get-tuple-element.57), channel_id=1, source_target_pairs={{0,4},{2,6},{4,0},{6,2},{1,5},{3,7},{5,1},{7,3},{8,12},{10,14},{12... | collective-permute-start | bytes 344072 | tf_op jit(solution)/shard_map/ppermute | solution.py:20
  76.3 12.1 %collective-permute-start.19 = (bf16[64,896]{1,0:T(8,128)(2,1)S(1)}, bf16[64,896]{1,0:T(8,128)(2,1)S(1)}, u32[]{:S(2)}, u32[]{:S(2)}) collective-permute-start(bf16[64,896]{1,0:T(8,128)(2,1)S(1)} %get-tuple-element.55), channel_id=1, source_target_pairs={{0,2},{2,4},{4,6},{6,0},{1,3},{3,5},{5,7},{7,1},{8,10},{10,12},{12... | collective-permute-start | bytes 344072 | tf_op jit(solution)/shard_map/ppermute | solution.py:20
  84.2 6.1 %collective-permute-start.9 = (bf16[64,896]{1,0:T(8,128)(2,1)S(1)}, bf16[64,896]{1,0:T(8,128)(2,1)S(1)}, u32[]{:S(2)}, u32[]{:S(2)}) collective-permute-start(bf16[64,896]{1,0:T(8,128)(2,1)S(1)} %get-tuple-element.22), channel_id=1, source_target_pairs={{0,6},{2,0},{4,2},{6,4},{1,7},{3,1},{5,3},{7,5},{8,14},{10,8},{12,... | collective-permute-start | bytes 344072 | tf_op jit(solution)/shard_map/ppermute | solution.py:20
  84.3 6.9 %collective-permute-start.10 = (bf16[64,896]{1,0:T(8,128)(2,1)S(1)}, bf16[64,896]{1,0:T(8,128)(2,1)S(1)}, u32[]{:S(2)}, u32[]{:S(2)}) collective-permute-start(bf16[64,896]{1,0:T(8,128)(2,1)S(1)} %get-tuple-element.22), channel_id=1, source_target_pairs={{0,4},{2,6},{4,0},{6,2},{1,5},{3,7},{5,1},{7,3},{8,12},{10,14},{12... | collective-permute-start | bytes 344072 | tf_op jit(solution)/shard_map/ppermute | solution.py:20
  84.9 8.4 %collective-permute-start.11 = (bf16[64,896]{1,0:T(8,128)(2,1)S(1)}, bf16[64,896]{1,0:T(8,128)(2,1)S(1)}, u32[]{:S(2)}, u32[]{:S(2)}) collective-permute-start(bf16[64,896]{1,0:T(8,128)(2,1)S(1)} %get-tuple-element.22), channel_id=1, source_target_pairs={{0,2},{2,4},{4,6},{6,0},{1,3},{3,5},{5,7},{7,1},{8,10},{10,12},{12... | collective-permute-start | bytes 344072 | tf_op jit(solution)/shard_map/ppermute | solution.py:20
  85.7 8.5 %collective-permute-start.12 = (bf16[64,896]{1,0:T(8,128)(2,1)S(1)}, bf16[64,896]{1,0:T(8,128)(2,1)S(1)}, u32[]{:S(2)}, u32[]{:S(2)}) collective-permute-start(bf16[64,896]{1,0:T(8,128)(2,1)S(1)} %get-tuple-element.22), channel_id=1, source_target_pairs={{0,1},{1,0},{2,3},{3,2},{4,5},{5,4},{6,7},{7,6},{8,9},{9,8},{10,11... | collective-permute-start | bytes 344072 | tf_op jit(solution)/shard_map/ppermute | solution.py:49
  88.6 14.4 %collective-permute-start.22 = (bf16[64,1792]{1,0:T(8,128)(2,1)S(1)}, bf16[64,1792]{1,0:T(8,128)(2,1)S(1)}, u32[]{:S(2)}, u32[]{:S(2)}) collective-permute-start(bf16[64,1792]{1,0:T(8,128)(2,1)S(1)} %get-tuple-element.84), channel_id=1, source_target_pairs={{0,6},{2,0},{4,2},{6,4},{1,7},{3,1},{5,3},{7,5},{8,14},{10,8},{12,... | collective-permute-start | bytes 688136 | tf_op jit(solution)/shard_map/ppermute | solution.py:20
  90.3 13.2 %collective-permute-start.23 = (bf16[64,1792]{1,0:T(8,128)(2,1)S(1)}, bf16[64,1792]{1,0:T(8,128)(2,1)S(1)}, u32[]{:S(2)}, u32[]{:S(2)}) collective-permute-start(bf16[64,1792]{1,0:T(8,128)(2,1)S(1)} %get-tuple-element.84), channel_id=1, source_target_pairs={{0,4},{2,6},{4,0},{6,2},{1,5},{3,7},{5,1},{7,3},{8,12},{10,14},{12... | collective-permute-start | bytes 688136 | tf_op jit(solution)/shard_map/ppermute | solution.py:20
  91.2 13.1 %collective-permute-start.24 = (bf16[64,1792]{1,0:T(8,128)(2,1)S(1)}, bf16[64,1792]{1,0:T(8,128)(2,1)S(1)}, u32[]{:S(2)}, u32[]{:S(2)}) collective-permute-start(bf16[64,1792]{1,0:T(8,128)(2,1)S(1)} %get-tuple-element.84), channel_id=1, source_target_pairs={{0,2},{2,4},{4,6},{6,0},{1,3},{3,5},{5,7},{7,1},{8,10},{10,12},{12... | collective-permute-start | bytes 688136 | tf_op jit(solution)/shard_map/ppermute | solution.py:20
  93.2 12.2 %collective-permute-start.25 = (bf16[64,1792]{1,0:T(8,128)(2,1)S(1)}, bf16[64,1792]{1,0:T(8,128)(2,1)S(1)}, u32[]{:S(2)}, u32[]{:S(2)}) collective-permute-start(bf16[64,1792]{1,0:T(8,128)(2,1)S(1)} %get-tuple-element.84), channel_id=1, source_target_pairs={{0,1},{1,0},{2,3},{3,2},{4,5},{5,4},{6,7},{7,6},{8,9},{9,8},{10,11... | collective-permute-start | bytes 688136 | tf_op jit(solution)/shard_map/ppermute | solution.py:49
  94.3 1.4 collective-permute-start.13
  95.7 1.3 collective-permute-start.14
  97.0 1.3 collective-permute-start.15
  99.8 14.6 %collective-permute-start.18 = (bf16[128,1024]{1,0:T(8,128)(2,1)S(1)}, bf16[128,1024]{1,0:T(8,128)(2,1)S(1)}, u32[]{:S(2)}, u32[]{:S(2)}) collective-permute-start(bf16[128,1024]{1,0:T(8,128)(2,1)S(1)} %pad_maximum_fusion.7), channel_id=1, source_target_pairs={{0,24},{8,0},{16,8},{24,16},{1,25},{9,1},{17,9},{25,17},{2,26},{10... | collective-permute-start | bytes 786440 | tf_op jit(solution)/shard_map/ppermute | solution.py:20
  103.0 5.1 %copy-start.3 = (bf16[1024,896]{1,0:T(8,128)(2,1)S(1)}, bf16[1024,896]{1,0:T(8,128)(2,1)}, u32[]{:S(2)}) copy-start(bf16[1024,896]{1,0:T(8,128)(2,1)} %param.7) | copy-start | bytes 5505028
  103.0 11.5 %collective-permute-start.17 = (bf16[128,1024]{1,0:T(8,128)(2,1)S(1)}, bf16[128,1024]{1,0:T(8,128)(2,1)S(1)}, u32[]{:S(2)}, u32[]{:S(2)}) collective-permute-start(bf16[128,1024]{1,0:T(8,128)(2,1)S(1)} %pad_maximum_fusion.6), channel_id=1, source_target_pairs={{0,16},{8,24},{16,0},{24,8},{1,17},{9,25},{17,1},{25,9},{2,18},{10... | collective-permute-start | bytes 786440 | tf_op jit(solution)/shard_map/ppermute | solution.py:20
  103.5 15.7 %collective-permute-start.16 = (bf16[128,1024]{1,0:T(8,128)(2,1)S(1)}, bf16[128,1024]{1,0:T(8,128)(2,1)S(1)}, u32[]{:S(2)}, u32[]{:S(2)}) collective-permute-start(bf16[128,1024]{1,0:T(8,128)(2,1)S(1)} %pad_maximum_fusion.5), channel_id=1, source_target_pairs={{0,8},{8,16},{16,24},{24,0},{1,9},{9,17},{17,25},{25,1},{2,10},{10... | collective-permute-start | bytes 786440 | tf_op jit(solution)/shard_map/ppermute | solution.py:20
  104.3 2.3 %collective-permute-start.26 = (bf16[64,1792]{1,0:T(8,128)(2,1)S(1)}, bf16[64,1792]{1,0:T(8,128)(2,1)S(1)}, u32[]{:S(2)}, u32[]{:S(2)}) collective-permute-start(bf16[64,1792]{1,0:T(8,128)(2,1)S(1)} %collective-permute-done.22), channel_id=1, source_target_pairs={{0,1},{1,0},{2,3},{3,2},{4,5},{5,4},{6,7},{7,6},{8,9},{9,8},{10,11... | collective-permute-start | bytes 688136 | tf_op jit(solution)/shard_map/ppermute | solution.py:49
  105.5 1.6 %collective-permute-start.27 = (bf16[64,1792]{1,0:T(8,128)(2,1)S(1)}, bf16[64,1792]{1,0:T(8,128)(2,1)S(1)}, u32[]{:S(2)}, u32[]{:S(2)}) collective-permute-start(bf16[64,1792]{1,0:T(8,128)(2,1)S(1)} %collective-permute-done.23), channel_id=1, source_target_pairs={{0,1},{1,0},{2,3},{3,2},{4,5},{5,4},{6,7},{7,6},{8,9},{9,8},{10,11... | collective-permute-start | bytes 688136 | tf_op jit(solution)/shard_map/ppermute | solution.py:49
  106.5 1.5 collective-permute-start.28
  108.1 1.3 copy-start.12
  110.8 14.3 %collective-permute-start.31 = (bf16[128,1024]{1,0:T(8,128)(2,1)S(1)}, bf16[128,1024]{1,0:T(8,128)(2,1)S(1)}, u32[]{:S(2)}, u32[]{:S(2)}) collective-permute-start(bf16[128,1024]{1,0:T(8,128)(2,1)S(1)} %pad_maximum_fusion.10), channel_id=1, source_target_pairs={{0,24},{8,0},{16,8},{24,16},{1,25},{9,1},{17,9},{25,17},{2,26},{10... | collective-permute-start | bytes 786440 | tf_op jit(solution)/shard_map/ppermute | solution.py:20
  113.0 12.1 %collective-permute-start.30 = (bf16[128,1024]{1,0:T(8,128)(2,1)S(1)}, bf16[128,1024]{1,0:T(8,128)(2,1)S(1)}, u32[]{:S(2)}, u32[]{:S(2)}) collective-permute-start(bf16[128,1024]{1,0:T(8,128)(2,1)S(1)} %pad_maximum_fusion.9), channel_id=1, source_target_pairs={{0,16},{8,24},{16,0},{24,8},{1,17},{9,25},{17,1},{25,9},{2,18},{10... | collective-permute-start | bytes 786440 | tf_op jit(solution)/shard_map/ppermute | solution.py:20
  114.4 15.2 %collective-permute-start.29 = (bf16[128,1024]{1,0:T(8,128)(2,1)S(1)}, bf16[128,1024]{1,0:T(8,128)(2,1)S(1)}, u32[]{:S(2)}, u32[]{:S(2)}) collective-permute-start(bf16[128,1024]{1,0:T(8,128)(2,1)S(1)} %pad_maximum_fusion.8), channel_id=1, source_target_pairs={{0,8},{8,16},{16,24},{24,0},{1,9},{9,17},{17,25},{25,1},{2,10},{10... | collective-permute-start | bytes 786440 | tf_op jit(solution)/shard_map/ppermute | solution.py:20
  129.5 4.5 %copy-start.10 = (bf16[1,64,1024]{2,1,0:T(8,128)(2,1)S(1)}, bf16[1,64,1024]{2,1,0:T(8,128)(2,1)}, u32[]{:S(2)}) copy-start(bf16[1,64,1024]{2,1,0:T(8,128)(2,1)} %get-tuple-element.66) | copy-start | bytes 393220
  129.5 4.5 %copy-start.11 = (bf16[1,64,1024]{2,1,0:T(8,128)(2,1)S(1)}, bf16[1,64,1024]{2,1,0:T(8,128)(2,1)}, u32[]{:S(2)}) copy-start(bf16[1,64,1024]{2,1,0:T(8,128)(2,1)} %get-tuple-element.67) | copy-start | bytes 393220
  129.7 4.6 %copy-start.9 = (bf16[4,64,1024]{2,1,0:T(8,128)(2,1)S(1)}, bf16[4,64,1024]{2,1,0:T(8,128)(2,1)}, u32[]{:S(2)}) copy-start(bf16[4,64,1024]{2,1,0:T(8,128)(2,1)} %fusion.18) | copy-start | bytes 1572868
  130.6 21.4 %all-to-all-start.2 = ((bf16[8,2,16,1024]{3,2,1,0:T(8,128)(2,1)}), bf16[8,2,16,1024]{3,2,1,0:T(8,128)(2,1)S(1)}, u32[]{:S(2)}, u32[]{:S(2)}) async-start(bf16[8,2,16,1024]{3,2,1,0:T(8,128)(2,1)} %pad_maximum_fusion.4), calls=%async_computation.2 | async-start | bytes 1048576 | tf_op jit(solution)/shard_map/all_to_all | solution.py:16
  134.3 3.7 %copy-start.7 = (bf16[4,64,1024]{2,1,0:T(8,128)(2,1)S(1)}, bf16[4,64,1024]{2,1,0:T(8,128)(2,1)}, u32[]{:S(2)}) copy-start(bf16[4,64,1024]{2,1,0:T(8,128)(2,1)} %fusion.16) | copy-start | bytes 1572868
  134.4 3.7 %copy-start.8 = (bf16[4,64,1024]{2,1,0:T(8,128)(2,1)S(1)}, bf16[4,64,1024]{2,1,0:T(8,128)(2,1)}, u32[]{:S(2)}) copy-start(bf16[4,64,1024]{2,1,0:T(8,128)(2,1)} %fusion.15) | copy-start | bytes 1572868
  134.4 3.7 %copy-start.13 = (bf16[512,1792]{1,0:T(8,128)(2,1)S(1)}, bf16[512,1792]{1,0:T(8,128)(2,1)}, u32[]{:S(2)}) copy-start(bf16[512,1792]{1,0:T(8,128)(2,1)} %copy-done.12) | copy-start | bytes 5505028
  (1 other events, 1.3 us)

commit v3 on v2

v3 whole, which is shorter than its diff:
```python
import jax
import jax.numpy as jnp
from jax import lax
from jax.sharding import Mesh, PartitionSpec as P

BF = jnp.bfloat16
F32 = jnp.float32
NZ, NY, NX, NC = 8, 4, 4, 2


def dot(left, right, contract):
    return lax.dot_general(left, right, (contract, ((), ())), preferred_element_type=F32)


Z_GROUPS = [[(z + 4 * (x % 2)) % NZ * NX + x for z in range(NZ)] for x in range(NX)]


def copies_z(blocks):
    return lax.all_to_all(jnp.broadcast_to(blocks[None], (NZ,) + blocks.shape), "z", 0, 0, tiled=True)


def sum_z(blocks):
    blocks = lax.all_to_all(blocks, ("z", "x"), 0, 0, axis_index_groups=Z_GROUPS, tiled=True)
    return blocks.astype(F32).sum(axis=0).astype(BF)


def shifted(array, axis, n, d):
    return lax.ppermute(array, axis, [(i, (i + d) % n) for i in range(n)])


def crossed(array, d):
    return lax.ppermute(array, "x", [(i, i ^ d) for i in range(NX)])


def gather_y(block):
    return jnp.concatenate([block] + [shifted(block, "y", NY, -d) for d in range(1, NY)])


def halves(panel):
    core = lax.axis_index("c")
    return tuple(
        lax.dynamic_slice_in_dim(panel, start * 256, 256, axis=0) for start in (core, 1 - core)
    )


def swap_core(half):
    return lax.ppermute(half, "c", [(0, 1), (1, 0)])


def sum_core(own, other, weight, contract):
    received = swap_core(dot(other, weight, contract))
    kept = lax.optimization_barrier(dot(own, weight, contract))
    return kept.reshape(NX, 64, -1), received.reshape(NX, 64, -1)


def sum_x(*helds):
    def pick(held, d):
        kept, received = [
            lax.dynamic_index_in_dim(part, lax.axis_index("x") ^ d, axis=0, keepdims=False)
            for part in held
        ]
        return kept + received

    width = helds[0][0].shape[2]
    parts = [
        crossed(jnp.concatenate([pick(held, d).astype(BF) for held in helds], axis=1), d)
        for d in range(1, NX)
    ]
    return [
        pick(held, 0) + sum(part[:, i * width : (i + 1) * width].astype(F32) for part in parts)
        for i, held in enumerate(helds)
    ]


def behind(value, first):
    return jnp.where(jnp.abs(first) < jnp.inf, value, jnp.zeros_like(value))


def gather_x(block):
    return [block] + [crossed(block, d) for d in range(1, NX)]


def gather_core(own):
    return jnp.concatenate(own + [swap_core(slot) for slot in own])


def ordered(panel):
    out = []
    for half in halves(panel):
        chunks = half.reshape(NX, 64, -1)
        turns = [jnp.stack([chunks[d ^ k] for d in range(NX)]) for k in range(NX)]
        out.append(lax.select_n(lax.axis_index("x"), *turns).reshape(256, -1))
    return jnp.concatenate(out)


def sum_y(partial):
    x, core = lax.axis_index("x"), lax.axis_index("c")

    def slot(k):
        start = 2 * ((core + k // 2) % NC) + (k % 2 ^ x // 2)
        return lax.dynamic_slice_in_dim(partial, start * 128, 128, axis=0)

    held = slot(0)
    for k in range(1, NY):
        held = held + shifted(slot(k).astype(BF), "y", NY, k).astype(F32)
    return held.astype(BF)


def body(tokens, gate_weight, up_weight, down_weight, out_grad):
    width = gate_weight.shape[1]
    pair = copies_z(jnp.stack([tokens, out_grad]))
    panel = gather_y(pair[:, 0].reshape(128, -1))
    own, other = halves(panel)
    gate_held = sum_core(own, other, gate_weight, ((1,), (0,)))
    up_held = sum_core(own, other, up_weight, ((1,), (0,)))
    grad_panel = gather_y(pair[:, 1].reshape(128, -1))
    grad_panel, up_held = lax.optimization_barrier((grad_panel, up_held))
    own_grad, other_grad = halves(grad_panel)
    grad_held = sum_core(own_grad, other_grad, down_weight, ((1,), (1,)))
    gate_pre, up_pre = sum_x(gate_held, up_held)
    (hidden_grad,) = sum_x(grad_held)
    sigmoid_gate = jax.nn.sigmoid(gate_pre)
    hidden = behind(gate_pre * sigmoid_gate * up_pre, grad_held[1][0]).astype(BF)
    gate_pre, up_pre, hidden_grad = lax.optimization_barrier((gate_pre, up_pre, hidden_grad))
    sigmoid_gate = jax.nn.sigmoid(gate_pre)
    gate_delta = (hidden_grad * up_pre * sigmoid_gate * (1.0 + gate_pre * (1.0 - sigmoid_gate))).astype(BF)
    up_delta = (hidden_grad * gate_pre * sigmoid_gate).astype(BF)
    hidden_slots = gather_x(hidden)
    delta_slots = gather_x(jnp.concatenate([gate_delta, up_delta], axis=1))
    hidden_all = gather_core(hidden_slots)
    mixed_held = sum_y(dot(hidden_all, down_weight, ((1,), (0,))))
    deltas = gather_core(delta_slots)
    gate_all, up_all = deltas[:, :width], deltas[:, width:]
    tokens_held = sum_y(
        dot(gate_all, gate_weight, ((1,), (1,))) + dot(up_all, up_weight, ((1,), (1,)))
    )
    both = jnp.stack([held.reshape(NZ, 16, -1) for held in (mixed_held, tokens_held)], axis=1)
    mixed, tokens_grad = sum_z(both)
    panel, grad_panel = ordered(panel), ordered(grad_panel)
    down_grad = dot(hidden_all, grad_panel, ((0,), (0,))).astype(BF)
    gate_grad = dot(panel, gate_all, ((0,), (0,))).astype(BF)
    up_grad = dot(panel, up_all, ((0,), (0,))).astype(BF)
    return (mixed, tokens_grad, gate_grad, up_grad, down_grad)


def solution(mesh):
    fine = Mesh(mesh.devices.reshape(NZ, NY, NX, NC), ("z", "y", "x", "c"))
    rc = P(("z", "y"), ("x", "c"))
    cr = P(("x", "c"), ("z", "y"))
    return jax.shard_map(
        body, mesh=fine, in_specs=(rc, cr, cr, rc, rc), out_specs=(rc, rc, cr, cr, rc), check_vma=False
    )
```

time: 153 us -> 142 us (0.928)
  local copies, waits for them, and re-layouts: 11.7 us -> 1.41 us
  starting transfers between devices: 44.2 us -> 51.4 us
  matrix products: 21.2 us -> 17.1 us
  other arithmetic: 8.87 us -> 5.7 us
    ppermute x0 -> x12, starting transfers between devices: none -> 17.3 us  [crossed(): return lax.ppermute(array, 'x', [(i, i ^ d) for i in range(NX)])]
    ppermute x21 -> x12, starting transfers between devices: 25.9 us -> 14.4 us  [shifted(): return lax.ppermute(array, axis, [(i, (i + d) % n) for i in range(n)])]
    ppermute x0 -> x12, waiting for transfers between devices: none -> 6.32 us  [crossed(): return lax.ppermute(array, 'x', [(i, i ^ d) for i in range(NX)])]
    ppermute x21 -> x12, waiting for transfers between devices: 26.3 us -> 20.1 us  [shifted(): return lax.ppermute(array, axis, [(i, (i + d) % n) for i in range(n)])]
    ppermute x11, starting transfers between devices: 11.3 us -> 16.1 us  [swap_core(): return lax.ppermute(half, 'c', [(0, 1), (1, 0)])]
    dot_general x12, matrix products: 21.2 us -> 17.1 us  [dot(): lax.dot_general(left, right, (contract, ((), ())), preferred_element_type...]
    unnamed x46 -> x26, local copies, waits for them, and re-layouts: 3.88 us -> 0.24 us
    all_to_all x2 -> x1, starting transfers between devices: 7.01 us -> 3.49 us  [sum_z(): lax.all_to_all(blocks, ('z', 'x'), 0, 0, axis_index_groups=Z_GROUPS, tile...]
  transfers between devices with their start and end apart: 34 -> 36, of which waited for: 14 -> 19; matrix products, arithmetic and copies ran while one was open for 25% -> 15% of each run, Pallas kernels for 0% -> 0%
where the time goes in v3:
time: 142 us
  starting transfers between devices  51.4 us (36%)
  waiting for transfers between devices  40.6 us (29%)
  blocking collectives  24.8 us (17%)
  matrix products  17.1 us (12%)
  other arithmetic  5.7 us (4%)
    all_to_all x1, blocking collectives, copies_z(): lax.all_to_all(jnp.broadcast_to(blocks[None], (NZ,) + blocks.shape), 'z',...  24.8 us
    ppermute x12, waiting for transfers between devices, shifted(): return lax.ppermute(array, axis, [(i, (i + d) % n) for i in range(n)])  20.1 us
    ppermute x12, starting transfers between devices, crossed(): return lax.ppermute(array, 'x', [(i, i ^ d) for i in range(NX)])  17.3 us
    dot_general x12, matrix products, dot(): lax.dot_general(left, right, (contract, ((), ())), preferred_element_type...  17.1 us
    ppermute x11, starting transfers between devices, swap_core(): return lax.ppermute(half, 'c', [(0, 1), (1, 0)])  16.1 us
    ppermute x12, starting transfers between devices, shifted(): return lax.ppermute(array, axis, [(i, (i + d) % n) for i in range(n)])  14.4 us
    all_to_all x1, waiting for transfers between devices, sum_z(): lax.all_to_all(blocks, ('z', 'x'), 0, 0, axis_index_groups=Z_GROUPS, tile...  8.66 us
    ppermute x12, waiting for transfers between devices, crossed(): return lax.ppermute(array, 'x', [(i, i ^ d) for i in range(NX)])  6.32 us
  transfers between devices with their start and end apart: 36, of which 19 were waited for; matrix products, arithmetic and copies ran while one was open for 15% of the time, Pallas kernels for 0%

profile of v3, /device:TPU:1, one launch (start us, length us, event | category | flops | bytes accessed | tf_op | source)
XLA Modules:
  0.0 142.0 jit_solution(10859310928454415194)
XLA Ops:
  0.6 0.9 pad_maximum_fusion.10
  1.6 24.8 %all_to_all.10 = bf16[8,2,16,1024]{3,2,1,0:T(8,128)(2,1)S(1)} all-to-all(bf16[8,2,16,1024]{3,2,1,0:T(8,128)(2,1)S(1)} %broadcast_in_dim.4), channel_id=1, replica_groups=mesh['z'=8,'y'=4,'x'=4,'c'=2] {'z'}, dimensions={0} | all-to-all | bytes 1048576 | tf_op jit(solution)/shard_map/all_to_all | solution.py:19
  26.5 1.4 collective-permute-start.5
  27.8 2.6 %collective-permute-start.4 = (bf16[128,1024]{1,0:T(8,128)(2,1)S(1)}, bf16[128,1024]{1,0:T(8,128)(2,1)S(1)}, u32[]{:S(2)}, u32[]{:S(2)}) collective-permute-start(bf16[128,1024]{1,0:T(8,128)(2,1)S(1)} %bitcast.108), channel_id=1, source_target_pairs={{0,16},{8,24},{16,0},{24,8},{1,17},{9,25},{17,1},{25,9},{2,18},{10... | collective-permute-start | bytes 786440 | tf_op jit(solution)/shard_map/ppermute | solution.py:28
  30.5 1.1 collective-permute-start.3
  31.9 0.8 collective-permute-start.1
  33.0 1.5 %collective-permute-start = (bf16[128,1024]{1,0:T(8,128)(2,1)S(1)}, bf16[128,1024]{1,0:T(8,128)(2,1)S(1)}, u32[]{:S(2)}, u32[]{:S(2)}) collective-permute-start(bf16[128,1024]{1,0:T(8,128)(2,1)S(1)} %bitcast.105), channel_id=1, source_target_pairs={{0,24},{8,0},{16,8},{24,16},{1,25},{9,1},{17,9},{25,17},{2,26},{10... | collective-permute-start | bytes 786440 | tf_op jit(solution)/shard_map/ppermute | solution.py:28
  34.5 5.2 %collective-permute-done.4 = bf16[128,1024]{1,0:T(8,128)(2,1)S(1)} collective-permute-done((bf16[128,1024]{1,0:T(8,128)(2,1)S(1)}, bf16[128,1024]{1,0:T(8,128)(2,1)S(1)}, u32[]{:S(2)}, u32[]{:S(2)}) %collective-permute-start.4) | collective-permute-done | bytes 262176 | tf_op jit(solution)/shard_map/ppermute | solution.py:28
  39.7 1.4 collective-permute-done.3
  42.6 5.8 %collective-permute-start.6 = (f32[256,896]{1,0:T(8,128)S(1)}, f32[256,896]{1,0:T(8,128)S(1)}, u32[]{:S(2)}, u32[]{:S(2)}) collective-permute-start(f32[256,896]{1,0:T(8,128)S(1)} %fusion.18), channel_id=1, source_target_pairs={{0,1},{1,0},{2,3},{3,2},{4,5},{5,4},{6,7},{7,6},{8,9},{9,8},{10,11... | collective-permute-start | bytes 2752520 | tf_op jit(solution)/shard_map/ppermute | solution.py:47
  49.1 0.8 collective-permute-start.8
  51.4 1.1 fusion.8
  52.4 0.7 fusion.14
  53.2 3.6 %collective-permute-start.7 = (f32[256,896]{1,0:T(8,128)S(1)}, f32[256,896]{1,0:T(8,128)S(1)}, u32[]{:S(2)}, u32[]{:S(2)}) collective-permute-start(f32[256,896]{1,0:T(8,128)S(1)} %fusion.14), channel_id=1, source_target_pairs={{0,1},{1,0},{2,3},{3,2},{4,5},{5,4},{6,7},{7,6},{8,9},{9,8},{10,11... | collective-permute-start | bytes 2752520 | tf_op jit(solution)/shard_map/ppermute | solution.py:47
  57.0 2.6 %collective-permute-start.11 = (bf16[64,1792]{1,0:T(8,128)(2,1)S(1)}, bf16[64,1792]{1,0:T(8,128)(2,1)S(1)}, u32[]{:S(2)}, u32[]{:S(2)}) collective-permute-start(bf16[64,1792]{1,0:T(8,128)(2,1)S(1)} %pad_maximum_fusion.8), channel_id=1, source_target_pairs={{0,6},{2,4},{4,2},{6,0},{1,7},{3,5},{5,3},{7,1},{8,14},{10,12},{12... | collective-permute-start | bytes 688136 | tf_op jit(solution)/shard_map/ppermute | solution.py:32
  61.7 2.6 %collective-permute-start.24 = (bf16[64,896]{1,0:T(8,128)(2,1)S(1)}, bf16[64,896]{1,0:T(8,128)(2,1)S(1)}, u32[]{:S(2)}, u32[]{:S(2)}) collective-permute-start(bf16[64,896]{1,0:T(8,128)(2,1)S(1)} %get-tuple-element.28), channel_id=1, source_target_pairs={{0,6},{2,4},{4,2},{6,0},{1,7},{3,5},{5,3},{7,1},{8,14},{10,12},{12... | collective-permute-start | bytes 344072 | tf_op jit(solution)/shard_map/ppermute | solution.py:32
  64.8 5.6 %collective-permute-done.11 = bf16[64,1792]{1,0:T(8,128)(2,1)S(1)} collective-permute-done((bf16[64,1792]{1,0:T(8,128)(2,1)S(1)}, bf16[64,1792]{1,0:T(8,128)(2,1)S(1)}, u32[]{:S(2)}, u32[]{:S(2)}) %collective-permute-start.11) | collective-permute-done | bytes 229408 | tf_op jit(solution)/shard_map/ppermute | solution.py:32
  71.1 1.3 collective-permute-start.12
  72.4 2.5 %collective-permute-start.13 = (bf16[64,896]{1,0:T(8,128)(2,1)S(1)}, bf16[64,896]{1,0:T(8,128)(2,1)S(1)}, u32[]{:S(2)}, u32[]{:S(2)}) collective-permute-start(bf16[64,896]{1,0:T(8,128)(2,1)S(1)} %get-tuple-element.18), channel_id=1, source_target_pairs={{0,4},{2,6},{4,0},{6,2},{1,5},{3,7},{5,1},{7,3},{8,12},{10,14},{12... | collective-permute-start | bytes 344072 | tf_op jit(solution)/shard_map/ppermute | solution.py:32
  74.8 3.0 %collective-permute-start.14 = (bf16[64,896]{1,0:T(8,128)(2,1)S(1)}, bf16[64,896]{1,0:T(8,128)(2,1)S(1)}, u32[]{:S(2)}, u32[]{:S(2)}) collective-permute-start(bf16[64,896]{1,0:T(8,128)(2,1)S(1)} %get-tuple-element.18), channel_id=1, source_target_pairs={{0,6},{2,4},{4,2},{6,0},{1,7},{3,5},{5,3},{7,1},{8,14},{10,12},{12... | collective-permute-start | bytes 344072 | tf_op jit(solution)/shard_map/ppermute | solution.py:32
  77.8 1.1 collective-permute-start.15
  79.3 2.4 %collective-permute-start.26 = (bf16[64,1792]{1,0:T(8,128)(2,1)S(1)}, bf16[64,1792]{1,0:T(8,128)(2,1)S(1)}, u32[]{:S(2)}, u32[]{:S(2)}) collective-permute-start(bf16[64,1792]{1,0:T(8,128)(2,1)S(1)} %get-tuple-element.56), channel_id=1, source_target_pairs={{0,4},{2,6},{4,0},{6,2},{1,5},{3,7},{5,1},{7,3},{8,12},{10,14},{12... | collective-permute-start | bytes 688136 | tf_op jit(solution)/shard_map/ppermute | solution.py:32
  82.0 1.3 collective-permute-start.27
  83.3 1.5 %collective-permute-start.28 = (bf16[64,1792]{1,0:T(8,128)(2,1)S(1)}, bf16[64,1792]{1,0:T(8,128)(2,1)S(1)}, u32[]{:S(2)}, u32[]{:S(2)}) collective-permute-start(bf16[64,1792]{1,0:T(8,128)(2,1)S(1)} %get-tuple-element.56), channel_id=1, source_target_pairs={{0,1},{1,0},{2,3},{3,2},{4,5},{5,4},{6,7},{7,6},{8,9},{9,8},{10,11... | collective-permute-start | bytes 688136 | tf_op jit(solution)/shard_map/ppermute | solution.py:47
  85.0 1.3 collective-permute-done.16
  86.5 1.1 collective-permute-done.17
  87.8 1.1 collective-permute-done.18
  88.9 1.3 fusion.44
  90.3 2.0 %collective-permute-start.21 = (bf16[128,1024]{1,0:T(8,128)(2,1)S(1)}, bf16[128,1024]{1,0:T(8,128)(2,1)S(1)}, u32[]{:S(2)}, u32[]{:S(2)}) collective-permute-start(bf16[128,1024]{1,0:T(8,128)(2,1)S(1)} %get-tuple-element.22), channel_id=1, source_target_pairs={{0,24},{8,0},{16,8},{24,16},{1,25},{9,1},{17,9},{25,17},{2,26},{10... | collective-permute-start | bytes 786440 | tf_op jit(solution)/shard_map/ppermute | solution.py:28
  92.3 0.9 collective-permute-start.20
  93.9 2.3 %collective-permute-start.29 = (bf16[64,1792]{1,0:T(8,128)(2,1)S(1)}, bf16[64,1792]{1,0:T(8,128)(2,1)S(1)}, u32[]{:S(2)}, u32[]{:S(2)}) collective-permute-start(bf16[64,1792]{1,0:T(8,128)(2,1)S(1)} %collective-permute-done.25), channel_id=1, source_target_pairs={{0,1},{1,0},{2,3},{3,2},{4,5},{5,4},{6,7},{7,6},{8,9},{9,8},{10,11... | collective-permute-start | bytes 688136 | tf_op jit(solution)/shard_map/ppermute | solution.py:47
  96.4 1.0 collective-permute-done.29
  97.9 1.0 collective-permute-done.31
  98.9 1.3 fusion.4
  100.2 1.3 convolution_add_fusion
  101.6 2.0 %collective-permute-start.34 = (bf16[128,1024]{1,0:T(8,128)(2,1)S(1)}, bf16[128,1024]{1,0:T(8,128)(2,1)S(1)}, u32[]{:S(2)}, u32[]{:S(2)}) collective-permute-start(bf16[128,1024]{1,0:T(8,128)(2,1)S(1)} %get-tuple-element.25), channel_id=1, source_target_pairs={{0,24},{8,0},{16,8},{24,16},{1,25},{9,1},{17,9},{25,17},{2,26},{10... | collective-permute-start | bytes 786440 | tf_op jit(solution)/shard_map/ppermute | solution.py:28
  103.5 0.9 collective-permute-start.33
  104.8 1.1 fusion.11
  105.9 1.7 %collective-permute-done.19 = bf16[128,1024]{1,0:T(8,128)(2,1)S(1)} collective-permute-done((bf16[128,1024]{1,0:T(8,128)(2,1)S(1)}, bf16[128,1024]{1,0:T(8,128)(2,1)S(1)}, u32[]{:S(2)}, u32[]{:S(2)}) %collective-permute-start.19) | collective-permute-done | bytes 262176 | tf_op jit(solution)/shard_map/ppermute | solution.py:28
  107.8 1.4 %collective-permute-done.34 = bf16[128,1024]{1,0:T(8,128)(2,1)S(1)} collective-permute-done((bf16[128,1024]{1,0:T(8,128)(2,1)S(1)}, bf16[128,1024]{1,0:T(8,128)(2,1)S(1)}, u32[]{:S(2)}, u32[]{:S(2)}) %collective-permute-start.34) | collective-permute-done | bytes 262176 | tf_op jit(solution)/shard_map/ppermute | solution.py:28
  109.2 3.1 %collective-permute-done.33 = bf16[128,1024]{1,0:T(8,128)(2,1)S(1)} collective-permute-done((bf16[128,1024]{1,0:T(8,128)(2,1)S(1)}, bf16[128,1024]{1,0:T(8,128)(2,1)S(1)}, u32[]{:S(2)}, u32[]{:S(2)}) %collective-permute-start.33) | collective-permute-done | bytes 262176 | tf_op jit(solution)/shard_map/ppermute | solution.py:28
  112.3 6.6 %collective-permute-done.32 = bf16[128,1024]{1,0:T(8,128)(2,1)S(1)} collective-permute-done((bf16[128,1024]{1,0:T(8,128)(2,1)S(1)}, bf16[128,1024]{1,0:T(8,128)(2,1)S(1)}, u32[]{:S(2)}, u32[]{:S(2)}) %collective-permute-start.32) | collective-permute-done | bytes 262176 | tf_op jit(solution)/shard_map/ppermute | solution.py:28
  119.1 0.8 pad_maximum_fusion.5
  119.9 3.5 %all-to-all-start.1 = ((bf16[8,2,16,1024]{3,2,1,0:T(8,128)(2,1)}), bf16[8,2,16,1024]{3,2,1,0:T(8,128)(2,1)S(1)}, u32[]{:S(2)}, u32[]{:S(2)}) async-start(bf16[8,2,16,1024]{3,2,1,0:T(8,128)(2,1)} %pad_maximum_fusion.5), calls=%async_computation.1 | async-start | bytes 1048576 | tf_op jit(solution)/shard_map/all_to_all | solution.py:23
  123.7 3.9 %convolution_convert_fusion = bf16[896,1024]{1,0:T(8,128)(2,1)} fusion(bf16[512,896]{1,0:T(8,128)(2,1)} %copy-done.6, bf16[256,1024]{1,0:T(8,128)(2,1)} %bitcast.119, bf16[256,1024]{1,0:T(8,128)(2,1)S(1)} %bitcast.120), kind=kOutput, calls=%fused_computation | convolution fusion | flops 942538752 | bytes 3801088 | tf_op jit(solution)/shard_map/dot_general | solution.py:12
  127.6 2.5 %convolution_convert_fusion.2 = bf16[1024,896]{1,0:T(8,128)(2,1)} fusion(bf16[512,1792]{1,0:T(8,128)(2,1)S(1)} %copy-done.5, bf16[256,1024]{1,0:T(8,128)(2,1)S(1)} %bitcast.115, bf16[256,1024]{1,0:T(8,128)(2,1)S(1)} %bitcast.117), kind=kOutput, calls=%fused_computation.2 | convolution fusion | flops 942538752 | bytes 3801088 | tf_op jit(solution)/shard_map/dot_general | solution.py:12
  130.1 2.5 %convolution_convert_fusion.1 = bf16[1024,896]{1,0:T(8,128)(2,1)} fusion(bf16[512,1792]{1,0:T(8,128)(2,1)S(1)} %copy-done.5, bf16[256,1024]{1,0:T(8,128)(2,1)S(1)} %bitcast.116, bf16[256,1024]{1,0:T(8,128)(2,1)S(1)} %bitcast.118), kind=kOutput, calls=%fused_computation.1 | convolution fusion | flops 942538752 | bytes 3801088 | tf_op jit(solution)/shard_map/dot_general | solution.py:12
  132.6 8.7 %all-to-all-done.1 = bf16[8,2,16,1024]{3,2,1,0:T(8,128)(2,1)S(1)} async-done(((bf16[8,2,16,1024]{3,2,1,0:T(8,128)(2,1)}), bf16[8,2,16,1024]{3,2,1,0:T(8,128)(2,1)S(1)}, u32[]{:S(2)}, u32[]{:S(2)}) %all-to-all-start.1) | async-done | bytes 524320 | tf_op jit(solution)/shard_map/all_to_all | solution.py:23
  (93 shorter events, 12.5 us)
Async XLA Ops:
  0.6 51.8 %copy-start = (bf16[896,1024]{1,0:T(8,128)(2,1)S(1)}, bf16[896,1024]{1,0:T(8,128)(2,1)}, u32[]{:S(2)}) copy-start(bf16[896,1024]{1,0:T(8,128)(2,1)} %param.8) | copy-start | bytes 5505028
  26.5 6.6 %collective-permute-start.5 = (bf16[128,1024]{1,0:T(8,128)(2,1)S(1)}, bf16[128,1024]{1,0:T(8,128)(2,1)S(1)}, u32[]{:S(2)}, u32[]{:S(2)}) collective-permute-start(bf16[128,1024]{1,0:T(8,128)(2,1)S(1)} %bitcast.107), channel_id=1, source_target_pairs={{0,8},{8,16},{16,24},{24,0},{1,9},{9,17},{17,25},{25,1},{2,10},{10... | collective-permute-start | bytes 786440 | tf_op jit(solution)/shard_map/ppermute | solution.py:28
  27.8 11.8 %collective-permute-start.4 = (bf16[128,1024]{1,0:T(8,128)(2,1)S(1)}, bf16[128,1024]{1,0:T(8,128)(2,1)S(1)}, u32[]{:S(2)}, u32[]{:S(2)}) collective-permute-start(bf16[128,1024]{1,0:T(8,128)(2,1)S(1)} %bitcast.108), channel_id=1, source_target_pairs={{0,16},{8,24},{16,0},{24,8},{1,17},{9,25},{17,1},{25,9},{2,18},{10... | collective-permute-start | bytes 786440 | tf_op jit(solution)/shard_map/ppermute | solution.py:28
  30.5 10.6 %collective-permute-start.3 = (bf16[128,1024]{1,0:T(8,128)(2,1)S(1)}, bf16[128,1024]{1,0:T(8,128)(2,1)S(1)}, u32[]{:S(2)}, u32[]{:S(2)}) collective-permute-start(bf16[128,1024]{1,0:T(8,128)(2,1)S(1)} %bitcast.109), channel_id=1, source_target_pairs={{0,24},{8,0},{16,8},{24,16},{1,25},{9,1},{17,9},{25,17},{2,26},{10... | collective-permute-start | bytes 786440 | tf_op jit(solution)/shard_map/ppermute | solution.py:28
  31.5 9.6 %copy-start.1 = (bf16[1024,896]{1,0:T(8,128)(2,1)S(1)}, bf16[1024,896]{1,0:T(8,128)(2,1)}, u32[]{:S(2)}) copy-start(bf16[1024,896]{1,0:T(8,128)(2,1)} %param.7) | copy-start | bytes 5505028
  31.5 19.2 %collective-permute-start.2 = (bf16[128,1024]{1,0:T(8,128)(2,1)S(1)}, bf16[128,1024]{1,0:T(8,128)(2,1)S(1)}, u32[]{:S(2)}, u32[]{:S(2)}) collective-permute-start(bf16[128,1024]{1,0:T(8,128)(2,1)S(1)} %bitcast.103), channel_id=1, source_target_pairs={{0,8},{8,16},{16,24},{24,0},{1,9},{9,17},{17,25},{25,1},{2,10},{10... | collective-permute-start | bytes 786440 | tf_op jit(solution)/shard_map/ppermute | solution.py:28
  31.9 19.0 %collective-permute-start.1 = (bf16[128,1024]{1,0:T(8,128)(2,1)S(1)}, bf16[128,1024]{1,0:T(8,128)(2,1)S(1)}, u32[]{:S(2)}, u32[]{:S(2)}) collective-permute-start(bf16[128,1024]{1,0:T(8,128)(2,1)S(1)} %bitcast.104), channel_id=1, source_target_pairs={{0,16},{8,24},{16,0},{24,8},{1,17},{9,25},{17,1},{25,9},{2,18},{10... | collective-permute-start | bytes 786440 | tf_op jit(solution)/shard_map/ppermute | solution.py:28
  33.0 18.0 %collective-permute-start = (bf16[128,1024]{1,0:T(8,128)(2,1)S(1)}, bf16[128,1024]{1,0:T(8,128)(2,1)S(1)}, u32[]{:S(2)}, u32[]{:S(2)}) collective-permute-start(bf16[128,1024]{1,0:T(8,128)(2,1)S(1)} %bitcast.105), channel_id=1, source_target_pairs={{0,24},{8,0},{16,8},{24,16},{1,25},{9,1},{17,9},{25,17},{2,26},{10... | collective-permute-start | bytes 786440 | tf_op jit(solution)/shard_map/ppermute | solution.py:28
  41.9 6.5 %copy-start.2 = (bf16[1024,896]{1,0:T(8,128)(2,1)S(1)}, bf16[1024,896]{1,0:T(8,128)(2,1)}, u32[]{:S(2)}) copy-start(bf16[1024,896]{1,0:T(8,128)(2,1)} %param.6) | copy-start | bytes 5505028
  42.6 9.8 %collective-permute-start.6 = (f32[256,896]{1,0:T(8,128)S(1)}, f32[256,896]{1,0:T(8,128)S(1)}, u32[]{:S(2)}, u32[]{:S(2)}) collective-permute-start(f32[256,896]{1,0:T(8,128)S(1)} %fusion.18), channel_id=1, source_target_pairs={{0,1},{1,0},{2,3},{3,2},{4,5},{5,4},{6,7},{7,6},{8,9},{9,8},{10,11... | collective-permute-start | bytes 2752520 | tf_op jit(solution)/shard_map/ppermute | solution.py:47
  49.1 7.8 %collective-permute-start.8 = (f32[256,896]{1,0:T(8,128)S(1)}, f32[256,896]{1,0:T(8,128)S(1)}, u32[]{:S(2)}, u32[]{:S(2)}) collective-permute-start(f32[256,896]{1,0:T(8,128)S(1)} %fusion.16), channel_id=1, source_target_pairs={{0,1},{1,0},{2,3},{3,2},{4,5},{5,4},{6,7},{7,6},{8,9},{9,8},{10,11... | collective-permute-start | bytes 2752520 | tf_op jit(solution)/shard_map/ppermute | solution.py:47
  53.2 8.4 %collective-permute-start.7 = (f32[256,896]{1,0:T(8,128)S(1)}, f32[256,896]{1,0:T(8,128)S(1)}, u32[]{:S(2)}, u32[]{:S(2)}) collective-permute-start(f32[256,896]{1,0:T(8,128)S(1)} %fusion.14), channel_id=1, source_target_pairs={{0,1},{1,0},{2,3},{3,2},{4,5},{5,4},{6,7},{7,6},{8,9},{9,8},{10,11... | collective-permute-start | bytes 2752520 | tf_op jit(solution)/shard_map/ppermute | solution.py:47
  57.0 13.4 %collective-permute-start.11 = (bf16[64,1792]{1,0:T(8,128)(2,1)S(1)}, bf16[64,1792]{1,0:T(8,128)(2,1)S(1)}, u32[]{:S(2)}, u32[]{:S(2)}) collective-permute-start(bf16[64,1792]{1,0:T(8,128)(2,1)S(1)} %pad_maximum_fusion.8), channel_id=1, source_target_pairs={{0,6},{2,4},{4,2},{6,0},{1,7},{3,5},{5,3},{7,1},{8,14},{10,12},{12... | collective-permute-start | bytes 688136 | tf_op jit(solution)/shard_map/ppermute | solution.py:32
  59.6 10.8 %collective-permute-start.10 = (bf16[64,1792]{1,0:T(8,128)(2,1)S(1)}, bf16[64,1792]{1,0:T(8,128)(2,1)S(1)}, u32[]{:S(2)}, u32[]{:S(2)}) collective-permute-start(bf16[64,1792]{1,0:T(8,128)(2,1)S(1)} %pad_maximum_fusion.7), channel_id=1, source_target_pairs={{0,4},{2,6},{4,0},{6,2},{1,5},{3,7},{5,1},{7,3},{8,12},{10,14},{12... | collective-permute-start | bytes 688136 | tf_op jit(solution)/shard_map/ppermute | solution.py:32
  60.2 10.6 %collective-permute-start.9 = (bf16[64,1792]{1,0:T(8,128)(2,1)S(1)}, bf16[64,1792]{1,0:T(8,128)(2,1)S(1)}, u32[]{:S(2)}, u32[]{:S(2)}) collective-permute-start(bf16[64,1792]{1,0:T(8,128)(2,1)S(1)} %pad_maximum_fusion.6), channel_id=1, source_target_pairs={{0,2},{2,0},{4,6},{6,4},{1,3},{3,1},{5,7},{7,5},{8,10},{10,8},{12,... | collective-permute-start | bytes 688136 | tf_op jit(solution)/shard_map/ppermute | solution.py:32
  61.7 13.1 %collective-permute-start.24 = (bf16[64,896]{1,0:T(8,128)(2,1)S(1)}, bf16[64,896]{1,0:T(8,128)(2,1)S(1)}, u32[]{:S(2)}, u32[]{:S(2)}) collective-permute-start(bf16[64,896]{1,0:T(8,128)(2,1)S(1)} %get-tuple-element.28), channel_id=1, source_target_pairs={{0,6},{2,4},{4,2},{6,0},{1,7},{3,5},{5,3},{7,1},{8,14},{10,12},{12... | collective-permute-start | bytes 344072 | tf_op jit(solution)/shard_map/ppermute | solution.py:32
  64.3 13.6 %collective-permute-start.23 = (bf16[64,896]{1,0:T(8,128)(2,1)S(1)}, bf16[64,896]{1,0:T(8,128)(2,1)S(1)}, u32[]{:S(2)}, u32[]{:S(2)}) collective-permute-start(bf16[64,896]{1,0:T(8,128)(2,1)S(1)} %get-tuple-element.29), channel_id=1, source_target_pairs={{0,4},{2,6},{4,0},{6,2},{1,5},{3,7},{5,1},{7,3},{8,12},{10,14},{12... | collective-permute-start | bytes 344072 | tf_op jit(solution)/shard_map/ppermute | solution.py:32
  70.5 8.5 %collective-permute-start.22 = (bf16[64,896]{1,0:T(8,128)(2,1)S(1)}, bf16[64,896]{1,0:T(8,128)(2,1)S(1)}, u32[]{:S(2)}, u32[]{:S(2)}) collective-permute-start(bf16[64,896]{1,0:T(8,128)(2,1)S(1)} %get-tuple-element.27), channel_id=1, source_target_pairs={{0,2},{2,0},{4,6},{6,4},{1,3},{3,1},{5,7},{7,5},{8,10},{10,8},{12,... | collective-permute-start | bytes 344072 | tf_op jit(solution)/shard_map/ppermute | solution.py:32
  71.1 8.2 %collective-permute-start.12 = (bf16[64,896]{1,0:T(8,128)(2,1)S(1)}, bf16[64,896]{1,0:T(8,128)(2,1)S(1)}, u32[]{:S(2)}, u32[]{:S(2)}) collective-permute-start(bf16[64,896]{1,0:T(8,128)(2,1)S(1)} %get-tuple-element.18), channel_id=1, source_target_pairs={{0,2},{2,0},{4,6},{6,4},{1,3},{3,1},{5,7},{7,5},{8,10},{10,8},{12,... | collective-permute-start | bytes 344072 | tf_op jit(solution)/shard_map/ppermute | solution.py:32
  72.4 9.6 %collective-permute-start.13 = (bf16[64,896]{1,0:T(8,128)(2,1)S(1)}, bf16[64,896]{1,0:T(8,128)(2,1)S(1)}, u32[]{:S(2)}, u32[]{:S(2)}) collective-permute-start(bf16[64,896]{1,0:T(8,128)(2,1)S(1)} %get-tuple-element.18), channel_id=1, source_target_pairs={{0,4},{2,6},{4,0},{6,2},{1,5},{3,7},{5,1},{7,3},{8,12},{10,14},{12... | collective-permute-start | bytes 344072 | tf_op jit(solution)/shard_map/ppermute | solution.py:32
  74.8 8.5 %collective-permute-start.14 = (bf16[64,896]{1,0:T(8,128)(2,1)S(1)}, bf16[64,896]{1,0:T(8,128)(2,1)S(1)}, u32[]{:S(2)}, u32[]{:S(2)}) collective-permute-start(bf16[64,896]{1,0:T(8,128)(2,1)S(1)} %get-tuple-element.18), channel_id=1, source_target_pairs={{0,6},{2,4},{4,2},{6,0},{1,7},{3,5},{5,3},{7,1},{8,14},{10,12},{12... | collective-permute-start | bytes 344072 | tf_op jit(solution)/shard_map/ppermute | solution.py:32
  77.8 7.0 %collective-permute-start.15 = (bf16[64,896]{1,0:T(8,128)(2,1)S(1)}, bf16[64,896]{1,0:T(8,128)(2,1)S(1)}, u32[]{:S(2)}, u32[]{:S(2)}) collective-permute-start(bf16[64,896]{1,0:T(8,128)(2,1)S(1)} %get-tuple-element.18), channel_id=1, source_target_pairs={{0,1},{1,0},{2,3},{3,2},{4,5},{5,4},{6,7},{7,6},{8,9},{9,8},{10,11... | collective-permute-start | bytes 344072 | tf_op jit(solution)/shard_map/ppermute | solution.py:47
  79.2 13.1 %collective-permute-start.25 = (bf16[64,1792]{1,0:T(8,128)(2,1)S(1)}, bf16[64,1792]{1,0:T(8,128)(2,1)S(1)}, u32[]{:S(2)}, u32[]{:S(2)}) collective-permute-start(bf16[64,1792]{1,0:T(8,128)(2,1)S(1)} %get-tuple-element.56), channel_id=1, source_target_pairs={{0,2},{2,0},{4,6},{6,4},{1,3},{3,1},{5,7},{7,5},{8,10},{10,8},{12,... | collective-permute-start | bytes 688136 | tf_op jit(solution)/shard_map/ppermute | solution.py:32
  79.3 13.9 %collective-permute-start.26 = (bf16[64,1792]{1,0:T(8,128)(2,1)S(1)}, bf16[64,1792]{1,0:T(8,128)(2,1)S(1)}, u32[]{:S(2)}, u32[]{:S(2)}) collective-permute-start(bf16[64,1792]{1,0:T(8,128)(2,1)S(1)} %get-tuple-element.56), channel_id=1, source_target_pairs={{0,4},{2,6},{4,0},{6,2},{1,5},{3,7},{5,1},{7,3},{8,12},{10,14},{12... | collective-permute-start | bytes 688136 | tf_op jit(solution)/shard_map/ppermute | solution.py:32
  82.0 11.9 %collective-permute-start.27 = (bf16[64,1792]{1,0:T(8,128)(2,1)S(1)}, bf16[64,1792]{1,0:T(8,128)(2,1)S(1)}, u32[]{:S(2)}, u32[]{:S(2)}) collective-permute-start(bf16[64,1792]{1,0:T(8,128)(2,1)S(1)} %get-tuple-element.56), channel_id=1, source_target_pairs={{0,6},{2,4},{4,2},{6,0},{1,7},{3,5},{5,3},{7,1},{8,14},{10,12},{12... | collective-permute-start | bytes 688136 | tf_op jit(solution)/shard_map/ppermute | solution.py:32
  83.3 13.0 %collective-permute-start.28 = (bf16[64,1792]{1,0:T(8,128)(2,1)S(1)}, bf16[64,1792]{1,0:T(8,128)(2,1)S(1)}, u32[]{:S(2)}, u32[]{:S(2)}) collective-permute-start(bf16[64,1792]{1,0:T(8,128)(2,1)S(1)} %get-tuple-element.56), channel_id=1, source_target_pairs={{0,1},{1,0},{2,3},{3,2},{4,5},{5,4},{6,7},{7,6},{8,9},{9,8},{10,11... | collective-permute-start | bytes 688136 | tf_op jit(solution)/shard_map/ppermute | solution.py:47
  84.8 1.4 collective-permute-start.16
  86.2 1.3 collective-permute-start.17
  87.6 1.3 collective-permute-start.18
  88.9 1.3 copy-start.6
  90.3 14.1 %collective-permute-start.21 = (bf16[128,1024]{1,0:T(8,128)(2,1)S(1)}, bf16[128,1024]{1,0:T(8,128)(2,1)S(1)}, u32[]{:S(2)}, u32[]{:S(2)}) collective-permute-start(bf16[128,1024]{1,0:T(8,128)(2,1)S(1)} %get-tuple-element.22), channel_id=1, source_target_pairs={{0,24},{8,0},{16,8},{24,16},{1,25},{9,1},{17,9},{25,17},{2,26},{10... | collective-permute-start | bytes 786440 | tf_op jit(solution)/shard_map/ppermute | solution.py:28
  92.3 13.6 %collective-permute-start.20 = (bf16[128,1024]{1,0:T(8,128)(2,1)S(1)}, bf16[128,1024]{1,0:T(8,128)(2,1)S(1)}, u32[]{:S(2)}, u32[]{:S(2)}) collective-permute-start(bf16[128,1024]{1,0:T(8,128)(2,1)S(1)} %get-tuple-element.23), channel_id=1, source_target_pairs={{0,16},{8,24},{16,0},{24,8},{1,17},{9,25},{17,1},{25,9},{2,18},{10... | collective-permute-start | bytes 786440 | tf_op jit(solution)/shard_map/ppermute | solution.py:28
  93.2 14.5 %collective-permute-start.19 = (bf16[128,1024]{1,0:T(8,128)(2,1)S(1)}, bf16[128,1024]{1,0:T(8,128)(2,1)S(1)}, u32[]{:S(2)}, u32[]{:S(2)}) collective-permute-start(bf16[128,1024]{1,0:T(8,128)(2,1)S(1)} %get-tuple-element.21), channel_id=1, source_target_pairs={{0,8},{8,16},{16,24},{24,0},{1,9},{9,17},{17,25},{25,1},{2,10},{10... | collective-permute-start | bytes 786440 | tf_op jit(solution)/shard_map/ppermute | solution.py:28
  93.9 3.5 %collective-permute-start.29 = (bf16[64,1792]{1,0:T(8,128)(2,1)S(1)}, bf16[64,1792]{1,0:T(8,128)(2,1)S(1)}, u32[]{:S(2)}, u32[]{:S(2)}) collective-permute-start(bf16[64,1792]{1,0:T(8,128)(2,1)S(1)} %collective-permute-done.25), channel_id=1, source_target_pairs={{0,1},{1,0},{2,3},{3,2},{4,5},{5,4},{6,7},{7,6},{8,9},{9,8},{10,11... | collective-permute-start | bytes 688136 | tf_op jit(solution)/shard_map/ppermute | solution.py:47
  96.3 1.6 %collective-permute-start.30 = (bf16[64,1792]{1,0:T(8,128)(2,1)S(1)}, bf16[64,1792]{1,0:T(8,128)(2,1)S(1)}, u32[]{:S(2)}, u32[]{:S(2)}) collective-permute-start(bf16[64,1792]{1,0:T(8,128)(2,1)S(1)} %collective-permute-done.26), channel_id=1, source_target_pairs={{0,1},{1,0},{2,3},{3,2},{4,5},{5,4},{6,7},{7,6},{8,9},{9,8},{10,11... | collective-permute-start | bytes 688136 | tf_op jit(solution)/shard_map/ppermute | solution.py:47
  97.4 1.5 %collective-permute-start.31 = (bf16[64,1792]{1,0:T(8,128)(2,1)S(1)}, bf16[64,1792]{1,0:T(8,128)(2,1)S(1)}, u32[]{:S(2)}, u32[]{:S(2)}) collective-permute-start(bf16[64,1792]{1,0:T(8,128)(2,1)S(1)} %collective-permute-done.27), channel_id=1, source_target_pairs={{0,1},{1,0},{2,3},{3,2},{4,5},{5,4},{6,7},{7,6},{8,9},{9,8},{10,11... | collective-permute-start | bytes 688136 | tf_op jit(solution)/shard_map/ppermute | solution.py:47
  98.9 1.3 copy-start.4
  101.6 7.6 %collective-permute-start.34 = (bf16[128,1024]{1,0:T(8,128)(2,1)S(1)}, bf16[128,1024]{1,0:T(8,128)(2,1)S(1)}, u32[]{:S(2)}, u32[]{:S(2)}) collective-permute-start(bf16[128,1024]{1,0:T(8,128)(2,1)S(1)} %get-tuple-element.25), channel_id=1, source_target_pairs={{0,24},{8,0},{16,8},{24,16},{1,25},{9,1},{17,9},{25,17},{2,26},{10... | collective-permute-start | bytes 786440 | tf_op jit(solution)/shard_map/ppermute | solution.py:28
  103.5 8.8 %collective-permute-start.33 = (bf16[128,1024]{1,0:T(8,128)(2,1)S(1)}, bf16[128,1024]{1,0:T(8,128)(2,1)S(1)}, u32[]{:S(2)}, u32[]{:S(2)}) collective-permute-start(bf16[128,1024]{1,0:T(8,128)(2,1)S(1)} %get-tuple-element.26), channel_id=1, source_target_pairs={{0,16},{8,24},{16,0},{24,8},{1,17},{9,25},{17,1},{25,9},{2,18},{10... | collective-permute-start | bytes 786440 | tf_op jit(solution)/shard_map/ppermute | solution.py:28
  104.4 14.5 %collective-permute-start.32 = (bf16[128,1024]{1,0:T(8,128)(2,1)S(1)}, bf16[128,1024]{1,0:T(8,128)(2,1)S(1)}, u32[]{:S(2)}, u32[]{:S(2)}) collective-permute-start(bf16[128,1024]{1,0:T(8,128)(2,1)S(1)} %get-tuple-element.24), channel_id=1, source_target_pairs={{0,8},{8,16},{16,24},{24,0},{1,9},{9,17},{17,25},{25,1},{2,10},{10... | collective-permute-start | bytes 786440 | tf_op jit(solution)/shard_map/ppermute | solution.py:28
  119.9 21.4 %all-to-all-start.1 = ((bf16[8,2,16,1024]{3,2,1,0:T(8,128)(2,1)}), bf16[8,2,16,1024]{3,2,1,0:T(8,128)(2,1)S(1)}, u32[]{:S(2)}, u32[]{:S(2)}) async-start(bf16[8,2,16,1024]{3,2,1,0:T(8,128)(2,1)} %pad_maximum_fusion.5), calls=%async_computation.1 | async-start | bytes 1048576 | tf_op jit(solution)/shard_map/all_to_all | solution.py:23
  123.7 3.9 %copy-start.3 = (bf16[4,64,1024]{2,1,0:T(8,128)(2,1)S(1)}, bf16[4,64,1024]{2,1,0:T(8,128)(2,1)}, u32[]{:S(2)}) copy-start(bf16[4,64,1024]{2,1,0:T(8,128)(2,1)} %fusion.8) | copy-start | bytes 1572868
  123.7 3.9 %copy-start.5 = (bf16[512,1792]{1,0:T(8,128)(2,1)S(1)}, bf16[512,1792]{1,0:T(8,128)(2,1)}, u32[]{:S(2)}) copy-start(bf16[512,1792]{1,0:T(8,128)(2,1)} %copy-done.4) | copy-start | bytes 5505028

commit v4 on v3

--- a/solution.py
+++ b/solution.py
@@ -134,8 +134,8 @@
     tokens_held = sum_y(
         dot(gate_all, gate_weight, ((1,), (1,))) + dot(up_all, up_weight, ((1,), (1,)))
     )
-    both = jnp.stack([held.reshape(NZ, 16, -1) for held in (mixed_held, tokens_held)], axis=1)
-    mixed, tokens_grad = sum_z(both)
+    both = sum_z(jnp.concatenate([mixed_held, tokens_held], axis=1).reshape(NZ, 16, -1))
+    mixed, tokens_grad = both[:, : both.shape[1] // 2], both[:, both.shape[1] // 2 :]
     panel, grad_panel = ordered(panel), ordered(grad_panel)
     down_grad = dot(hidden_all, grad_panel, ((0,), (0,))).astype(BF)
     gate_grad = dot(panel, gate_all, ((0,), (0,))).astype(BF)

time: 142 us -> 142 us (level)
  no operation moved by 1% of the time
where the time goes in v4:
time: 142 us
  starting transfers between devices  51.4 us (36%)
  waiting for transfers between devices  40.6 us (29%)
  blocking collectives  24.8 us (17%)
  matrix products  17.1 us (12%)
  other arithmetic  5.68 us (4%)
    all_to_all x1, blocking collectives, copies_z(): lax.all_to_all(jnp.broadcast_to(blocks[None], (NZ,) + blocks.shape), 'z',...  24.8 us
    ppermute x12, waiting for transfers between devices, shifted(): return lax.ppermute(array, axis, [(i, (i + d) % n) for i in range(n)])  20.1 us
    ppermute x12, starting transfers between devices, crossed(): return lax.ppermute(array, 'x', [(i, i ^ d) for i in range(NX)])  17.3 us
    dot_general x12, matrix products, dot(): lax.dot_general(left, right, (contract, ((), ())), preferred_element_type...  17.1 us
    ppermute x11, starting transfers between devices, swap_core(): return lax.ppermute(half, 'c', [(0, 1), (1, 0)])  16.1 us
    ppermute x12, starting transfers between devices, shifted(): return lax.ppermute(array, axis, [(i, (i + d) % n) for i in range(n)])  14.4 us
    all_to_all x1, waiting for transfers between devices, sum_z(): lax.all_to_all(blocks, ('z', 'x'), 0, 0, axis_index_groups=Z_GROUPS, tile...  8.66 us
    ppermute x12, waiting for transfers between devices, crossed(): return lax.ppermute(array, 'x', [(i, i ^ d) for i in range(NX)])  6.32 us
  transfers between devices with their start and end apart: 36, of which 19 were waited for; matrix products, arithmetic and copies ran while one was open for 15% of the time, Pallas kernels for 0%

profile of v4, /device:TPU:1, one launch (start us, length us, event | category | flops | bytes accessed | tf_op | source)
XLA Modules:
  0.0 142.0 jit_solution(15580416000021135812)
XLA Ops:
  0.6 0.9 pad_maximum_fusion.10
  1.6 24.8 %all_to_all.10 = bf16[8,2,16,1024]{3,2,1,0:T(8,128)(2,1)S(1)} all-to-all(bf16[8,2,16,1024]{3,2,1,0:T(8,128)(2,1)S(1)} %broadcast_in_dim.4), channel_id=1, replica_groups=mesh['z'=8,'y'=4,'x'=4,'c'=2] {'z'}, dimensions={0} | all-to-all | bytes 1048576 | tf_op jit(solution)/shard_map/all_to_all | solution.py:19
  26.5 1.4 collective-permute-start.5
  27.8 2.6 %collective-permute-start.4 = (bf16[128,1024]{1,0:T(8,128)(2,1)S(1)}, bf16[128,1024]{1,0:T(8,128)(2,1)S(1)}, u32[]{:S(2)}, u32[]{:S(2)}) collective-permute-start(bf16[128,1024]{1,0:T(8,128)(2,1)S(1)} %bitcast.97), channel_id=1, source_target_pairs={{0,16},{8,24},{16,0},{24,8},{1,17},{9,25},{17,1},{25,9},{2,18},{10... | collective-permute-start | bytes 786440 | tf_op jit(solution)/shard_map/ppermute | solution.py:28
  30.5 1.1 collective-permute-start.3
  31.9 0.8 collective-permute-start.1
  33.0 1.5 %collective-permute-start = (bf16[128,1024]{1,0:T(8,128)(2,1)S(1)}, bf16[128,1024]{1,0:T(8,128)(2,1)S(1)}, u32[]{:S(2)}, u32[]{:S(2)}) collective-permute-start(bf16[128,1024]{1,0:T(8,128)(2,1)S(1)} %bitcast.94), channel_id=1, source_target_pairs={{0,24},{8,0},{16,8},{24,16},{1,25},{9,1},{17,9},{25,17},{2,26},{10... | collective-permute-start | bytes 786440 | tf_op jit(solution)/shard_map/ppermute | solution.py:28
  34.5 5.2 %collective-permute-done.4 = bf16[128,1024]{1,0:T(8,128)(2,1)S(1)} collective-permute-done((bf16[128,1024]{1,0:T(8,128)(2,1)S(1)}, bf16[128,1024]{1,0:T(8,128)(2,1)S(1)}, u32[]{:S(2)}, u32[]{:S(2)}) %collective-permute-start.4) | collective-permute-done | bytes 262176 | tf_op jit(solution)/shard_map/ppermute | solution.py:28
  39.7 1.4 collective-permute-done.3
  42.6 5.8 %collective-permute-start.6 = (f32[256,896]{1,0:T(8,128)S(1)}, f32[256,896]{1,0:T(8,128)S(1)}, u32[]{:S(2)}, u32[]{:S(2)}) collective-permute-start(f32[256,896]{1,0:T(8,128)S(1)} %fusion.18), channel_id=1, source_target_pairs={{0,1},{1,0},{2,3},{3,2},{4,5},{5,4},{6,7},{7,6},{8,9},{9,8},{10,11... | collective-permute-start | bytes 2752520 | tf_op jit(solution)/shard_map/ppermute | solution.py:47
  49.1 0.8 collective-permute-start.8
  51.4 1.1 fusion.8
  52.4 0.7 fusion.14
  53.2 3.6 %collective-permute-start.7 = (f32[256,896]{1,0:T(8,128)S(1)}, f32[256,896]{1,0:T(8,128)S(1)}, u32[]{:S(2)}, u32[]{:S(2)}) collective-permute-start(f32[256,896]{1,0:T(8,128)S(1)} %fusion.14), channel_id=1, source_target_pairs={{0,1},{1,0},{2,3},{3,2},{4,5},{5,4},{6,7},{7,6},{8,9},{9,8},{10,11... | collective-permute-start | bytes 2752520 | tf_op jit(solution)/shard_map/ppermute | solution.py:47
  57.0 2.6 %collective-permute-start.11 = (bf16[64,1792]{1,0:T(8,128)(2,1)S(1)}, bf16[64,1792]{1,0:T(8,128)(2,1)S(1)}, u32[]{:S(2)}, u32[]{:S(2)}) collective-permute-start(bf16[64,1792]{1,0:T(8,128)(2,1)S(1)} %pad_maximum_fusion.8), channel_id=1, source_target_pairs={{0,6},{2,4},{4,2},{6,0},{1,7},{3,5},{5,3},{7,1},{8,14},{10,12},{12... | collective-permute-start | bytes 688136 | tf_op jit(solution)/shard_map/ppermute | solution.py:32
  61.7 2.6 %collective-permute-start.24 = (bf16[64,896]{1,0:T(8,128)(2,1)S(1)}, bf16[64,896]{1,0:T(8,128)(2,1)S(1)}, u32[]{:S(2)}, u32[]{:S(2)}) collective-permute-start(bf16[64,896]{1,0:T(8,128)(2,1)S(1)} %get-tuple-element.28), channel_id=1, source_target_pairs={{0,6},{2,4},{4,2},{6,0},{1,7},{3,5},{5,3},{7,1},{8,14},{10,12},{12... | collective-permute-start | bytes 344072 | tf_op jit(solution)/shard_map/ppermute | solution.py:32
  64.8 5.6 %collective-permute-done.11 = bf16[64,1792]{1,0:T(8,128)(2,1)S(1)} collective-permute-done((bf16[64,1792]{1,0:T(8,128)(2,1)S(1)}, bf16[64,1792]{1,0:T(8,128)(2,1)S(1)}, u32[]{:S(2)}, u32[]{:S(2)}) %collective-permute-start.11) | collective-permute-done | bytes 229408 | tf_op jit(solution)/shard_map/ppermute | solution.py:32
  71.1 1.3 collective-permute-start.12
  72.4 2.5 %collective-permute-start.13 = (bf16[64,896]{1,0:T(8,128)(2,1)S(1)}, bf16[64,896]{1,0:T(8,128)(2,1)S(1)}, u32[]{:S(2)}, u32[]{:S(2)}) collective-permute-start(bf16[64,896]{1,0:T(8,128)(2,1)S(1)} %get-tuple-element.18), channel_id=1, source_target_pairs={{0,4},{2,6},{4,0},{6,2},{1,5},{3,7},{5,1},{7,3},{8,12},{10,14},{12... | collective-permute-start | bytes 344072 | tf_op jit(solution)/shard_map/ppermute | solution.py:32
  74.8 3.0 %collective-permute-start.14 = (bf16[64,896]{1,0:T(8,128)(2,1)S(1)}, bf16[64,896]{1,0:T(8,128)(2,1)S(1)}, u32[]{:S(2)}, u32[]{:S(2)}) collective-permute-start(bf16[64,896]{1,0:T(8,128)(2,1)S(1)} %get-tuple-element.18), channel_id=1, source_target_pairs={{0,6},{2,4},{4,2},{6,0},{1,7},{3,5},{5,3},{7,1},{8,14},{10,12},{12... | collective-permute-start | bytes 344072 | tf_op jit(solution)/shard_map/ppermute | solution.py:32
  77.8 1.1 collective-permute-start.15
  79.3 2.4 %collective-permute-start.26 = (bf16[64,1792]{1,0:T(8,128)(2,1)S(1)}, bf16[64,1792]{1,0:T(8,128)(2,1)S(1)}, u32[]{:S(2)}, u32[]{:S(2)}) collective-permute-start(bf16[64,1792]{1,0:T(8,128)(2,1)S(1)} %get-tuple-element.56), channel_id=1, source_target_pairs={{0,4},{2,6},{4,0},{6,2},{1,5},{3,7},{5,1},{7,3},{8,12},{10,14},{12... | collective-permute-start | bytes 688136 | tf_op jit(solution)/shard_map/ppermute | solution.py:32
  82.0 1.3 collective-permute-start.27
  83.3 1.5 %collective-permute-start.28 = (bf16[64,1792]{1,0:T(8,128)(2,1)S(1)}, bf16[64,1792]{1,0:T(8,128)(2,1)S(1)}, u32[]{:S(2)}, u32[]{:S(2)}) collective-permute-start(bf16[64,1792]{1,0:T(8,128)(2,1)S(1)} %get-tuple-element.56), channel_id=1, source_target_pairs={{0,1},{1,0},{2,3},{3,2},{4,5},{5,4},{6,7},{7,6},{8,9},{9,8},{10,11... | collective-permute-start | bytes 688136 | tf_op jit(solution)/shard_map/ppermute | solution.py:47
  85.0 1.3 collective-permute-done.16
  86.5 1.1 collective-permute-done.17
  87.8 1.1 collective-permute-done.18
  88.9 1.3 fusion.45
  90.3 2.0 %collective-permute-start.21 = (bf16[128,1024]{1,0:T(8,128)(2,1)S(1)}, bf16[128,1024]{1,0:T(8,128)(2,1)S(1)}, u32[]{:S(2)}, u32[]{:S(2)}) collective-permute-start(bf16[128,1024]{1,0:T(8,128)(2,1)S(1)} %get-tuple-element.22), channel_id=1, source_target_pairs={{0,24},{8,0},{16,8},{24,16},{1,25},{9,1},{17,9},{25,17},{2,26},{10... | collective-permute-start | bytes 786440 | tf_op jit(solution)/shard_map/ppermute | solution.py:28
  92.3 0.9 collective-permute-start.20
  93.9 2.3 %collective-permute-start.29 = (bf16[64,1792]{1,0:T(8,128)(2,1)S(1)}, bf16[64,1792]{1,0:T(8,128)(2,1)S(1)}, u32[]{:S(2)}, u32[]{:S(2)}) collective-permute-start(bf16[64,1792]{1,0:T(8,128)(2,1)S(1)} %collective-permute-done.25), channel_id=1, source_target_pairs={{0,1},{1,0},{2,3},{3,2},{4,5},{5,4},{6,7},{7,6},{8,9},{9,8},{10,11... | collective-permute-start | bytes 688136 | tf_op jit(solution)/shard_map/ppermute | solution.py:47
  96.4 1.0 collective-permute-done.29
  97.9 1.0 collective-permute-done.31
  98.9 1.3 fusion.4
  100.2 1.3 convolution_add_fusion
  101.6 2.0 %collective-permute-start.34 = (bf16[128,1024]{1,0:T(8,128)(2,1)S(1)}, bf16[128,1024]{1,0:T(8,128)(2,1)S(1)}, u32[]{:S(2)}, u32[]{:S(2)}) collective-permute-start(bf16[128,1024]{1,0:T(8,128)(2,1)S(1)} %get-tuple-element.25), channel_id=1, source_target_pairs={{0,24},{8,0},{16,8},{24,16},{1,25},{9,1},{17,9},{25,17},{2,26},{10... | collective-permute-start | bytes 786440 | tf_op jit(solution)/shard_map/ppermute | solution.py:28
  103.5 0.9 collective-permute-start.33
  104.8 1.1 fusion.11
  105.9 1.7 %collective-permute-done.19 = bf16[128,1024]{1,0:T(8,128)(2,1)S(1)} collective-permute-done((bf16[128,1024]{1,0:T(8,128)(2,1)S(1)}, bf16[128,1024]{1,0:T(8,128)(2,1)S(1)}, u32[]{:S(2)}, u32[]{:S(2)}) %collective-permute-start.19) | collective-permute-done | bytes 262176 | tf_op jit(solution)/shard_map/ppermute | solution.py:28
  107.8 1.4 %collective-permute-done.34 = bf16[128,1024]{1,0:T(8,128)(2,1)S(1)} collective-permute-done((bf16[128,1024]{1,0:T(8,128)(2,1)S(1)}, bf16[128,1024]{1,0:T(8,128)(2,1)S(1)}, u32[]{:S(2)}, u32[]{:S(2)}) %collective-permute-start.34) | collective-permute-done | bytes 262176 | tf_op jit(solution)/shard_map/ppermute | solution.py:28
  109.2 3.1 %collective-permute-done.33 = bf16[128,1024]{1,0:T(8,128)(2,1)S(1)} collective-permute-done((bf16[128,1024]{1,0:T(8,128)(2,1)S(1)}, bf16[128,1024]{1,0:T(8,128)(2,1)S(1)}, u32[]{:S(2)}, u32[]{:S(2)}) %collective-permute-start.33) | collective-permute-done | bytes 262176 | tf_op jit(solution)/shard_map/ppermute | solution.py:28
  112.3 6.6 %collective-permute-done.32 = bf16[128,1024]{1,0:T(8,128)(2,1)S(1)} collective-permute-done((bf16[128,1024]{1,0:T(8,128)(2,1)S(1)}, bf16[128,1024]{1,0:T(8,128)(2,1)S(1)}, u32[]{:S(2)}, u32[]{:S(2)}) %collective-permute-start.32) | collective-permute-done | bytes 262176 | tf_op jit(solution)/shard_map/ppermute | solution.py:28
  119.1 0.8 pad_maximum_fusion.5
  119.9 3.5 %all-to-all-start.1 = ((bf16[8,16,2048]{2,1,0:T(8,128)(2,1)}), bf16[8,16,2048]{2,1,0:T(8,128)(2,1)S(1)}, u32[]{:S(2)}, u32[]{:S(2)}) async-start(bf16[8,16,2048]{2,1,0:T(8,128)(2,1)} %bitcast.22), calls=%async_computation.1 | async-start | bytes 1048576 | tf_op jit(solution)/shard_map/all_to_all | solution.py:23
  123.7 3.9 %convolution_convert_fusion = bf16[896,1024]{1,0:T(8,128)(2,1)} fusion(bf16[512,896]{1,0:T(8,128)(2,1)} %copy-done.6, bf16[256,1024]{1,0:T(8,128)(2,1)} %bitcast.108, bf16[256,1024]{1,0:T(8,128)(2,1)S(1)} %bitcast.109), kind=kOutput, calls=%fused_computation | convolution fusion | flops 942538752 | bytes 3801088 | tf_op jit(solution)/shard_map/dot_general | solution.py:12
  127.6 2.5 %convolution_convert_fusion.2 = bf16[1024,896]{1,0:T(8,128)(2,1)} fusion(bf16[512,1792]{1,0:T(8,128)(2,1)S(1)} %copy-done.5, bf16[256,1024]{1,0:T(8,128)(2,1)S(1)} %bitcast.104, bf16[256,1024]{1,0:T(8,128)(2,1)S(1)} %bitcast.106), kind=kOutput, calls=%fused_computation.2 | convolution fusion | flops 942538752 | bytes 3801088 | tf_op jit(solution)/shard_map/dot_general | solution.py:12
  130.1 2.5 %convolution_convert_fusion.1 = bf16[1024,896]{1,0:T(8,128)(2,1)} fusion(bf16[512,1792]{1,0:T(8,128)(2,1)S(1)} %copy-done.5, bf16[256,1024]{1,0:T(8,128)(2,1)S(1)} %bitcast.105, bf16[256,1024]{1,0:T(8,128)(2,1)S(1)} %bitcast.107), kind=kOutput, calls=%fused_computation.1 | convolution fusion | flops 942538752 | bytes 3801088 | tf_op jit(solution)/shard_map/dot_general | solution.py:12
  132.6 8.7 %all-to-all-done.1 = bf16[8,16,2048]{2,1,0:T(8,128)(2,1)S(1)} async-done(((bf16[8,16,2048]{2,1,0:T(8,128)(2,1)}), bf16[8,16,2048]{2,1,0:T(8,128)(2,1)S(1)}, u32[]{:S(2)}, u32[]{:S(2)}) %all-to-all-start.1) | async-done | bytes 524320 | tf_op jit(solution)/shard_map/all_to_all | solution.py:23
  (93 shorter events, 12.5 us)
Async XLA Ops:
  0.6 51.8 %copy-start = (bf16[896,1024]{1,0:T(8,128)(2,1)S(1)}, bf16[896,1024]{1,0:T(8,128)(2,1)}, u32[]{:S(2)}) copy-start(bf16[896,1024]{1,0:T(8,128)(2,1)} %param.8) | copy-start | bytes 5505028
  26.5 6.6 %collective-permute-start.5 = (bf16[128,1024]{1,0:T(8,128)(2,1)S(1)}, bf16[128,1024]{1,0:T(8,128)(2,1)S(1)}, u32[]{:S(2)}, u32[]{:S(2)}) collective-permute-start(bf16[128,1024]{1,0:T(8,128)(2,1)S(1)} %bitcast.96), channel_id=1, source_target_pairs={{0,8},{8,16},{16,24},{24,0},{1,9},{9,17},{17,25},{25,1},{2,10},{10... | collective-permute-start | bytes 786440 | tf_op jit(solution)/shard_map/ppermute | solution.py:28
  27.8 11.8 %collective-permute-start.4 = (bf16[128,1024]{1,0:T(8,128)(2,1)S(1)}, bf16[128,1024]{1,0:T(8,128)(2,1)S(1)}, u32[]{:S(2)}, u32[]{:S(2)}) collective-permute-start(bf16[128,1024]{1,0:T(8,128)(2,1)S(1)} %bitcast.97), channel_id=1, source_target_pairs={{0,16},{8,24},{16,0},{24,8},{1,17},{9,25},{17,1},{25,9},{2,18},{10... | collective-permute-start | bytes 786440 | tf_op jit(solution)/shard_map/ppermute | solution.py:28
  30.5 10.6 %collective-permute-start.3 = (bf16[128,1024]{1,0:T(8,128)(2,1)S(1)}, bf16[128,1024]{1,0:T(8,128)(2,1)S(1)}, u32[]{:S(2)}, u32[]{:S(2)}) collective-permute-start(bf16[128,1024]{1,0:T(8,128)(2,1)S(1)} %bitcast.98), channel_id=1, source_target_pairs={{0,24},{8,0},{16,8},{24,16},{1,25},{9,1},{17,9},{25,17},{2,26},{10... | collective-permute-start | bytes 786440 | tf_op jit(solution)/shard_map/ppermute | solution.py:28
  31.5 9.6 %copy-start.1 = (bf16[1024,896]{1,0:T(8,128)(2,1)S(1)}, bf16[1024,896]{1,0:T(8,128)(2,1)}, u32[]{:S(2)}) copy-start(bf16[1024,896]{1,0:T(8,128)(2,1)} %param.7) | copy-start | bytes 5505028
  31.5 19.2 %collective-permute-start.2 = (bf16[128,1024]{1,0:T(8,128)(2,1)S(1)}, bf16[128,1024]{1,0:T(8,128)(2,1)S(1)}, u32[]{:S(2)}, u32[]{:S(2)}) collective-permute-start(bf16[128,1024]{1,0:T(8,128)(2,1)S(1)} %bitcast.92), channel_id=1, source_target_pairs={{0,8},{8,16},{16,24},{24,0},{1,9},{9,17},{17,25},{25,1},{2,10},{10... | collective-permute-start | bytes 786440 | tf_op jit(solution)/shard_map/ppermute | solution.py:28
  31.9 19.0 %collective-permute-start.1 = (bf16[128,1024]{1,0:T(8,128)(2,1)S(1)}, bf16[128,1024]{1,0:T(8,128)(2,1)S(1)}, u32[]{:S(2)}, u32[]{:S(2)}) collective-permute-start(bf16[128,1024]{1,0:T(8,128)(2,1)S(1)} %bitcast.93), channel_id=1, source_target_pairs={{0,16},{8,24},{16,0},{24,8},{1,17},{9,25},{17,1},{25,9},{2,18},{10... | collective-permute-start | bytes 786440 | tf_op jit(solution)/shard_map/ppermute | solution.py:28
  33.0 18.0 %collective-permute-start = (bf16[128,1024]{1,0:T(8,128)(2,1)S(1)}, bf16[128,1024]{1,0:T(8,128)(2,1)S(1)}, u32[]{:S(2)}, u32[]{:S(2)}) collective-permute-start(bf16[128,1024]{1,0:T(8,128)(2,1)S(1)} %bitcast.94), channel_id=1, source_target_pairs={{0,24},{8,0},{16,8},{24,16},{1,25},{9,1},{17,9},{25,17},{2,26},{10... | collective-permute-start | bytes 786440 | tf_op jit(solution)/shard_map/ppermute | solution.py:28
  41.9 6.5 %copy-start.2 = (bf16[1024,896]{1,0:T(8,128)(2,1)S(1)}, bf16[1024,896]{1,0:T(8,128)(2,1)}, u32[]{:S(2)}) copy-start(bf16[1024,896]{1,0:T(8,128)(2,1)} %param.6) | copy-start | bytes 5505028
  42.6 9.8 %collective-permute-start.6 = (f32[256,896]{1,0:T(8,128)S(1)}, f32[256,896]{1,0:T(8,128)S(1)}, u32[]{:S(2)}, u32[]{:S(2)}) collective-permute-start(f32[256,896]{1,0:T(8,128)S(1)} %fusion.18), channel_id=1, source_target_pairs={{0,1},{1,0},{2,3},{3,2},{4,5},{5,4},{6,7},{7,6},{8,9},{9,8},{10,11... | collective-permute-start | bytes 2752520 | tf_op jit(solution)/shard_map/ppermute | solution.py:47
  49.1 7.8 %collective-permute-start.8 = (f32[256,896]{1,0:T(8,128)S(1)}, f32[256,896]{1,0:T(8,128)S(1)}, u32[]{:S(2)}, u32[]{:S(2)}) collective-permute-start(f32[256,896]{1,0:T(8,128)S(1)} %fusion.16), channel_id=1, source_target_pairs={{0,1},{1,0},{2,3},{3,2},{4,5},{5,4},{6,7},{7,6},{8,9},{9,8},{10,11... | collective-permute-start | bytes 2752520 | tf_op jit(solution)/shard_map/ppermute | solution.py:47
  53.2 8.4 %collective-permute-start.7 = (f32[256,896]{1,0:T(8,128)S(1)}, f32[256,896]{1,0:T(8,128)S(1)}, u32[]{:S(2)}, u32[]{:S(2)}) collective-permute-start(f32[256,896]{1,0:T(8,128)S(1)} %fusion.14), channel_id=1, source_target_pairs={{0,1},{1,0},{2,3},{3,2},{4,5},{5,4},{6,7},{7,6},{8,9},{9,8},{10,11... | collective-permute-start | bytes 2752520 | tf_op jit(solution)/shard_map/ppermute | solution.py:47
  57.0 13.4 %collective-permute-start.11 = (bf16[64,1792]{1,0:T(8,128)(2,1)S(1)}, bf16[64,1792]{1,0:T(8,128)(2,1)S(1)}, u32[]{:S(2)}, u32[]{:S(2)}) collective-permute-start(bf16[64,1792]{1,0:T(8,128)(2,1)S(1)} %pad_maximum_fusion.8), channel_id=1, source_target_pairs={{0,6},{2,4},{4,2},{6,0},{1,7},{3,5},{5,3},{7,1},{8,14},{10,12},{12... | collective-permute-start | bytes 688136 | tf_op jit(solution)/shard_map/ppermute | solution.py:32
  59.6 10.8 %collective-permute-start.10 = (bf16[64,1792]{1,0:T(8,128)(2,1)S(1)}, bf16[64,1792]{1,0:T(8,128)(2,1)S(1)}, u32[]{:S(2)}, u32[]{:S(2)}) collective-permute-start(bf16[64,1792]{1,0:T(8,128)(2,1)S(1)} %pad_maximum_fusion.7), channel_id=1, source_target_pairs={{0,4},{2,6},{4,0},{6,2},{1,5},{3,7},{5,1},{7,3},{8,12},{10,14},{12... | collective-permute-start | bytes 688136 | tf_op jit(solution)/shard_map/ppermute | solution.py:32
  60.2 10.6 %collective-permute-start.9 = (bf16[64,1792]{1,0:T(8,128)(2,1)S(1)}, bf16[64,1792]{1,0:T(8,128)(2,1)S(1)}, u32[]{:S(2)}, u32[]{:S(2)}) collective-permute-start(bf16[64,1792]{1,0:T(8,128)(2,1)S(1)} %pad_maximum_fusion.6), channel_id=1, source_target_pairs={{0,2},{2,0},{4,6},{6,4},{1,3},{3,1},{5,7},{7,5},{8,10},{10,8},{12,... | collective-permute-start | bytes 688136 | tf_op jit(solution)/shard_map/ppermute | solution.py:32
  61.7 13.1 %collective-permute-start.24 = (bf16[64,896]{1,0:T(8,128)(2,1)S(1)}, bf16[64,896]{1,0:T(8,128)(2,1)S(1)}, u32[]{:S(2)}, u32[]{:S(2)}) collective-permute-start(bf16[64,896]{1,0:T(8,128)(2,1)S(1)} %get-tuple-element.28), channel_id=1, source_target_pairs={{0,6},{2,4},{4,2},{6,0},{1,7},{3,5},{5,3},{7,1},{8,14},{10,12},{12... | collective-permute-start | bytes 344072 | tf_op jit(solution)/shard_map/ppermute | solution.py:32
  64.3 13.6 %collective-permute-start.23 = (bf16[64,896]{1,0:T(8,128)(2,1)S(1)}, bf16[64,896]{1,0:T(8,128)(2,1)S(1)}, u32[]{:S(2)}, u32[]{:S(2)}) collective-permute-start(bf16[64,896]{1,0:T(8,128)(2,1)S(1)} %get-tuple-element.29), channel_id=1, source_target_pairs={{0,4},{2,6},{4,0},{6,2},{1,5},{3,7},{5,1},{7,3},{8,12},{10,14},{12... | collective-permute-start | bytes 344072 | tf_op jit(solution)/shard_map/ppermute | solution.py:32
  70.5 8.5 %collective-permute-start.22 = (bf16[64,896]{1,0:T(8,128)(2,1)S(1)}, bf16[64,896]{1,0:T(8,128)(2,1)S(1)}, u32[]{:S(2)}, u32[]{:S(2)}) collective-permute-start(bf16[64,896]{1,0:T(8,128)(2,1)S(1)} %get-tuple-element.27), channel_id=1, source_target_pairs={{0,2},{2,0},{4,6},{6,4},{1,3},{3,1},{5,7},{7,5},{8,10},{10,8},{12,... | collective-permute-start | bytes 344072 | tf_op jit(solution)/shard_map/ppermute | solution.py:32
  71.1 8.2 %collective-permute-start.12 = (bf16[64,896]{1,0:T(8,128)(2,1)S(1)}, bf16[64,896]{1,0:T(8,128)(2,1)S(1)}, u32[]{:S(2)}, u32[]{:S(2)}) collective-permute-start(bf16[64,896]{1,0:T(8,128)(2,1)S(1)} %get-tuple-element.18), channel_id=1, source_target_pairs={{0,2},{2,0},{4,6},{6,4},{1,3},{3,1},{5,7},{7,5},{8,10},{10,8},{12,... | collective-permute-start | bytes 344072 | tf_op jit(solution)/shard_map/ppermute | solution.py:32
  72.4 9.6 %collective-permute-start.13 = (bf16[64,896]{1,0:T(8,128)(2,1)S(1)}, bf16[64,896]{1,0:T(8,128)(2,1)S(1)}, u32[]{:S(2)}, u32[]{:S(2)}) collective-permute-start(bf16[64,896]{1,0:T(8,128)(2,1)S(1)} %get-tuple-element.18), channel_id=1, source_target_pairs={{0,4},{2,6},{4,0},{6,2},{1,5},{3,7},{5,1},{7,3},{8,12},{10,14},{12... | collective-permute-start | bytes 344072 | tf_op jit(solution)/shard_map/ppermute | solution.py:32
  74.8 8.5 %collective-permute-start.14 = (bf16[64,896]{1,0:T(8,128)(2,1)S(1)}, bf16[64,896]{1,0:T(8,128)(2,1)S(1)}, u32[]{:S(2)}, u32[]{:S(2)}) collective-permute-start(bf16[64,896]{1,0:T(8,128)(2,1)S(1)} %get-tuple-element.18), channel_id=1, source_target_pairs={{0,6},{2,4},{4,2},{6,0},{1,7},{3,5},{5,3},{7,1},{8,14},{10,12},{12... | collective-permute-start | bytes 344072 | tf_op jit(solution)/shard_map/ppermute | solution.py:32
  77.8 7.0 %collective-permute-start.15 = (bf16[64,896]{1,0:T(8,128)(2,1)S(1)}, bf16[64,896]{1,0:T(8,128)(2,1)S(1)}, u32[]{:S(2)}, u32[]{:S(2)}) collective-permute-start(bf16[64,896]{1,0:T(8,128)(2,1)S(1)} %get-tuple-element.18), channel_id=1, source_target_pairs={{0,1},{1,0},{2,3},{3,2},{4,5},{5,4},{6,7},{7,6},{8,9},{9,8},{10,11... | collective-permute-start | bytes 344072 | tf_op jit(solution)/shard_map/ppermute | solution.py:47
  79.2 13.1 %collective-permute-start.25 = (bf16[64,1792]{1,0:T(8,128)(2,1)S(1)}, bf16[64,1792]{1,0:T(8,128)(2,1)S(1)}, u32[]{:S(2)}, u32[]{:S(2)}) collective-permute-start(bf16[64,1792]{1,0:T(8,128)(2,1)S(1)} %get-tuple-element.56), channel_id=1, source_target_pairs={{0,2},{2,0},{4,6},{6,4},{1,3},{3,1},{5,7},{7,5},{8,10},{10,8},{12,... | collective-permute-start | bytes 688136 | tf_op jit(solution)/shard_map/ppermute | solution.py:32
  79.3 13.9 %collective-permute-start.26 = (bf16[64,1792]{1,0:T(8,128)(2,1)S(1)}, bf16[64,1792]{1,0:T(8,128)(2,1)S(1)}, u32[]{:S(2)}, u32[]{:S(2)}) collective-permute-start(bf16[64,1792]{1,0:T(8,128)(2,1)S(1)} %get-tuple-element.56), channel_id=1, source_target_pairs={{0,4},{2,6},{4,0},{6,2},{1,5},{3,7},{5,1},{7,3},{8,12},{10,14},{12... | collective-permute-start | bytes 688136 | tf_op jit(solution)/shard_map/ppermute | solution.py:32
  82.0 11.9 %collective-permute-start.27 = (bf16[64,1792]{1,0:T(8,128)(2,1)S(1)}, bf16[64,1792]{1,0:T(8,128)(2,1)S(1)}, u32[]{:S(2)}, u32[]{:S(2)}) collective-permute-start(bf16[64,1792]{1,0:T(8,128)(2,1)S(1)} %get-tuple-element.56), channel_id=1, source_target_pairs={{0,6},{2,4},{4,2},{6,0},{1,7},{3,5},{5,3},{7,1},{8,14},{10,12},{12... | collective-permute-start | bytes 688136 | tf_op jit(solution)/shard_map/ppermute | solution.py:32
  83.3 13.0 %collective-permute-start.28 = (bf16[64,1792]{1,0:T(8,128)(2,1)S(1)}, bf16[64,1792]{1,0:T(8,128)(2,1)S(1)}, u32[]{:S(2)}, u32[]{:S(2)}) collective-permute-start(bf16[64,1792]{1,0:T(8,128)(2,1)S(1)} %get-tuple-element.56), channel_id=1, source_target_pairs={{0,1},{1,0},{2,3},{3,2},{4,5},{5,4},{6,7},{7,6},{8,9},{9,8},{10,11... | collective-permute-start | bytes 688136 | tf_op jit(solution)/shard_map/ppermute | solution.py:47
  84.8 1.4 collective-permute-start.16
  86.2 1.3 collective-permute-start.17
  87.6 1.3 collective-permute-start.18
  88.9 1.3 copy-start.6
  90.3 14.1 %collective-permute-start.21 = (bf16[128,1024]{1,0:T(8,128)(2,1)S(1)}, bf16[128,1024]{1,0:T(8,128)(2,1)S(1)}, u32[]{:S(2)}, u32[]{:S(2)}) collective-permute-start(bf16[128,1024]{1,0:T(8,128)(2,1)S(1)} %get-tuple-element.22), channel_id=1, source_target_pairs={{0,24},{8,0},{16,8},{24,16},{1,25},{9,1},{17,9},{25,17},{2,26},{10... | collective-permute-start | bytes 786440 | tf_op jit(solution)/shard_map/ppermute | solution.py:28
  92.3 13.6 %collective-permute-start.20 = (bf16[128,1024]{1,0:T(8,128)(2,1)S(1)}, bf16[128,1024]{1,0:T(8,128)(2,1)S(1)}, u32[]{:S(2)}, u32[]{:S(2)}) collective-permute-start(bf16[128,1024]{1,0:T(8,128)(2,1)S(1)} %get-tuple-element.23), channel_id=1, source_target_pairs={{0,16},{8,24},{16,0},{24,8},{1,17},{9,25},{17,1},{25,9},{2,18},{10... | collective-permute-start | bytes 786440 | tf_op jit(solution)/shard_map/ppermute | solution.py:28
  93.2 14.5 %collective-permute-start.19 = (bf16[128,1024]{1,0:T(8,128)(2,1)S(1)}, bf16[128,1024]{1,0:T(8,128)(2,1)S(1)}, u32[]{:S(2)}, u32[]{:S(2)}) collective-permute-start(bf16[128,1024]{1,0:T(8,128)(2,1)S(1)} %get-tuple-element.21), channel_id=1, source_target_pairs={{0,8},{8,16},{16,24},{24,0},{1,9},{9,17},{17,25},{25,1},{2,10},{10... | collective-permute-start | bytes 786440 | tf_op jit(solution)/shard_map/ppermute | solution.py:28
  93.9 3.5 %collective-permute-start.29 = (bf16[64,1792]{1,0:T(8,128)(2,1)S(1)}, bf16[64,1792]{1,0:T(8,128)(2,1)S(1)}, u32[]{:S(2)}, u32[]{:S(2)}) collective-permute-start(bf16[64,1792]{1,0:T(8,128)(2,1)S(1)} %collective-permute-done.25), channel_id=1, source_target_pairs={{0,1},{1,0},{2,3},{3,2},{4,5},{5,4},{6,7},{7,6},{8,9},{9,8},{10,11... | collective-permute-start | bytes 688136 | tf_op jit(solution)/shard_map/ppermute | solution.py:47
  96.3 1.6 %collective-permute-start.30 = (bf16[64,1792]{1,0:T(8,128)(2,1)S(1)}, bf16[64,1792]{1,0:T(8,128)(2,1)S(1)}, u32[]{:S(2)}, u32[]{:S(2)}) collective-permute-start(bf16[64,1792]{1,0:T(8,128)(2,1)S(1)} %collective-permute-done.26), channel_id=1, source_target_pairs={{0,1},{1,0},{2,3},{3,2},{4,5},{5,4},{6,7},{7,6},{8,9},{9,8},{10,11... | collective-permute-start | bytes 688136 | tf_op jit(solution)/shard_map/ppermute | solution.py:47
  97.4 1.5 %collective-permute-start.31 = (bf16[64,1792]{1,0:T(8,128)(2,1)S(1)}, bf16[64,1792]{1,0:T(8,128)(2,1)S(1)}, u32[]{:S(2)}, u32[]{:S(2)}) collective-permute-start(bf16[64,1792]{1,0:T(8,128)(2,1)S(1)} %collective-permute-done.27), channel_id=1, source_target_pairs={{0,1},{1,0},{2,3},{3,2},{4,5},{5,4},{6,7},{7,6},{8,9},{9,8},{10,11... | collective-permute-start | bytes 688136 | tf_op jit(solution)/shard_map/ppermute | solution.py:47
  98.9 1.3 copy-start.4
  101.6 7.6 %collective-permute-start.34 = (bf16[128,1024]{1,0:T(8,128)(2,1)S(1)}, bf16[128,1024]{1,0:T(8,128)(2,1)S(1)}, u32[]{:S(2)}, u32[]{:S(2)}) collective-permute-start(bf16[128,1024]{1,0:T(8,128)(2,1)S(1)} %get-tuple-element.25), channel_id=1, source_target_pairs={{0,24},{8,0},{16,8},{24,16},{1,25},{9,1},{17,9},{25,17},{2,26},{10... | collective-permute-start | bytes 786440 | tf_op jit(solution)/shard_map/ppermute | solution.py:28
  103.5 8.8 %collective-permute-start.33 = (bf16[128,1024]{1,0:T(8,128)(2,1)S(1)}, bf16[128,1024]{1,0:T(8,128)(2,1)S(1)}, u32[]{:S(2)}, u32[]{:S(2)}) collective-permute-start(bf16[128,1024]{1,0:T(8,128)(2,1)S(1)} %get-tuple-element.26), channel_id=1, source_target_pairs={{0,16},{8,24},{16,0},{24,8},{1,17},{9,25},{17,1},{25,9},{2,18},{10... | collective-permute-start | bytes 786440 | tf_op jit(solution)/shard_map/ppermute | solution.py:28
  104.4 14.5 %collective-permute-start.32 = (bf16[128,1024]{1,0:T(8,128)(2,1)S(1)}, bf16[128,1024]{1,0:T(8,128)(2,1)S(1)}, u32[]{:S(2)}, u32[]{:S(2)}) collective-permute-start(bf16[128,1024]{1,0:T(8,128)(2,1)S(1)} %get-tuple-element.24), channel_id=1, source_target_pairs={{0,8},{8,16},{16,24},{24,0},{1,9},{9,17},{17,25},{25,1},{2,10},{10... | collective-permute-start | bytes 786440 | tf_op jit(solution)/shard_map/ppermute | solution.py:28
  119.9 21.4 %all-to-all-start.1 = ((bf16[8,16,2048]{2,1,0:T(8,128)(2,1)}), bf16[8,16,2048]{2,1,0:T(8,128)(2,1)S(1)}, u32[]{:S(2)}, u32[]{:S(2)}) async-start(bf16[8,16,2048]{2,1,0:T(8,128)(2,1)} %bitcast.22), calls=%async_computation.1 | async-start | bytes 1048576 | tf_op jit(solution)/shard_map/all_to_all | solution.py:23
  123.7 3.9 %copy-start.3 = (bf16[4,64,1024]{2,1,0:T(8,128)(2,1)S(1)}, bf16[4,64,1024]{2,1,0:T(8,128)(2,1)}, u32[]{:S(2)}) copy-start(bf16[4,64,1024]{2,1,0:T(8,128)(2,1)} %fusion.8) | copy-start | bytes 1572868
  123.7 3.9 %copy-start.5 = (bf16[512,1792]{1,0:T(8,128)(2,1)S(1)}, bf16[512,1792]{1,0:T(8,128)(2,1)}, u32[]{:S(2)}) copy-start(bf16[512,1792]{1,0:T(8,128)(2,1)} %copy-done.4) | copy-start | bytes 5505028
